TPU v7x, 1024 devices: a whole 4x4x32 slice. The times are simulated.
1024 devices in a mesh: node: 32 (over x, z_hi, core), feat: 32 (over z_lo, y).
Axes of the slice: x: 4, y: 4, z: 32 (z_hi: 4, z_lo: 8; z = z_hi * 8 + z_lo), core: 2. Of those that a mesh axis runs over, the one named last changes fastest.
Arguments:
- features: bfloat16 [768, 131072], P('feat', 'node'), may hold values from -6 to 6
- counts: int32 [512], P('node'), may hold values from 1 to 3
- src_owner: int32 [1536, 1], P('node'), may hold values from 0 to 31; in each aligned block of 48 rows (0 to 47, 48 to 95, ...) at most 4 rows name the same one
- src_local: int32 [1536], P('node'), may hold values from 0 to 15
- tiles: bfloat16 [1536, 256, 256], P('node'), may hold values from -0.375 to 0.375
- w_neigh: bfloat16 [768, 512], replicated, may hold values from -0.21875 to 0.21875
- self_part: bfloat16 [512, 131072], P(None, ('node', 'feat')), may hold values from -6 to 6
- cotangent: bfloat16 [512, 131072], P(None, ('node', 'feat')), may hold values from -24 to 24
Outputs:
- hidden: bfloat16 [512, 131072], P(None, ('node', 'feat'))
- grad_neigh: float32 [512, 768], P('feat', 'node')
Inputs may be any that keep to these rules, and one draw needn't show every extreme that they name: `src_owner`: within the 48 slots of one node device (aligned blocks of rows), no owner is named by more than 4 slots.
All inputs are finite; a program needn't handle non-finite values.
Results may differ from a plain program's by a relative error of at most 0.0052.
Values may be sent and summed in bfloat16 or wider, within the bound.
No kernel may reach another device: no remote copies, remote signals or barrier semaphores. Data moves between devices by JAX's collectives and lax.ppermute only.
A program may use at most 64 MiB of HBM per device.

v0:
```python
import math

import jax
import jax.numpy as jnp
from jax import lax
from jax.sharding import PartitionSpec as P

MAXT = 3


def silu_slope(values):
    sig = jax.nn.sigmoid(values)
    return sig * (1.0 + values * (1.0 - sig))


def per_device(features, counts, src_owner, src_local, tiles, w_neigh, self_part, cotangent):
    feat_cols = features.shape[0]
    blocks_dev = counts.shape[0]
    tile_width = tiles.shape[1]
    slot_count = blocks_dev * MAXT
    node_count = lax.axis_size("node")
    owners = src_owner[:, 0]
    live_mask = (
        (jnp.arange(MAXT, dtype=jnp.int32)[None, :] < counts[:, None])
        .reshape(slot_count)
        .astype(jnp.bfloat16)
    )
    tile_blocks = tiles.reshape(blocks_dev, MAXT, tile_width, tile_width)
    gathered = lax.all_gather(features, "node", axis=1, tiled=True)
    all_blocks = gathered.reshape(feat_cols, node_count * blocks_dev, tile_width)
    source_pos = owners * blocks_dev + src_local
    picked = jnp.take(all_blocks, source_pos, axis=1) * live_mask[None, :, None]
    picked = picked.reshape(feat_cols, blocks_dev, MAXT, tile_width)
    summed = jnp.einsum("cbms,bmds->cbd", picked, tile_blocks, preferred_element_type=jnp.float32)
    aggregated = (summed / counts.astype(jnp.float32)[None, :, None]).astype(jnp.bfloat16)
    aggregated = aggregated.reshape(feat_cols, blocks_dev * tile_width)
    node_rows = lax.all_to_all(aggregated, "feat", split_axis=1, concat_axis=0, tiled=True)
    pre_act = lax.dot_general(
        w_neigh, node_rows, (((0,), (0,)), ((), ())), preferred_element_type=jnp.float32
    )
    pre_act = pre_act + self_part.astype(jnp.float32)
    hidden = jax.nn.silu(pre_act).astype(jnp.bfloat16)
    grad_pre = (cotangent.astype(jnp.float32) * silu_slope(pre_act)).astype(jnp.bfloat16)
    total_nodes = blocks_dev * tile_width * node_count
    grad_scale = 1.0 / math.sqrt(total_nodes)
    partial_grad = lax.psum_scatter(
        lax.dot_general(
            grad_pre, node_rows, (((1,), (1,)), ((), ())), preferred_element_type=jnp.float32
        )
        * grad_scale,
        "feat",
        scatter_dimension=0,
        tiled=True,
    )
    grad_neigh = lax.psum_scatter(partial_grad, "node", scatter_dimension=1, tiled=True)
    return (hidden, grad_neigh)


def solution(mesh):
    return jax.shard_map(
        per_device,
        mesh=mesh,
        in_specs=(
            P("feat", "node"),
            P("node"),
            P("node", None),
            P("node"),
            P("node", None, None),
            P(),
            P(None, ("node", "feat")),
            P(None, ("node", "feat")),
        ),
        out_specs=(P(None, ("node", "feat")), P("feat", "node")),
        check_vma=False,
    )
```

profile of v0, /device:TPU:8, one launch (start us, length us, event | category | flops | bytes accessed | tf_op | source)
XLA Modules:
  0.0 750.7 jit_solution(1072586620830982839)
XLA Ops:
  7.2 0.0 copy-start
  7.2 0.0 all-gather.2.cloned.1.call-start
  7.2 0.7 all-gather.2.cloned.1.call-update
  7.9 0.7 convert_element_type.29
  8.6 0.7 compare_and_fusion
  9.3 0.1 broadcast_in_dim.18
  9.4 0.7 fusion.10
  10.1 216.0 %all-gather.2.cloned.1.call-done = bf16[24,131072]{1,0:T(8,128)(2,1)} async-done(((bf16[24,4096]{1,0:T(8,128)(2,1)}), bf16[24,131072]{1,0:T(8,128)(2,1)}) %all-gather.2.cloned.1.call-update) | async-done | bytes 6291472 | tf_op jit(solution)/shard_map/all_gather | solution.py:29
  226.1 5.8 copy.36
  231.9 0.0 copy-start.1
  231.9 0.0 copy-start.2
  231.9 3.4 gather_fusion
  235.4 4.5 fusion.3
  240.0 0.1 all_to_all.14
  240.0 0.7 copy.27
  240.8 7.2 all-to-all-start
  248.0 0.0 reduce-scatter.3.cloned.1.call-start
  248.1 0.0 copy-done.1
  248.1 0.1 copy.28
  248.2 0.0 copy-done.2
  248.2 0.1 copy.29
  248.3 15.6 %all-to-all-done = bf16[24,32,128]{2,0,1:T(8,128)(2,1)S(1)} async-done(((bf16[24,32,128]{2,0,1:T(8,128)(2,1)}), bf16[24,32,128]{2,0,1:T(8,128)(2,1)S(1)}, u32[]{:S(2)}, u32[]{:S(2)}) %all-to-all-start) | async-done | bytes 196640 | tf_op jit(solution)/shard_map/all_to_all | solution.py:37
  264.0 0.0 copy-done
  264.0 0.3 multiply_convert_fusion.1
  264.3 1.6 convolution_multiply_fusion
  266.0 0.0 reduce-scatter.3.cloned.1.call-update
  266.0 1.3 dynamic-slice
  267.9 0.8 copy.30
  268.7 230.5 %reduce-scatter.3.cloned.1.call-done = f32[16,768]{1,0:T(8,128)} async-done(((f32[512,768]{1,0:T(8,128)}), f32[16,768]{1,0:T(8,128)}) %reduce-scatter.3.cloned.1.call-update) | async-done | bytes 49168 | tf_op jit(solution)/shard_map/reduce_scatter | solution.py:46
  499.2 243.9 %all-reduce = f32[16,768]{1,0:T(8,128)S(1)} all-reduce(f32[16,768]{1,0:T(8,128)} %reduce-scatter.3.cloned.1.call-done), channel_id=3, replica_groups=mesh['node'=32,'feat'=32] {'node'}, use_global_device_ids=true, to_apply=%region_1.2.clone | all-reduce | flops 12288 | bytes 98304
  743.1 0.7 constant_dynamic-slice_fusion
  (2 shorter events, 0.1 us)
Async XLA Ops:
  7.2 256.8 %copy-start = (bf16[768,512]{1,0:T(8,128)(2,1)S(1)}, bf16[768,512]{1,0:T(8,128)(2,1)}, u32[]{:S(2)}) copy-start(bf16[768,512]{1,0:T(8,128)(2,1)} %param.13) | copy-start | bytes 2359300
  7.2 218.9 %all-gather.2.cloned.1.call-start = ((), (), s32[]{:S(2)}) async-start(), calls=%async_computation.2 | async-start | bytes 6488064 | tf_op jit(solution)/shard_map/all_gather | solution.py:29
  231.9 16.2 %copy-start.1 = (bf16[512,128]{1,0:T(8,128)(2,1)S(1)}, bf16[512,128]{1,0:T(8,128)(2,1)}, u32[]{:S(2)}) copy-start(bf16[512,128]{1,0:T(8,128)(2,1)} %param.14) | copy-start | bytes 393220
  231.9 16.3 %copy-start.2 = (bf16[512,128]{1,0:T(8,128)(2,1)S(1)}, bf16[512,128]{1,0:T(8,128)(2,1)}, u32[]{:S(2)}) copy-start(bf16[512,128]{1,0:T(8,128)(2,1)} %param.15) | copy-start | bytes 393220
  240.8 23.2 %all-to-all-start = ((bf16[24,32,128]{2,0,1:T(8,128)(2,1)}), bf16[24,32,128]{2,0,1:T(8,128)(2,1)S(1)}, u32[]{:S(2)}, u32[]{:S(2)}) async-start(bf16[24,32,128]{2,0,1:T(8,128)(2,1)} %copy.27), calls=%async_computation | async-start | bytes 393216 | tf_op jit(solution)/shard_map/all_to_all | solution.py:37
  248.0 251.2 %reduce-scatter.3.cloned.1.call-start = ((), (), s32[]{:S(2)}) async-start(), calls=%async_computation.3 | async-start | bytes 1622016 | tf_op jit(solution)/shard_map/reduce_scatter | solution.py:46
Sparse Core Ops, SparseCore 0:
  12.4 213.6 all-gather.1
  266.1 233.0 reduce-scatter.2
where the time goes:
time: 751 us
  waiting for transfers between devices  463 us (62%)
  blocking collectives  244 us (32%)
  between operations  14.8 us (2%)
  local copies, waits for them, and re-layouts  13.2 us (2%)
    unnamed x1, blocking collectives  244 us
    reduce_scatter x1, waiting for transfers between devices, per_device(): lax.psum_scatter(lax.dot_general(grad_pre, node_rows, (((1,), (1,)), ((),...  231 us
    all_gather x1, waiting for transfers between devices, per_device(): gathered = lax.all_gather(features, 'node', axis=1, tiled=True)  216 us
    all_to_all x1, waiting for transfers between devices, per_device(): lax.all_to_all(aggregated, 'feat', split_axis=1, concat_axis=0, tiled=True)  15.6 us
  transfers between devices with their start and end apart: 3, of which 3 were waited for; matrix products, arithmetic and copies ran while one was open for 1% of the time, Pallas kernels for 0%

commit v1 on v0

v1 whole, which is shorter than its diff:
```python
import math

import jax
import jax.numpy as jnp
from jax import lax
from jax.experimental import pallas as pl
from jax.experimental.pallas import tpu as pltpu
from jax.sharding import Mesh
from jax.sharding import PartitionSpec as P

MAXT = 3
CAP = 4
X, ZH, CORE, ZL, Y = 4, 4, 2, 8, 4
NEAR = 3 * CAP
FAR = CAP
VMEM = 48 * 1024 * 1024
f32, bf16 = jnp.float32, jnp.bfloat16


def vmem():
    return pl.BlockSpec(memory_space=pltpu.VMEM)


def smem():
    return pl.BlockSpec(memory_space=pltpu.SMEM)


def pack_kernel(first, each, stride, width, codes, *refs):
    held, out = refs[:-1], refs[-1]

    def one(i, carry):
        code = codes[(i // each) * stride + first + i % each]
        local = code % 16
        for j, ref in enumerate(held):

            @pl.when(code // 16 == j)
            def _(ref=ref):
                out[i] = ref[:, pl.ds(pl.multiple_of(local * width, width), width)]

        return carry

    lax.fori_loop(0, out.shape[0], one, 0, unroll=4)


def pack(codes, held, first, each, width):
    peers = X * CORE
    return pl.pallas_call(
        lambda *refs: pack_kernel(first, each, NEAR + FAR, width, *refs),
        out_shape=jax.ShapeDtypeStruct((peers * each, held[0].shape[0], width), held[0].dtype),
        in_specs=[smem()] + [vmem()] * len(held),
        out_specs=vmem(),
        compiler_params=pltpu.CompilerParams(vmem_limit_bytes=VMEM),
        cost_estimate=pl.CostEstimate(flops=0, bytes_accessed=4 << 20, transcendentals=0),
        name="pack",
    )(codes, *held)


def agg_kernel(pos, counts, near, far, tiles, out, acc):
    b = pl.program_id(0)
    count = counts[b]
    near_size = near.shape[0]
    for m in range(MAXT):
        p = pos[b * MAXT + m]

        def add(block, m=m):
            part = lax.dot_general(
                block, tiles[m], (((1,), (1,)), ((), ())), preferred_element_type=f32
            )
            if m == 0:
                acc[...] = part
            else:
                acc[...] += part

        @pl.when((m < count) & (p < near_size))
        def _():
            add(near[jnp.minimum(p, near_size - 1)])

        @pl.when((m < count) & (p >= near_size))
        def _():
            add(far[jnp.maximum(p - near_size, 0)])

    total = (acc[...] / count.astype(f32)).astype(out.dtype)
    half = out.shape[-1]
    for j in range(out.shape[0]):
        out[j] = total[:, j * half : (j + 1) * half]


def aggregate(pos, counts, near, far, tiles, node_cols):
    rows, width = near.shape[1:]
    blocks = counts.shape[0]
    per = width // node_cols
    return pl.pallas_call(
        agg_kernel,
        grid=(blocks,),
        out_shape=jax.ShapeDtypeStruct((blocks * per, rows, node_cols), bf16),
        in_specs=[
            smem(),
            smem(),
            vmem(),
            vmem(),
            pl.BlockSpec((MAXT, width, width), lambda b: (b, 0, 0)),
        ],
        out_specs=pl.BlockSpec((per, rows, node_cols), lambda b: (b, 0, 0)),
        scratch_shapes=[pltpu.VMEM((rows, width), f32)],
        compiler_params=pltpu.CompilerParams(vmem_limit_bytes=VMEM),
        cost_estimate=pl.CostEstimate(flops=2 * 48 * 24 * 65536, bytes_accessed=7 << 20, transcendentals=0),
        name="aggregate",
    )(pos, counts, near, far, tiles)


def dense_kernel(rows, w_t, self_part, cotangent, hidden, grad, gp):
    pre = jnp.dot(w_t[...], rows[...], preferred_element_type=f32) + self_part[...].astype(f32)
    sig = jax.nn.sigmoid(pre)
    hidden[...] = (pre * sig).astype(hidden.dtype)
    slope = sig * (1.0 + pre * (1.0 - sig))
    grad_pre = (cotangent[...].astype(f32) * slope).astype(bf16)
    piece = grad_pre.shape[0] // (ZL * Y)
    for zl in range(ZL):
        for y in range(Y):
            start = (zl * Y + y) * piece
            gp[y, zl] = grad_pre[start : start + piece]
    chunk = rows.shape[0] // (X * ZH * CORE)
    for y in range(Y):
        right = gp[y].reshape(ZL * piece, gp.shape[-1])
        part = lax.dot_general(
            rows[...], right, (((1,), (1,)), ((), ())), preferred_element_type=f32
        ).astype(grad.dtype)
        for x in range(X):
            for zh in range(ZH):
                for c in range(CORE):
                    start = ((x * ZH + zh) * CORE + c) * chunk
                    grad[(x * CORE + c) * Y + y, zh] = part[start : start + chunk]


def dense(rows, w_t, self_part, cotangent):
    hid, nodes = self_part.shape
    width = rows.shape[0]
    chunk, piece = width // (X * ZH * CORE), hid // (ZL * Y)
    return pl.pallas_call(
        dense_kernel,
        out_shape=(
            jax.ShapeDtypeStruct((hid, nodes), bf16),
            jax.ShapeDtypeStruct((X * CORE * Y, ZH, chunk, ZL * piece), bf16),
        ),
        in_specs=[vmem()] * 4,
        out_specs=(vmem(), vmem()),
        scratch_shapes=[pltpu.VMEM((Y, ZL, piece, nodes), bf16)],
        compiler_params=pltpu.CompilerParams(vmem_limit_bytes=VMEM),
        cost_estimate=pl.CostEstimate(flops=4 * 512 * 768 * 128, bytes_accessed=2 << 20, transcendentals=512 * 128),
        name="dense",
    )(rows, w_t, self_part, cotangent)


def ring(value, step):
    return lax.ppermute(value, "zh", [(i, (i + step) % ZH) for i in range(ZH)])


def plan(counts, owners, local):
    me = lax.axis_index("zh")
    slots = owners.shape[0]
    column = (owners // (ZH * CORE)) * CORE + owners % CORE
    apart = (owners // CORE + ZH - me) % ZH
    far = apart == 2
    group = column + jnp.where(far, X * CORE, 0)
    same = group[:, None] == group[None, :]
    s = jnp.arange(slots, dtype=jnp.int32)
    rank = jnp.sum((same & (s[None, :] < s[:, None])).astype(jnp.int32), axis=1)
    pos = jnp.where(far, X * CORE * NEAR + column * FAR + rank, column * NEAR + rank)
    code = local + jnp.where(apart == 1, 16, jnp.where(apart == 3, 32, 0))
    place = column * (NEAR + FAR) + rank + jnp.where(far, NEAR, 0)
    asked = X * CORE * (NEAR + FAR)
    hit = place[:, None] == jnp.arange(asked, dtype=jnp.int32)[None, :]
    ask = jnp.sum(jnp.where(hit, code[:, None], 0), axis=0)
    return pos, ask


def per_device(features, counts, src_owner, src_local, tiles, w_neigh, self_part, cotangent):
    rows, cols = features.shape
    blocks = counts.shape[0]
    width = tiles.shape[1]
    node_cols = self_part.shape[1]
    peers = X * CORE
    up = ring(features, -1)
    down = ring(features, 1)
    pos, ask = plan(counts, src_owner[:, 0], src_local)
    codes = lax.all_to_all(ask.reshape(peers, -1), ("x", "c"), 0, 0).reshape(-1)
    w_t = w_neigh.T
    half = cols // 2
    across = jnp.concatenate([ring(up[:, :half], -1), ring(down[:, half:], 1)], axis=1)
    near = pack(codes, (features, up, down), 0, NEAR, width)
    near = lax.all_to_all(
        near.reshape(peers, NEAR, rows, width), ("x", "c"), 0, 0
    ).reshape(peers * NEAR, rows, width)
    far = pack(codes, (across,), NEAR, FAR, width)
    far = lax.all_to_all(
        far.reshape(peers, FAR, rows, width), ("x", "c"), 0, 0
    ).reshape(peers * FAR, rows, width)
    aggregated = aggregate(pos, counts, near, far, tiles, node_cols)
    node_rows = lax.all_to_all(aggregated, ("zl", "y"), 0, 0).reshape(-1, node_cols)
    hidden, grad = dense(node_rows, w_t, self_part, cotangent)
    grad = lax.all_to_all(grad, ("x", "c", "y"), 0, 0)
    grad = jnp.sum(grad.astype(f32), axis=0)
    me = lax.axis_index("zh")
    total = lax.dynamic_index_in_dim(grad, me, 0, keepdims=False)
    for step in (1, 2, 3):
        total = total + ring(lax.dynamic_index_in_dim(grad, (me + step) % ZH, 0, keepdims=False), step)
    total = total.T.reshape(ZL, -1, rows)
    total = lax.all_to_all(total, "zl", 0, 0)
    grad_scale = 1.0 / math.sqrt(cols * X * ZH * CORE)
    return hidden, jnp.sum(total, axis=0) * grad_scale


def solution(mesh):
    fine = Mesh(mesh.devices.reshape(X, ZH, CORE, ZL, Y), ("x", "zh", "c", "zl", "y"))
    node, feat = ("x", "zh", "c"), ("zl", "y")
    return jax.shard_map(
        per_device,
        mesh=fine,
        in_specs=(
            P(feat, node),
            P(node),
            P(node, None),
            P(node),
            P(node, None, None),
            P(),
            P(None, node + feat),
            P(None, node + feat),
        ),
        out_specs=(P(None, node + feat), P(feat, node)),
        check_vma=False,
    )
```

time: 751 us -> 241 us (0.32)
  the two profiles are of different devices: /device:TPU:8 before, /device:TPU:2 now
where the time goes in v1:
time: 241 us; the launch traced here: 240 us
  starting transfers between devices  101 us (42%)
  waiting for transfers between devices  81.1 us (34%)
  blocking collectives  29.4 us (12%)
  Pallas kernels  21.7 us (9%)
  other arithmetic  3.82 us (2%)
  local copies, waits for them, and re-layouts  2.53 us (1%)
    ppermute x7, starting transfers between devices, ring(): return lax.ppermute(value, 'zh', [(i, (i + step) % ZH) for i in range(ZH)])  69.9 us
    ppermute x7, waiting for transfers between devices, ring(): return lax.ppermute(value, 'zh', [(i, (i + step) % ZH) for i in range(ZH)])  34.2 us
    all_to_all x1, waiting for transfers between devices, per_device(): lax.all_to_all(aggregated, ('zl', 'y'), 0, 0).reshape(-1, node_cols)  16 us
    all_to_all x1, waiting for transfers between devices, per_device(): lax.all_to_all(near.reshape(peers, NEAR, rows, width), ('x', 'c'), 0, 0)  15.9 us
    all_to_all x1, blocking collectives, per_device(): codes = lax.all_to_all(ask.reshape(peers, -1), ('x', 'c'), 0, 0).reshape(-1)  15 us
    all_to_all x1, blocking collectives, per_device(): total = lax.all_to_all(total, 'zl', 0, 0)  14.4 us
    all_to_all x1, waiting for transfers between devices, per_device(): grad = lax.all_to_all(grad, ('x', 'c', 'y'), 0, 0)  12.8 us
    all_to_all x1, starting transfers between devices, per_device(): lax.all_to_all(aggregated, ('zl', 'y'), 0, 0).reshape(-1, node_cols)  12.6 us
  transfers between devices with their start and end apart: 11, of which 8 were waited for; matrix products, arithmetic and copies ran while one was open for 2% of the time, Pallas kernels for 2%

profile of v1, /device:TPU:2, one launch (start us, length us, event | category | flops | bytes accessed | tf_op | source)
XLA Modules:
  0.0 240.1 jit_solution(14895948895010112631)
XLA Ops:
  0.6 0.0 copy-start
  0.6 23.1 %collective-permute-start = (bf16[24,4096]{1,0:T(8,128)(2,1)}, bf16[24,4096]{1,0:T(8,128)(2,1)S(1)}, u32[]{:S(2)}, u32[]{:S(2)}) collective-permute-start(bf16[24,4096]{1,0:T(8,128)(2,1)} %refs_1_.1), channel_id=1, source_target_pairs={{0,192},{64,0},{128,64},{192,128},{1,193},{65,1},{129,65},{193,129... | collective-permute-start | bytes 589832 | tf_op jit(solution)/shard_map/ppermute | solution.py:155
  23.8 1.9 collective-permute-start.1
  25.7 0.7 fusion.12
  26.4 0.7 fusion.9
  27.1 0.7 fusion.6
  27.7 0.2 convert_reduce_fusion.1
  27.9 22.1 %collective-permute-done.1.refs_3_ = bf16[24,4096]{1,0:T(8,128)(2,1)S(1)} collective-permute-done((bf16[24,4096]{1,0:T(8,128)(2,1)}, bf16[24,4096]{1,0:T(8,128)(2,1)S(1)}, u32[]{:S(2)}, u32[]{:S(2)}) %collective-permute-start.1) | collective-permute-done | bytes 196640 | tf_op jit(solution)/shard_map/ppermute | solution.py:155
  50.0 1.9 collective-permute-start.3
  51.9 6.0 %collective-permute-done.refs_2_ = bf16[24,4096]{1,0:T(8,128)(2,1)S(1)} collective-permute-done((bf16[24,4096]{1,0:T(8,128)(2,1)}, bf16[24,4096]{1,0:T(8,128)(2,1)S(1)}, u32[]{:S(2)}, u32[]{:S(2)}) %collective-permute-start) | collective-permute-done | bytes 196640 | tf_op jit(solution)/shard_map/ppermute | solution.py:155
  58.0 13.0 %collective-permute-start.2 = (bf16[24,2048]{1,0:T(8,128)(2,1)S(1)}, bf16[24,2048]{1,0:T(8,128)(2,1)S(1)}, u32[]{:S(2)}, u32[]{:S(2)}) collective-permute-start(bf16[24,2048]{1,0:T(8,128)(2,1)S(1)} %slice.8), channel_id=1, source_target_pairs={{0,192},{64,0},{128,64},{192,128},{1,193},{65,1},{129,65},{193,129... | collective-permute-start | bytes 294920 | tf_op jit(solution)/shard_map/ppermute | solution.py:155
  71.0 0.1 select_reduce_fusion
  71.0 0.1 all_to_all.21
  71.1 15.0 %all_to_all.34 = s32[8,1,16]{2,1,0:T(1,128)S(1)} all-to-all(s32[8,1,16]{2,1,0:T(1,128)S(1)} %bitcast.65), channel_id=1, replica_groups=mesh['x'=4,'zh'=4,'c'=2,'zl'=8,'y'=4] {'x','c'}, dimensions={0} | all-to-all | bytes 1024 | tf_op jit(solution)/shard_map/all_to_all | solution.py:186
  86.1 0.5 broadcast.264
  86.6 0.7 reduce.3
  87.3 0.1 reshape.108.refs_0_
  87.4 0.0 collective-permute-done.3
  87.4 0.0 collective-permute-done.2
  87.4 2.1 pack.3
  89.5 7.1 %all-to-all-start.2 = ((bf16[8,4,24,256]{3,2,1,0:T(8,128)(2,1)}), bf16[8,4,24,256]{3,2,1,0:T(8,128)(2,1)S(1)}, u32[]{:S(2)}, u32[]{:S(2)}) async-start(bf16[8,4,24,256]{3,2,1,0:T(8,128)(2,1)} %bitcast.7), calls=%async_computation.2 | async-start | bytes 786432 | tf_op jit(solution)/shard_map/all_to_all | solution.py:195
  96.6 0.0 copy-done
  96.6 5.3 %pack.2 = bf16[96,24,256]{2,1,0:T(8,128)(2,1)} custom-call(s32[128]{0:T(128)S(1)} %reshape.108.refs_0_, bf16[24,4096]{1,0:T(8,128)(2,1)S(1)} %copy-done, bf16[24,4096]{1,0:T(8,128)(2,1)S(1)} %collective-permute-done.refs_2_, bf16[24,4096]{1,0:T(8,128)(2,1)S(1)} %collective-permute-done.1.refs_3_), custom_call_target="tpu_custom_call" | custom-call | bytes 4194304 | tf_op jit(solution)/shard_map/pack/pallas_call | solution.py:47
  101.9 0.0 copy-start.3
  101.9 2.2 all-to-all-done.2
  104.1 4.9 %all-to-all-start.1 = ((bf16[8,12,24,256]{3,2,1,0:T(8,128)(2,1)}), bf16[8,12,24,256]{3,2,1,0:T(8,128)(2,1)S(1)}, u32[]{:S(2)}, u32[]{:S(2)}) async-start(bf16[8,12,24,256]{3,2,1,0:T(8,128)(2,1)} %bitcast.5), calls=%async_computation.1 | async-start | bytes 2359296 | tf_op jit(solution)/shard_map/all_to_all | solution.py:191
  109.0 15.9 %all-to-all-done.1 = bf16[8,12,24,256]{3,2,1,0:T(8,128)(2,1)S(1)} async-done(((bf16[8,12,24,256]{3,2,1,0:T(8,128)(2,1)}), bf16[8,12,24,256]{3,2,1,0:T(8,128)(2,1)S(1)}, u32[]{:S(2)}, u32[]{:S(2)}) %all-to-all-start.1) | async-done | bytes 1179680 | tf_op jit(solution)/shard_map/all_to_all | solution.py:191
  125.0 0.0 copy-done.3
  125.0 0.0 copy-start.4
  125.0 12.4 %aggregate.1 = bf16[32,24,128]{2,1,0:T(8,128)(2,1)} custom-call(s32[48]{0:T(128)S(1)} %compare_select_fusion.8.pos, s32[16]{0:T(128)S(1)} %copy-done.3, bf16[96,24,256]{2,1,0:T(8,128)(2,1)S(1)} %bitcast.60, bf16[32,24,256]{2,1,0:T(8,128)(2,1)S(1)} %bitcast.62, bf16[48,256,256]{2,1,0:T(8,128)(2,1)} %tiles.1), custom_call_target="tpu_custom_call" | custom-call | flops 150994944 | bytes 7340032 | tf_op jit(solution)/shard_map/aggregate/pallas_call | solution.py:92
  137.4 0.0 copy-start.1
  137.4 0.0 copy-start.2
  137.4 12.6 %all-to-all-start.3 = ((bf16[32,24,128]{2,1,0:T(8,128)(2,1)}), bf16[32,24,128]{2,1,0:T(8,128)(2,1)S(1)}, u32[]{:S(2)}, u32[]{:S(2)}) async-start(bf16[32,24,128]{2,1,0:T(8,128)(2,1)} %aggregate.1), calls=%async_computation.3 | async-start | bytes 393216 | tf_op jit(solution)/shard_map/all_to_all | solution.py:199
  150.0 0.0 copy-done.4
  150.0 0.3 copy.18
  150.3 16.0 %all-to-all-done.3 = bf16[32,24,128]{2,1,0:T(8,128)(2,1)S(1)} async-done(((bf16[32,24,128]{2,1,0:T(8,128)(2,1)}), bf16[32,24,128]{2,1,0:T(8,128)(2,1)S(1)}, u32[]{:S(2)}, u32[]{:S(2)}) %all-to-all-start.3) | async-done | bytes 196640 | tf_op jit(solution)/shard_map/all_to_all | solution.py:199
  166.2 0.0 copy-done.1
  166.2 0.0 copy-done.2
  166.2 2.0 dense.1
  168.2 6.1 %all-to-all-start.4 = ((bf16[32,4,24,128]{3,2,1,0:T(8,128)(2,1)}), bf16[32,4,24,128]{3,2,1,0:T(8,128)(2,1)S(1)}, u32[]{:S(2)}, u32[]{:S(2)}) async-start(bf16[32,4,24,128]{3,2,1,0:T(8,128)(2,1)} %get-tuple-element.5), calls=%async_computation.4 | async-start | bytes 1572864 | tf_op jit(solution)/shard_map/all_to_all | solution.py:201
  174.4 12.8 %all-to-all-done.4 = bf16[32,4,24,128]{3,2,1,0:T(8,128)(2,1)S(1)} async-done(((bf16[32,4,24,128]{3,2,1,0:T(8,128)(2,1)}), bf16[32,4,24,128]{3,2,1,0:T(8,128)(2,1)S(1)}, u32[]{:S(2)}, u32[]{:S(2)}) %all-to-all-start.4) | async-done | bytes 786464 | tf_op jit(solution)/shard_map/all_to_all | solution.py:201
  187.2 0.1 convert_reduce_fusion
  187.3 10.7 %collective-permute-start.6 = (f32[24,128]{1,0:T(8,128)S(1)}, f32[24,128]{1,0:T(8,128)S(1)}, u32[]{:S(2)}, u32[]{:S(2)}) collective-permute-start(f32[24,128]{1,0:T(8,128)S(1)} %get-tuple-element.18), channel_id=1, source_target_pairs={{0,192},{64,0},{128,64},{192,128},{1,193},{65,1},{129,65},{193,129... | collective-permute-start | bytes 36872 | tf_op jit(solution)/shard_map/ppermute | solution.py:155
  198.1 10.9 %collective-permute-start.5 = (f32[24,128]{1,0:T(8,128)S(1)}, f32[24,128]{1,0:T(8,128)S(1)}, u32[]{:S(2)}, u32[]{:S(2)}) collective-permute-start(f32[24,128]{1,0:T(8,128)S(1)} %get-tuple-element.19), channel_id=1, source_target_pairs={{0,128},{64,192},{128,0},{192,64},{1,129},{65,193},{129,1},{193,65... | collective-permute-start | bytes 36872 | tf_op jit(solution)/shard_map/ppermute | solution.py:155
  209.0 8.4 %collective-permute-start.4 = (f32[24,128]{1,0:T(8,128)S(1)}, f32[24,128]{1,0:T(8,128)S(1)}, u32[]{:S(2)}, u32[]{:S(2)}) collective-permute-start(f32[24,128]{1,0:T(8,128)S(1)} %get-tuple-element.17), channel_id=1, source_target_pairs={{0,64},{64,128},{128,192},{192,0},{1,65},{65,129},{129,193},{193,1... | collective-permute-start | bytes 36872 | tf_op jit(solution)/shard_map/ppermute | solution.py:155
  217.3 0.0 collective-permute-done.6
  217.4 4.6 %collective-permute-done.5 = f32[24,128]{1,0:T(8,128)S(1)} collective-permute-done((f32[24,128]{1,0:T(8,128)S(1)}, f32[24,128]{1,0:T(8,128)S(1)}, u32[]{:S(2)}, u32[]{:S(2)}) %collective-permute-start.5) | collective-permute-done | bytes 12320 | tf_op jit(solution)/shard_map/ppermute | solution.py:155
  222.0 1.4 collective-permute-done.4
  223.4 0.1 copy.22
  223.5 0.1 reshape.124
  223.6 14.4 %all_to_all.35 = f32[8,1,384]{2,1,0:T(1,128)S(1)} all-to-all(f32[8,1,384]{2,1,0:T(1,128)S(1)} %reshape.124), channel_id=1, replica_groups=mesh['x'=4,'zh'=4,'c'=2,'zl'=8,'y'=4] {'zl'}, dimensions={0} | all-to-all | bytes 24576 | tf_op jit(solution)/shard_map/all_to_all | solution.py:208
  238.0 0.5 broadcast.275
  238.5 0.7 reduce.4
  239.2 0.1 reshape.125
  239.3 0.1 copy.23
  239.4 0.7 copy.21
  (9 shorter events, 0.1 us)
Async XLA Ops:
  0.6 96.0 %copy-start = (bf16[24,4096]{1,0:T(8,128)(2,1)S(1)}, bf16[24,4096]{1,0:T(8,128)(2,1)}, u32[]{:S(2)}) copy-start(bf16[24,4096]{1,0:T(8,128)(2,1)} %refs_1_.1) | copy-start | bytes 589828
  0.6 57.3 %collective-permute-start = (bf16[24,4096]{1,0:T(8,128)(2,1)}, bf16[24,4096]{1,0:T(8,128)(2,1)S(1)}, u32[]{:S(2)}, u32[]{:S(2)}) collective-permute-start(bf16[24,4096]{1,0:T(8,128)(2,1)} %refs_1_.1), channel_id=1, source_target_pairs={{0,192},{64,0},{128,64},{192,128},{1,193},{65,1},{129,65},{193,129... | collective-permute-start | bytes 589832 | tf_op jit(solution)/shard_map/ppermute | solution.py:155
  23.8 26.2 %collective-permute-start.1 = (bf16[24,4096]{1,0:T(8,128)(2,1)}, bf16[24,4096]{1,0:T(8,128)(2,1)S(1)}, u32[]{:S(2)}, u32[]{:S(2)}) collective-permute-start(bf16[24,4096]{1,0:T(8,128)(2,1)} %refs_1_.1), channel_id=1, source_target_pairs={{0,64},{64,128},{128,192},{192,0},{1,65},{65,129},{129,193},{193,1... | collective-permute-start | bytes 589832 | tf_op jit(solution)/shard_map/ppermute | solution.py:155
  50.0 37.4 %collective-permute-start.3 = (bf16[24,2048]{1,0:T(8,128)(2,1)S(1)}, bf16[24,2048]{1,0:T(8,128)(2,1)S(1)}, u32[]{:S(2)}, u32[]{:S(2)}) collective-permute-start(bf16[24,2048]{1,0:T(8,128)(2,1)S(1)} %slice.9), channel_id=1, source_target_pairs={{0,64},{64,128},{128,192},{192,0},{1,65},{65,129},{129,193},{193,1... | collective-permute-start | bytes 294920 | tf_op jit(solution)/shard_map/ppermute | solution.py:155
  58.0 29.4 %collective-permute-start.2 = (bf16[24,2048]{1,0:T(8,128)(2,1)S(1)}, bf16[24,2048]{1,0:T(8,128)(2,1)S(1)}, u32[]{:S(2)}, u32[]{:S(2)}) collective-permute-start(bf16[24,2048]{1,0:T(8,128)(2,1)S(1)} %slice.8), channel_id=1, source_target_pairs={{0,192},{64,0},{128,64},{192,128},{1,193},{65,1},{129,65},{193,129... | collective-permute-start | bytes 294920 | tf_op jit(solution)/shard_map/ppermute | solution.py:155
  89.5 14.6 %all-to-all-start.2 = ((bf16[8,4,24,256]{3,2,1,0:T(8,128)(2,1)}), bf16[8,4,24,256]{3,2,1,0:T(8,128)(2,1)S(1)}, u32[]{:S(2)}, u32[]{:S(2)}) async-start(bf16[8,4,24,256]{3,2,1,0:T(8,128)(2,1)} %bitcast.7), calls=%async_computation.2 | async-start | bytes 786432 | tf_op jit(solution)/shard_map/all_to_all | solution.py:195
  101.9 23.1 %copy-start.3 = (s32[16]{0:T(128)S(1)}, s32[16]{0:T(128)}, u32[]{:S(2)}) copy-start(s32[16]{0:T(128)} %counts.1) | copy-start | bytes 196
  104.1 20.9 %all-to-all-start.1 = ((bf16[8,12,24,256]{3,2,1,0:T(8,128)(2,1)}), bf16[8,12,24,256]{3,2,1,0:T(8,128)(2,1)S(1)}, u32[]{:S(2)}, u32[]{:S(2)}) async-start(bf16[8,12,24,256]{3,2,1,0:T(8,128)(2,1)} %bitcast.5), calls=%async_computation.1 | async-start | bytes 2359296 | tf_op jit(solution)/shard_map/all_to_all | solution.py:191
  125.0 25.0 %copy-start.4 = (bf16[768,512]{1,0:T(8,128)(2,1)S(1)}, bf16[768,512]{1,0:T(8,128)(2,1)}, u32[]{:S(2)}) copy-start(bf16[768,512]{1,0:T(8,128)(2,1)} %param.13) | copy-start | bytes 2359300
  137.4 28.9 %copy-start.1 = (bf16[512,128]{1,0:T(8,128)(2,1)S(1)}, bf16[512,128]{1,0:T(8,128)(2,1)}, u32[]{:S(2)}) copy-start(bf16[512,128]{1,0:T(8,128)(2,1)} %self_part.1) | copy-start | bytes 393220
  137.4 28.9 %copy-start.2 = (bf16[512,128]{1,0:T(8,128)(2,1)S(1)}, bf16[512,128]{1,0:T(8,128)(2,1)}, u32[]{:S(2)}) copy-start(bf16[512,128]{1,0:T(8,128)(2,1)} %cotangent.1) | copy-start | bytes 393220
  137.4 28.9 %all-to-all-start.3 = ((bf16[32,24,128]{2,1,0:T(8,128)(2,1)}), bf16[32,24,128]{2,1,0:T(8,128)(2,1)S(1)}, u32[]{:S(2)}, u32[]{:S(2)}) async-start(bf16[32,24,128]{2,1,0:T(8,128)(2,1)} %aggregate.1), calls=%async_computation.3 | async-start | bytes 393216 | tf_op jit(solution)/shard_map/all_to_all | solution.py:199
  168.2 19.0 %all-to-all-start.4 = ((bf16[32,4,24,128]{3,2,1,0:T(8,128)(2,1)}), bf16[32,4,24,128]{3,2,1,0:T(8,128)(2,1)S(1)}, u32[]{:S(2)}, u32[]{:S(2)}) async-start(bf16[32,4,24,128]{3,2,1,0:T(8,128)(2,1)} %get-tuple-element.5), calls=%async_computation.4 | async-start | bytes 1572864 | tf_op jit(solution)/shard_map/all_to_all | solution.py:201
  187.3 30.0 %collective-permute-start.6 = (f32[24,128]{1,0:T(8,128)S(1)}, f32[24,128]{1,0:T(8,128)S(1)}, u32[]{:S(2)}, u32[]{:S(2)}) collective-permute-start(f32[24,128]{1,0:T(8,128)S(1)} %get-tuple-element.18), channel_id=1, source_target_pairs={{0,192},{64,0},{128,64},{192,128},{1,193},{65,1},{129,65},{193,129... | collective-permute-start | bytes 36872 | tf_op jit(solution)/shard_map/ppermute | solution.py:155
  198.1 23.9 %collective-permute-start.5 = (f32[24,128]{1,0:T(8,128)S(1)}, f32[24,128]{1,0:T(8,128)S(1)}, u32[]{:S(2)}, u32[]{:S(2)}) collective-permute-start(f32[24,128]{1,0:T(8,128)S(1)} %get-tuple-element.19), channel_id=1, source_target_pairs={{0,128},{64,192},{128,0},{192,64},{1,129},{65,193},{129,1},{193,65... | collective-permute-start | bytes 36872 | tf_op jit(solution)/shard_map/ppermute | solution.py:155
  209.0 14.5 %collective-permute-start.4 = (f32[24,128]{1,0:T(8,128)S(1)}, f32[24,128]{1,0:T(8,128)S(1)}, u32[]{:S(2)}, u32[]{:S(2)}) collective-permute-start(f32[24,128]{1,0:T(8,128)S(1)} %get-tuple-element.17), channel_id=1, source_target_pairs={{0,64},{64,128},{128,192},{192,0},{1,65},{65,129},{129,193},{193,1... | collective-permute-start | bytes 36872 | tf_op jit(solution)/shard_map/ppermute | solution.py:155

commit v2 on v1

v2 whole, which is shorter than its diff:
```python
import math

import jax
import jax.numpy as jnp
from jax import lax
from jax.experimental import pallas as pl
from jax.experimental.pallas import tpu as pltpu
from jax.sharding import Mesh
from jax.sharding import PartitionSpec as P

MAXT = 3
CAP = 4
X, ZH, CORE, ZL, Y = 4, 4, 2, 8, 4
EACH = ZH * CAP
VMEM = 48 * 1024 * 1024
f32, bf16 = jnp.float32, jnp.bfloat16


def vmem():
    return pl.BlockSpec(memory_space=pltpu.VMEM)


def smem():
    return pl.BlockSpec(memory_space=pltpu.SMEM)


def pack_kernel(width, codes, *refs):
    held, out = refs[:-1], refs[-1]

    def one(i, carry):
        code = codes[i]
        local = code % 16
        for j, ref in enumerate(held):

            @pl.when(code // 16 == j)
            def _(ref=ref):
                out[i] = ref[:, pl.ds(pl.multiple_of(local * width, width), width)]

        return carry

    lax.fori_loop(0, out.shape[0], one, 0, unroll=4)


def pack(codes, held, width):
    return pl.pallas_call(
        lambda *refs: pack_kernel(width, *refs),
        out_shape=jax.ShapeDtypeStruct((codes.shape[0], held[0].shape[0], width), held[0].dtype),
        in_specs=[smem()] + [vmem()] * len(held),
        out_specs=vmem(),
        compiler_params=pltpu.CompilerParams(vmem_limit_bytes=VMEM),
        cost_estimate=pl.CostEstimate(flops=0, bytes_accessed=2 << 20, transcendentals=0),
        name="pack",
    )(codes, *held)


def agg_kernel(pos, counts, blocks, tiles, out):
    half = out.shape[-1]
    per = tiles.shape[1] // half

    def one(b, carry):
        count = counts[b]
        total = None
        for m in range(MAXT):
            block = blocks[pos[b * MAXT + m]]
            block = jnp.where(m < count, block, jnp.zeros_like(block))
            part = lax.dot_general(
                block, tiles[b * MAXT + m], (((1,), (1,)), ((), ())), preferred_element_type=f32
            )
            total = part if m == 0 else total + part
        total = (total / count.astype(f32)).astype(out.dtype)
        for j in range(per):
            out[b * per + j] = total[:, j * half : (j + 1) * half]
        return carry

    lax.fori_loop(0, counts.shape[0], one, 0, unroll=8)


def aggregate(pos, counts, blocks, tiles, node_cols):
    rows, width = blocks.shape[1:]
    return pl.pallas_call(
        agg_kernel,
        out_shape=jax.ShapeDtypeStruct((counts.shape[0] * width // node_cols, rows, node_cols), bf16),
        in_specs=[smem(), smem(), vmem(), vmem()],
        out_specs=vmem(),
        compiler_params=pltpu.CompilerParams(vmem_limit_bytes=VMEM),
        cost_estimate=pl.CostEstimate(flops=2 * 48 * 24 * 65536, bytes_accessed=7 << 20, transcendentals=0),
        name="aggregate",
    )(pos, counts, blocks, tiles)


def dense_kernel(rows, w_t, self_part, cotangent, hidden, grad, gp):
    pre = jnp.dot(w_t[...], rows[...], preferred_element_type=f32) + self_part[...].astype(f32)
    sig = jax.nn.sigmoid(pre)
    hidden[...] = (pre * sig).astype(hidden.dtype)
    slope = sig * (1.0 + pre * (1.0 - sig))
    grad_pre = (cotangent[...].astype(f32) * slope).astype(bf16)
    piece = grad_pre.shape[0] // (ZL * Y)
    for zl in range(ZL):
        for y in range(Y):
            start = (zl * Y + y) * piece
            gp[y, zl] = grad_pre[start : start + piece]
    chunk = rows.shape[0] // (X * ZH * CORE)
    for y in range(Y):
        right = gp[y].reshape(ZL * piece, gp.shape[-1])
        part = lax.dot_general(
            rows[...], right, (((1,), (1,)), ((), ())), preferred_element_type=f32
        ).astype(grad.dtype)
        for x in range(X):
            for zh in range(ZH):
                for c in range(CORE):
                    start = ((x * ZH + zh) * CORE + c) * chunk
                    grad[(x * CORE + c) * Y + y, zh] = part[start : start + chunk]


def dense(rows, w_t, self_part, cotangent):
    hid, nodes = self_part.shape
    width = rows.shape[0]
    chunk, piece = width // (X * ZH * CORE), hid // (ZL * Y)
    return pl.pallas_call(
        dense_kernel,
        out_shape=(
            jax.ShapeDtypeStruct((hid, nodes), bf16),
            jax.ShapeDtypeStruct((X * CORE * Y, ZH, chunk, ZL * piece), bf16),
        ),
        in_specs=[vmem()] * 4,
        out_specs=(vmem(), vmem()),
        scratch_shapes=[pltpu.VMEM((Y, ZL, piece, nodes), bf16)],
        compiler_params=pltpu.CompilerParams(vmem_limit_bytes=VMEM),
        cost_estimate=pl.CostEstimate(flops=4 * 512 * 768 * 128, bytes_accessed=2 << 20, transcendentals=512 * 128),
        name="dense",
    )(rows, w_t, self_part, cotangent)


def onward(value, step):
    pairs = []
    for z in range(ZH):
        pairs.append((z * CORE, (z + step) % ZH * CORE))
        pairs.append((z * CORE + 1, (z - step) % ZH * CORE + 1))
    return lax.ppermute(value, ("zh", "c"), pairs)


def plan(owners, local):
    me = lax.axis_index("zh")
    slots = owners.shape[0]
    core = owners % CORE
    apart = (me + ZH - owners // CORE % ZH) % ZH
    apart = jnp.where(core == 0, apart, (ZH - apart) % ZH)
    held = jnp.where(apart == 2, 3, jnp.where(apart == 3, 2, apart))
    column = (owners // (ZH * CORE)) * CORE + core
    s = jnp.arange(slots, dtype=jnp.int32)
    earlier = (column[:, None] == column[None, :]) & (s[None, :] < s[:, None])
    pos = column * EACH + jnp.sum(earlier.astype(jnp.int32), axis=1)
    hit = pos[:, None] == jnp.arange(X * CORE * EACH, dtype=jnp.int32)[None, :]
    return pos, jnp.sum(jnp.where(hit, (held * 16 + local)[:, None], 0), axis=0)


def per_device(features, counts, src_owner, src_local, tiles, w_neigh, self_part, cotangent):
    rows, cols = features.shape
    width = tiles.shape[1]
    node_cols = self_part.shape[1]
    first = onward(features, 1)
    second = onward(features, -1)
    pos, ask = plan(src_owner[:, 0], src_local)
    codes = lax.all_to_all(ask.reshape(X * CORE, EACH), ("x", "c"), 0, 0).reshape(-1)
    codes, first = lax.optimization_barrier((codes, first))
    third = onward(first, 1)
    blocks = pack(codes, (features, first, second, third), width)
    blocks = lax.all_to_all(blocks.reshape(X * CORE, EACH, rows, width), ("x", "c"), 0, 0)
    aggregated = aggregate(pos, counts, blocks.reshape(-1, rows, width), tiles, node_cols)
    node_rows = lax.all_to_all(aggregated, ("zl", "y"), 0, 0).reshape(-1, node_cols)
    hidden, grad = dense(node_rows, w_neigh.T, self_part, cotangent)
    grad = lax.all_to_all(grad, ("x", "c", "y"), 0, 0)
    grad = jnp.sum(grad.astype(f32), axis=0)
    grad = jnp.sum(lax.all_to_all(grad, "zh", 0, 0), axis=0)
    grad = lax.all_to_all(grad.T.reshape(ZL, -1, rows), "zl", 0, 0)
    grad_scale = 1.0 / math.sqrt(cols * X * ZH * CORE)
    return hidden, jnp.sum(grad, axis=0) * grad_scale


def solution(mesh):
    fine = Mesh(mesh.devices.reshape(X, ZH, CORE, ZL, Y), ("x", "zh", "c", "zl", "y"))
    node, feat = ("x", "zh", "c"), ("zl", "y")
    return jax.shard_map(
        per_device,
        mesh=fine,
        in_specs=(
            P(feat, node),
            P(node),
            P(node, None),
            P(node),
            P(node, None, None),
            P(),
            P(None, node + feat),
            P(None, node + feat),
        ),
        out_specs=(P(None, node + feat), P(feat, node)),
        check_vma=False,
    )
```

time: 241 us -> 224 us (0.929)
  blocking collectives: 29.4 us -> 77.2 us
  waiting for transfers between devices: 81.1 us -> 39.6 us
  starting transfers between devices: 101 us -> 85.9 us
  Pallas kernels: 21.7 us -> 12.7 us
    all_to_all x2 -> x3, blocking collectives: 29.4 us -> 77.2 us  [the longest x1 45.3 us: per_device(): grad = jnp.sum(lax.all_to_all(grad, 'zh', 0, 0), axis=0)]
    ppermute x7 -> x3, waiting for transfers between devices: 34.2 us -> 3.16 us  [onward(): return lax.ppermute(value, ('zh', 'c'), pairs)]
    all_to_all x3 -> x2, waiting for transfers between devices: 31 us -> 20.1 us  [the longest x1 20.1 us: per_device(): lax.all_to_all(blocks.reshape(X * CORE, EACH, rows, width), ('x', 'c'), 0...]
    pallas_call x3 -> x2, Pallas kernels: 19.7 us -> 11.4 us  [the longest x1 5.83 us: pack(): pl.pallas_call(lambda *refs: pack_kernel(width, *refs), out_shape=jax.Sha...]
    all_to_all x1, starting transfers between devices: 12.6 us -> 4.99 us  [per_device(): lax.all_to_all(aggregated, ('zl', 'y'), 0, 0).reshape(-1, node_cols)]
    ppermute x7 -> x3, starting transfers between devices: 69.9 us -> 64.5 us  [onward(): return lax.ppermute(value, ('zh', 'c'), pairs)]
    all_to_all x3 -> x2, starting transfers between devices: 18.1 us -> 16.4 us  [the longest x1 11.3 us: per_device(): lax.all_to_all(ask.reshape(X * CORE, EACH), ('x', 'c'), 0, 0).reshape(-1)]
  transfers between devices with their start and end apart: 11 -> 6, of which waited for: 8 -> 3; matrix products, arithmetic and copies ran while one was open for 2% -> 2% of each run, Pallas kernels for 2% -> 0%
where the time goes in v2:
time: 224 us
  starting transfers between devices  85.9 us (38%)
  blocking collectives  77.2 us (34%)
  waiting for transfers between devices  39.6 us (18%)
  Pallas kernels  12.7 us (6%)
  local copies, waits for them, and re-layouts  4.03 us (2%)
  other arithmetic  3.81 us (2%)
    ppermute x3, starting transfers between devices, onward(): return lax.ppermute(value, ('zh', 'c'), pairs)  64.5 us
    all_to_all x1, blocking collectives, per_device(): grad = jnp.sum(lax.all_to_all(grad, 'zh', 0, 0), axis=0)  45.3 us
    all_to_all x1, waiting for transfers between devices, per_device(): lax.all_to_all(blocks.reshape(X * CORE, EACH, rows, width), ('x', 'c'), 0...  20.1 us
    all_to_all x1, blocking collectives, per_device(): grad = lax.all_to_all(grad, ('x', 'c', 'y'), 0, 0)  17 us
    all_to_all x1, waiting for transfers between devices, per_device(): lax.all_to_all(aggregated, ('zl', 'y'), 0, 0).reshape(-1, node_cols)  16.3 us
    all_to_all x1, blocking collectives, per_device(): grad = lax.all_to_all(grad.T.reshape(ZL, -1, rows), 'zl', 0, 0)  14.9 us
    all_to_all x1, starting transfers between devices, per_device(): lax.all_to_all(ask.reshape(X * CORE, EACH), ('x', 'c'), 0, 0).reshape(-1)  11.3 us
    pallas_call x1, Pallas kernels, pack(): pl.pallas_call(lambda *refs: pack_kernel(width, *refs), out_shape=jax.Sha...  5.83 us
  transfers between devices with their start and end apart: 6, of which 3 were waited for; matrix products, arithmetic and copies ran while one was open for 2% of the time, Pallas kernels for 0%

profile of v2, /device:TPU:2, one launch (start us, length us, event | category | flops | bytes accessed | tf_op | source)
XLA Modules:
  0.0 223.9 jit_solution(1653174522375606287)
XLA Ops:
  0.6 15.7 %collective-permute-start = (bf16[24,4096]{1,0:T(8,128)(2,1)}, bf16[24,4096]{1,0:T(8,128)(2,1)S(1)}, u32[]{:S(2)}, u32[]{:S(2)}) collective-permute-start(bf16[24,4096]{1,0:T(8,128)(2,1)} %refs_1_.1), channel_id=1, source_target_pairs={{0,64},{32,224},{64,128},{96,32},{128,192},{160,96},{192,0},{224,1... | collective-permute-start | bytes 589832 | tf_op jit(solution)/shard_map/ppermute | solution.py:139
  16.4 0.7 fusion.9
  17.0 0.7 fusion.4
  17.7 0.2 convert_reduce_fusion.1
  17.9 0.7 fusion.8
  18.6 0.1 select_reduce_fusion
  18.7 0.7 all_to_all.21
  19.4 11.3 %all-to-all-start = ((s32[8,1,16]{2,1,0:T(1,128)}), s32[8,1,16]{2,1,0:T(1,128)S(1)}, u32[]{:S(2)}, u32[]{:S(2)}) async-start(s32[8,1,16]{2,1,0:T(1,128)} %bitcast.4), calls=%async_computation | async-start | bytes 8192 | tf_op jit(solution)/shard_map/all_to_all | solution.py:164
  30.6 8.4 %collective-permute-start.1 = (bf16[24,4096]{1,0:T(8,128)(2,1)}, bf16[24,4096]{1,0:T(8,128)(2,1)S(1)}, u32[]{:S(2)}, u32[]{:S(2)}) collective-permute-start(bf16[24,4096]{1,0:T(8,128)(2,1)} %refs_1_.1), channel_id=1, source_target_pairs={{0,192},{32,96},{64,0},{96,160},{128,64},{160,224},{192,128},{224,... | collective-permute-start | bytes 589832 | tf_op jit(solution)/shard_map/ppermute | solution.py:139
  39.1 0.0 all-to-all-done
  39.1 0.5 broadcast.162
  39.6 0.7 reduce.3
  40.3 0.1 reshape.76.refs_0_
  40.3 0.0 collective-permute-done.refs_2_
  40.4 40.3 %collective-permute-start.2 = (bf16[24,4096]{1,0:T(8,128)(2,1)S(1)}, bf16[24,4096]{1,0:T(8,128)(2,1)S(1)}, u32[]{:S(2)}, u32[]{:S(2)}) collective-permute-start(bf16[24,4096]{1,0:T(8,128)(2,1)S(1)} %collective-permute-done.refs_2_), channel_id=1, source_target_pairs={{0,64},{32,224},{64,128},{96,32},{128,192},{160,96},{192,0},{224,1... | collective-permute-start | bytes 589832 | tf_op jit(solution)/shard_map/ppermute | solution.py:139
  80.7 0.0 collective-permute-done.1.refs_3_
  80.7 3.2 %collective-permute-done.2.refs_4_ = bf16[24,4096]{1,0:T(8,128)(2,1)S(1)} collective-permute-done((bf16[24,4096]{1,0:T(8,128)(2,1)S(1)}, bf16[24,4096]{1,0:T(8,128)(2,1)S(1)}, u32[]{:S(2)}, u32[]{:S(2)}) %collective-permute-start.2) | collective-permute-done | bytes 196640 | tf_op jit(solution)/shard_map/ppermute | solution.py:139
  83.9 0.0 copy-start
  83.9 0.9 copy-done
  84.8 5.8 %pack.1 = bf16[128,24,256]{2,1,0:T(8,128)(2,1)} custom-call(s32[128]{0:T(128)S(1)} %reshape.76.refs_0_, bf16[24,4096]{1,0:T(8,128)(2,1)S(1)} %copy-done, bf16[24,4096]{1,0:T(8,128)(2,1)S(1)} %collective-permute-done.refs_2_, bf16[24,4096]{1,0:T(8,128)(2,1)S(1)} %collective-permute-done.1.refs_3_, bf16[24,4096]{1,0:T(8,128)(2,1)S(1)} %collective-permute-done.2.refs_4_), custom_call_target="tpu_custom_call" | custom-call | bytes 2097152 | tf_op jit(solution)/shard_map/pack/pallas_call | solution.py:45
  90.6 0.0 copy-start.3
  90.6 5.1 %all-to-all-start.1 = ((bf16[8,16,24,256]{3,2,1,0:T(8,128)(2,1)}), bf16[8,16,24,256]{3,2,1,0:T(8,128)(2,1)S(1)}, u32[]{:S(2)}, u32[]{:S(2)}) async-start(bf16[8,16,24,256]{3,2,1,0:T(8,128)(2,1)} %bitcast.5), calls=%async_computation.1 | async-start | bytes 3145728 | tf_op jit(solution)/shard_map/all_to_all | solution.py:168
  95.8 20.1 %all-to-all-done.1 = bf16[8,16,24,256]{3,2,1,0:T(8,128)(2,1)S(1)} async-done(((bf16[8,16,24,256]{3,2,1,0:T(8,128)(2,1)}), bf16[8,16,24,256]{3,2,1,0:T(8,128)(2,1)S(1)}, u32[]{:S(2)}, u32[]{:S(2)}) %all-to-all-start.1) | async-done | bytes 1572896 | tf_op jit(solution)/shard_map/all_to_all | solution.py:168
  115.9 0.0 copy-done.3
  115.9 0.0 copy-start.4
  115.9 5.6 %aggregate.1 = bf16[32,24,128]{2,1,0:T(8,128)(2,1)} custom-call(s32[48]{0:T(128)S(1)} %multiply_add_fusion.pos, s32[16]{0:T(128)S(1)} %copy-done.3, bf16[128,24,256]{2,1,0:T(8,128)(2,1)S(1)} %bitcast.41, bf16[48,256,256]{2,1,0:T(8,128)(2,1)} %tiles.1), custom_call_target="tpu_custom_call" | custom-call | flops 150994944 | bytes 7340032 | tf_op jit(solution)/shard_map/aggregate/pallas_call | solution.py:80
  121.5 0.0 copy-start.1
  121.5 0.0 copy-start.2
  121.5 5.0 %all-to-all-start.2 = ((bf16[32,24,128]{2,1,0:T(8,128)(2,1)}), bf16[32,24,128]{2,1,0:T(8,128)(2,1)S(1)}, u32[]{:S(2)}, u32[]{:S(2)}) async-start(bf16[32,24,128]{2,1,0:T(8,128)(2,1)} %aggregate.1), calls=%async_computation.2 | async-start | bytes 393216 | tf_op jit(solution)/shard_map/all_to_all | solution.py:170
  126.5 0.0 copy-done.4
  126.5 0.3 copy.18
  126.8 16.3 %all-to-all-done.2 = bf16[32,24,128]{2,1,0:T(8,128)(2,1)S(1)} async-done(((bf16[32,24,128]{2,1,0:T(8,128)(2,1)}), bf16[32,24,128]{2,1,0:T(8,128)(2,1)S(1)}, u32[]{:S(2)}, u32[]{:S(2)}) %all-to-all-start.2) | async-done | bytes 196640 | tf_op jit(solution)/shard_map/all_to_all | solution.py:170
  143.1 0.0 copy-done.1
  143.1 0.0 copy-done.2
  143.1 1.2 dense.1
  144.3 17.0 %all_to_all.34 = bf16[32,4,24,128]{3,2,1,0:T(8,128)(2,1)S(1)} all-to-all(bf16[32,4,24,128]{3,2,1,0:T(8,128)(2,1)S(1)} %get-tuple-element.9), channel_id=1, replica_groups=mesh['x'=4,'zh'=4,'c'=2,'zl'=8,'y'=4] {'x','c','y'}, dimensions={0} | all-to-all | bytes 1572864 | tf_op jit(solution)/shard_map/all_to_all | solution.py:172
  161.3 0.1 convert_reduce_fusion
  161.4 45.3 %all_to_all.35 = f32[4,24,128]{2,1,0:T(8,128)S(1)} all-to-all(f32[4,24,128]{2,1,0:T(8,128)S(1)} %convert_reduce_fusion), channel_id=1, replica_groups=mesh['x'=4,'zh'=4,'c'=2,'zl'=8,'y'=4] {'zh'}, dimensions={0} | all-to-all | bytes 98304 | tf_op jit(solution)/shard_map/all_to_all | solution.py:174
  206.7 0.1 copy.22
  206.8 0.1 reshape.90
  206.9 14.9 %all_to_all.36 = f32[8,1,384]{2,1,0:T(1,128)S(1)} all-to-all(f32[8,1,384]{2,1,0:T(1,128)S(1)} %reshape.90), channel_id=1, replica_groups=mesh['x'=4,'zh'=4,'c'=2,'zl'=8,'y'=4] {'zl'}, dimensions={0} | all-to-all | bytes 24576 | tf_op jit(solution)/shard_map/all_to_all | solution.py:175
  221.9 0.5 broadcast.171
  222.4 0.7 reduce.4
  223.1 0.1 reshape.91
  223.2 0.1 copy.23
  223.2 0.7 copy.21
  (4 shorter events, 0.0 us)
Async XLA Ops:
  0.6 39.7 %collective-permute-start = (bf16[24,4096]{1,0:T(8,128)(2,1)}, bf16[24,4096]{1,0:T(8,128)(2,1)S(1)}, u32[]{:S(2)}, u32[]{:S(2)}) collective-permute-start(bf16[24,4096]{1,0:T(8,128)(2,1)} %refs_1_.1), channel_id=1, source_target_pairs={{0,64},{32,224},{64,128},{96,32},{128,192},{160,96},{192,0},{224,1... | collective-permute-start | bytes 589832 | tf_op jit(solution)/shard_map/ppermute | solution.py:139
  19.4 19.7 %all-to-all-start = ((s32[8,1,16]{2,1,0:T(1,128)}), s32[8,1,16]{2,1,0:T(1,128)S(1)}, u32[]{:S(2)}, u32[]{:S(2)}) async-start(s32[8,1,16]{2,1,0:T(1,128)} %bitcast.4), calls=%async_computation | async-start | bytes 8192 | tf_op jit(solution)/shard_map/all_to_all | solution.py:164
  30.6 50.1 %collective-permute-start.1 = (bf16[24,4096]{1,0:T(8,128)(2,1)}, bf16[24,4096]{1,0:T(8,128)(2,1)S(1)}, u32[]{:S(2)}, u32[]{:S(2)}) collective-permute-start(bf16[24,4096]{1,0:T(8,128)(2,1)} %refs_1_.1), channel_id=1, source_target_pairs={{0,192},{32,96},{64,0},{96,160},{128,64},{160,224},{192,128},{224,... | collective-permute-start | bytes 589832 | tf_op jit(solution)/shard_map/ppermute | solution.py:139
  40.4 43.5 %collective-permute-start.2 = (bf16[24,4096]{1,0:T(8,128)(2,1)S(1)}, bf16[24,4096]{1,0:T(8,128)(2,1)S(1)}, u32[]{:S(2)}, u32[]{:S(2)}) collective-permute-start(bf16[24,4096]{1,0:T(8,128)(2,1)S(1)} %collective-permute-done.refs_2_), channel_id=1, source_target_pairs={{0,64},{32,224},{64,128},{96,32},{128,192},{160,96},{192,0},{224,1... | collective-permute-start | bytes 589832 | tf_op jit(solution)/shard_map/ppermute | solution.py:139
  83.9 0.9 copy-start
  90.6 25.3 %copy-start.3 = (s32[16]{0:T(128)S(1)}, s32[16]{0:T(128)}, u32[]{:S(2)}) copy-start(s32[16]{0:T(128)} %counts.1) | copy-start | bytes 196
  90.6 25.3 %all-to-all-start.1 = ((bf16[8,16,24,256]{3,2,1,0:T(8,128)(2,1)}), bf16[8,16,24,256]{3,2,1,0:T(8,128)(2,1)S(1)}, u32[]{:S(2)}, u32[]{:S(2)}) async-start(bf16[8,16,24,256]{3,2,1,0:T(8,128)(2,1)} %bitcast.5), calls=%async_computation.1 | async-start | bytes 3145728 | tf_op jit(solution)/shard_map/all_to_all | solution.py:168
  115.9 10.6 %copy-start.4 = (bf16[768,512]{1,0:T(8,128)(2,1)S(1)}, bf16[768,512]{1,0:T(8,128)(2,1)}, u32[]{:S(2)}) copy-start(bf16[768,512]{1,0:T(8,128)(2,1)} %param.13) | copy-start | bytes 2359300
  121.5 21.6 %copy-start.1 = (bf16[512,128]{1,0:T(8,128)(2,1)S(1)}, bf16[512,128]{1,0:T(8,128)(2,1)}, u32[]{:S(2)}) copy-start(bf16[512,128]{1,0:T(8,128)(2,1)} %self_part.1) | copy-start | bytes 393220
  121.5 21.6 %copy-start.2 = (bf16[512,128]{1,0:T(8,128)(2,1)S(1)}, bf16[512,128]{1,0:T(8,128)(2,1)}, u32[]{:S(2)}) copy-start(bf16[512,128]{1,0:T(8,128)(2,1)} %cotangent.1) | copy-start | bytes 393220
  121.5 21.6 %all-to-all-start.2 = ((bf16[32,24,128]{2,1,0:T(8,128)(2,1)}), bf16[32,24,128]{2,1,0:T(8,128)(2,1)S(1)}, u32[]{:S(2)}, u32[]{:S(2)}) async-start(bf16[32,24,128]{2,1,0:T(8,128)(2,1)} %aggregate.1), calls=%async_computation.2 | async-start | bytes 393216 | tf_op jit(solution)/shard_map/all_to_all | solution.py:170

commit v3 on v2

--- a/solution.py
+++ b/solution.py
@@ -11,7 +11,7 @@
 MAXT = 3
 CAP = 4
 X, ZH, CORE, ZL, Y = 4, 4, 2, 8, 4
-EACH = ZH * CAP
+EACH = 2 * CAP
 VMEM = 48 * 1024 * 1024
 f32, bf16 = jnp.float32, jnp.bfloat16
 
@@ -24,27 +24,25 @@
     return pl.BlockSpec(memory_space=pltpu.SMEM)
 
 
-def pack_kernel(width, codes, *refs):
+def pack_kernel(first, width, codes, *refs):
     held, out = refs[:-1], refs[-1]
-
-    def one(i, carry):
-        code = codes[i]
-        local = code % 16
-        for j, ref in enumerate(held):
-
-            @pl.when(code // 16 == j)
-            def _(ref=ref):
-                out[i] = ref[:, pl.ds(pl.multiple_of(local * width, width), width)]
-
+    peers, each = out.shape[0], out.shape[1]
+    asked = codes.shape[0] // peers
+
+    def one(d, carry):
+        for k in range(each):
+            code = codes[d * asked + first + k]
+            place = pl.ds(pl.multiple_of(code % 16 * width, width), width)
+            out[d, k] = jnp.where(code < 16, held[0][:, place], held[1][:, place])
         return carry
 
-    lax.fori_loop(0, out.shape[0], one, 0, unroll=4)
-
-
-def pack(codes, held, width):
-    return pl.pallas_call(
-        lambda *refs: pack_kernel(width, *refs),
-        out_shape=jax.ShapeDtypeStruct((codes.shape[0], held[0].shape[0], width), held[0].dtype),
+    lax.fori_loop(0, peers, one, 0, unroll=2)
+
+
+def pack(codes, held, first, width):
+    return pl.pallas_call(
+        lambda *refs: pack_kernel(first, width, *refs),
+        out_shape=jax.ShapeDtypeStruct((X * CORE, EACH, held[0].shape[0], width), held[0].dtype),
         in_specs=[smem()] + [vmem()] * len(held),
         out_specs=vmem(),
         compiler_params=pltpu.CompilerParams(vmem_limit_bytes=VMEM),
@@ -53,7 +51,8 @@
     )(codes, *held)
 
 
-def agg_kernel(pos, counts, blocks, tiles, out):
+def agg_kernel(pos, counts, early, late, tiles, out):
+    early_size = early.shape[0]
     half = out.shape[-1]
     per = tiles.shape[1] // half
 
@@ -61,7 +60,12 @@
         count = counts[b]
         total = None
         for m in range(MAXT):
-            block = blocks[pos[b * MAXT + m]]
+            p = pos[b * MAXT + m]
+            block = jnp.where(
+                p < early_size,
+                early[jnp.minimum(p, early_size - 1)],
+                late[jnp.maximum(p - early_size, 0)],
+            )
             block = jnp.where(m < count, block, jnp.zeros_like(block))
             part = lax.dot_general(
                 block, tiles[b * MAXT + m], (((1,), (1,)), ((), ())), preferred_element_type=f32
@@ -75,17 +79,17 @@
     lax.fori_loop(0, counts.shape[0], one, 0, unroll=8)
 
 
-def aggregate(pos, counts, blocks, tiles, node_cols):
-    rows, width = blocks.shape[1:]
+def aggregate(pos, counts, early, late, tiles, node_cols):
+    rows, width = early.shape[1:]
     return pl.pallas_call(
         agg_kernel,
         out_shape=jax.ShapeDtypeStruct((counts.shape[0] * width // node_cols, rows, node_cols), bf16),
-        in_specs=[smem(), smem(), vmem(), vmem()],
+        in_specs=[smem(), smem(), vmem(), vmem(), vmem()],
         out_specs=vmem(),
         compiler_params=pltpu.CompilerParams(vmem_limit_bytes=VMEM),
         cost_estimate=pl.CostEstimate(flops=2 * 48 * 24 * 65536, bytes_accessed=7 << 20, transcendentals=0),
         name="aggregate",
-    )(pos, counts, blocks, tiles)
+    )(pos, counts, early, late, tiles)
 
 
 def dense_kernel(rows, w_t, self_part, cotangent, hidden, grad, gp):
@@ -112,6 +116,25 @@
                     grad[(x * CORE + c) * Y + y, zh] = part[start : start + chunk]
 
 
+def fold_kernel(parts, out):
+    total = jnp.sum(parts[...].astype(f32), axis=0)
+    total = jnp.concatenate([total[z] for z in range(total.shape[0])], axis=0)
+    out[...] = total.T.reshape(out.shape)
+
+
+def fold(parts):
+    chunk, lanes = parts.shape[2:]
+    return pl.pallas_call(
+        fold_kernel,
+        out_shape=jax.ShapeDtypeStruct((ZL, lanes // ZL, ZH * chunk), f32),
+        in_specs=[vmem()],
+        out_specs=vmem(),
+        compiler_params=pltpu.CompilerParams(vmem_limit_bytes=VMEM),
+        cost_estimate=pl.CostEstimate(flops=32 * 96 * 128, bytes_accessed=1 << 20, transcendentals=0),
+        name="fold",
+    )(parts)
+
+
 def dense(rows, w_t, self_part, cotangent):
     hid, nodes = self_part.shape
     width = rows.shape[0]
@@ -145,13 +168,21 @@
     core = owners % CORE
     apart = (me + ZH - owners // CORE % ZH) % ZH
     apart = jnp.where(core == 0, apart, (ZH - apart) % ZH)
-    held = jnp.where(apart == 2, 3, jnp.where(apart == 3, 2, apart))
+    second = apart > 1
+    held = (apart == 1) | (apart == 2)
     column = (owners // (ZH * CORE)) * CORE + core
+    group = column + jnp.where(second, X * CORE, 0)
     s = jnp.arange(slots, dtype=jnp.int32)
-    earlier = (column[:, None] == column[None, :]) & (s[None, :] < s[:, None])
-    pos = column * EACH + jnp.sum(earlier.astype(jnp.int32), axis=1)
-    hit = pos[:, None] == jnp.arange(X * CORE * EACH, dtype=jnp.int32)[None, :]
-    return pos, jnp.sum(jnp.where(hit, (held * 16 + local)[:, None], 0), axis=0)
+    earlier = (group[:, None] == group[None, :]) & (s[None, :] < s[:, None])
+    rank = jnp.sum(earlier.astype(jnp.int32), axis=1)
+    place = column * 2 * EACH + jnp.where(second, EACH, 0) + rank
+    hit = place[:, None] == jnp.arange(X * CORE * 2 * EACH, dtype=jnp.int32)[None, :]
+    ask = jnp.sum(jnp.where(hit, (held.astype(jnp.int32) * 16 + local)[:, None], 0), axis=0)
+    return group * EACH + rank, ask
+
+
+def exchange(packed):
+    return lax.all_to_all(packed, ("x", "c"), 0, 0).reshape((-1,) + packed.shape[2:])
 
 
 def per_device(features, counts, src_owner, src_local, tiles, w_neigh, self_part, cotangent):
@@ -159,22 +190,22 @@
     width = tiles.shape[1]
     node_cols = self_part.shape[1]
     first = onward(features, 1)
-    second = onward(features, -1)
     pos, ask = plan(src_owner[:, 0], src_local)
-    codes = lax.all_to_all(ask.reshape(X * CORE, EACH), ("x", "c"), 0, 0).reshape(-1)
-    codes, first = lax.optimization_barrier((codes, first))
+    codes = lax.all_to_all(ask.reshape(X * CORE, -1), ("x", "c"), 0, 0).reshape(-1)
+    codes, first, again = lax.optimization_barrier((codes, first, features))
     third = onward(first, 1)
-    blocks = pack(codes, (features, first, second, third), width)
-    blocks = lax.all_to_all(blocks.reshape(X * CORE, EACH, rows, width), ("x", "c"), 0, 0)
-    aggregated = aggregate(pos, counts, blocks.reshape(-1, rows, width), tiles, node_cols)
+    second = onward(again, -1)
+    early = exchange(pack(codes, (features, first), 0, width))
+    early, second, third = lax.optimization_barrier((early, second, third))
+    late = exchange(pack(codes, (second, third), EACH, width))
+    aggregated = aggregate(pos, counts, early, late, tiles, node_cols)
     node_rows = lax.all_to_all(aggregated, ("zl", "y"), 0, 0).reshape(-1, node_cols)
     hidden, grad = dense(node_rows, w_neigh.T, self_part, cotangent)
-    grad = lax.all_to_all(grad, ("x", "c", "y"), 0, 0)
-    grad = jnp.sum(grad.astype(f32), axis=0)
-    grad = jnp.sum(lax.all_to_all(grad, "zh", 0, 0), axis=0)
-    grad = lax.all_to_all(grad.T.reshape(ZL, -1, rows), "zl", 0, 0)
+    grad = fold(lax.all_to_all(grad, ("x", "c", "y"), 0, 0))
+    grad = jnp.sum(lax.all_to_all(grad, "zl", 0, 0), axis=0)
+    grad = jnp.transpose(grad.reshape(-1, ZH, rows), (1, 0, 2))
     grad_scale = 1.0 / math.sqrt(cols * X * ZH * CORE)
-    return hidden, jnp.sum(grad, axis=0) * grad_scale
+    return hidden, jnp.sum(lax.all_to_all(grad, "zh", 0, 0), axis=0) * grad_scale
 
 
 def solution(mesh):

time: 224 us -> 218 us (0.973)
  starting transfers between devices: 85.9 us -> 62.5 us
  waiting for transfers between devices: 39.6 us -> 53.8 us
  blocking collectives: 77.2 us -> 82 us
    ppermute x3, starting transfers between devices: 64.5 us -> 31.7 us  [onward(): return lax.ppermute(value, ('zh', 'c'), pairs)]
    ppermute x3, waiting for transfers between devices: 3.16 us -> 25.8 us  [onward(): return lax.ppermute(value, ('zh', 'c'), pairs)]
    all_to_all x1, starting transfers between devices: 4.99 us -> 15.2 us  [per_device(): lax.all_to_all(aggregated, ('zl', 'y'), 0, 0).reshape(-1, node_cols)]
    all_to_all x2, waiting for transfers between devices: 20.1 us -> 11.7 us  [exchange(): lax.all_to_all(packed, ('x', 'c'), 0, 0).reshape((-1,) + packed.shape[2:])]
    all_to_all x3 -> x4, blocking collectives: 77.2 us -> 82 us  [the longest x1 34.9 us: per_device(): lax.all_to_all(grad, 'zh', 0, 0)]
    pallas_call x1 -> x3, Pallas kernels: 5.83 us -> 3.73 us  [the longest x2 3.53 us: pack(): pl.pallas_call(lambda *refs: pack_kernel(first, width, *refs), out_shape=...]
where the time goes in v3:
time: 218 us; the launch traced here: 217 us
  blocking collectives  82 us (38%)
  starting transfers between devices  62.5 us (29%)
  waiting for transfers between devices  53.8 us (25%)
  Pallas kernels  10.5 us (5%)
  other arithmetic  4.31 us (2%)
  local copies, waits for them, and re-layouts  3.31 us (2%)
    all_to_all x1, blocking collectives, per_device(): lax.all_to_all(grad, 'zh', 0, 0)  34.9 us
    ppermute x3, starting transfers between devices, onward(): return lax.ppermute(value, ('zh', 'c'), pairs)  31.7 us
    ppermute x3, waiting for transfers between devices, onward(): return lax.ppermute(value, ('zh', 'c'), pairs)  25.8 us
    all_to_all x1, blocking collectives, per_device(): grad = fold(lax.all_to_all(grad, ('x', 'c', 'y'), 0, 0))  17 us
    all_to_all x1, waiting for transfers between devices, per_device(): lax.all_to_all(aggregated, ('zl', 'y'), 0, 0).reshape(-1, node_cols)  16.3 us
    all_to_all x2, starting transfers between devices, exchange(): lax.all_to_all(packed, ('x', 'c'), 0, 0).reshape((-1,) + packed.shape[2:])  15.5 us
    all_to_all x1, starting transfers between devices, per_device(): lax.all_to_all(aggregated, ('zl', 'y'), 0, 0).reshape(-1, node_cols)  15.2 us
    all_to_all x1, blocking collectives, per_device(): grad = jnp.sum(lax.all_to_all(grad, 'zl', 0, 0), axis=0)  15.2 us
  transfers between devices with their start and end apart: 6, of which 3 were waited for; matrix products, arithmetic and copies ran while one was open for 2% of the time, Pallas kernels for 0%

profile of v3, /device:TPU:2, one launch (start us, length us, event | category | flops | bytes accessed | tf_op | source)
XLA Modules:
  0.0 217.1 jit_solution(17496530671469051105)
XLA Ops:
  0.6 15.7 %collective-permute-start = (bf16[24,4096]{1,0:T(8,128)(2,1)}, bf16[24,4096]{1,0:T(8,128)(2,1)S(1)}, u32[]{:S(2)}, u32[]{:S(2)}) collective-permute-start(bf16[24,4096]{1,0:T(8,128)(2,1)} %refs_1_.1), channel_id=1, source_target_pairs={{0,64},{32,224},{64,128},{96,32},{128,192},{160,96},{192,0},{224,1... | collective-permute-start | bytes 589832 | tf_op jit(solution)/shard_map/ppermute | solution.py:162
  16.4 0.7 add_bitcast_fusion
  17.1 0.7 fusion.1
  17.8 0.7 fusion.3
  18.4 0.2 convert_reduce_fusion
  18.6 0.1 select_reduce_fusion
  18.7 0.1 all_to_all.24
  18.8 14.9 %all_to_all.39 = s32[8,1,16]{2,1,0:T(1,128)S(1)} all-to-all(s32[8,1,16]{2,1,0:T(1,128)S(1)} %bitcast.46), channel_id=1, replica_groups=mesh['x'=4,'zh'=4,'c'=2,'zl'=8,'y'=4] {'x','c'}, dimensions={0} | all-to-all | bytes 1024 | tf_op jit(solution)/shard_map/all_to_all | solution.py:194
  33.7 0.5 broadcast.359
  34.2 0.7 reduce.3
  34.9 0.1 reshape.126.refs_0_
  34.9 0.0 collective-permute-done.refs_2_
  34.9 0.0 copy-start
  34.9 0.9 copy-done
  35.9 1.8 pack.2
  37.6 0.0 copy-start.4
  37.6 10.7 %all-to-all-start.1 = ((bf16[8,8,24,256]{3,2,1,0:T(8,128)(2,1)}), bf16[8,8,24,256]{3,2,1,0:T(8,128)(2,1)S(1)}, u32[]{:S(2)}, u32[]{:S(2)}) async-start(bf16[8,8,24,256]{3,2,1,0:T(8,128)(2,1)} %pack.2), calls=%async_computation.1 | async-start | bytes 1572864 | tf_op jit(solution)/shard_map/all_to_all | solution.py:185
  48.3 14.1 %collective-permute-start.1 = (bf16[24,4096]{1,0:T(8,128)(2,1)}, bf16[24,4096]{1,0:T(8,128)(2,1)S(1)}, u32[]{:S(2)}, u32[]{:S(2)}) collective-permute-start(bf16[24,4096]{1,0:T(8,128)(2,1)} %refs_1_.1), channel_id=1, source_target_pairs={{0,192},{32,96},{64,0},{96,160},{128,64},{160,224},{192,128},{224,... | collective-permute-start | bytes 589832 | tf_op jit(solution)/shard_map/ppermute | solution.py:162
  62.4 1.9 collective-permute-start.2
  64.3 25.8 %collective-permute-done.1.refs_1_ = bf16[24,4096]{1,0:T(8,128)(2,1)S(1)} collective-permute-done((bf16[24,4096]{1,0:T(8,128)(2,1)}, bf16[24,4096]{1,0:T(8,128)(2,1)S(1)}, u32[]{:S(2)}, u32[]{:S(2)}) %collective-permute-start.1) | collective-permute-done | bytes 196640 | tf_op jit(solution)/shard_map/ppermute | solution.py:162
  90.1 0.0 collective-permute-done.2.refs_2_
  90.1 0.0 all-to-all-done.1
  90.1 0.0 copy-start.1
  90.1 0.0 copy-start.2
  90.1 1.8 pack.3
  91.9 4.8 %all-to-all-start.2 = ((bf16[8,8,24,256]{3,2,1,0:T(8,128)(2,1)}), bf16[8,8,24,256]{3,2,1,0:T(8,128)(2,1)S(1)}, u32[]{:S(2)}, u32[]{:S(2)}) async-start(bf16[8,8,24,256]{3,2,1,0:T(8,128)(2,1)} %pack.3), calls=%async_computation.2 | async-start | bytes 1572864 | tf_op jit(solution)/shard_map/all_to_all | solution.py:185
  96.7 11.7 %all-to-all-done.2 = bf16[8,8,24,256]{3,2,1,0:T(8,128)(2,1)S(1)} async-done(((bf16[8,8,24,256]{3,2,1,0:T(8,128)(2,1)}), bf16[8,8,24,256]{3,2,1,0:T(8,128)(2,1)S(1)}, u32[]{:S(2)}, u32[]{:S(2)}) %all-to-all-start.2) | async-done | bytes 786464 | tf_op jit(solution)/shard_map/all_to_all | solution.py:185
  108.4 0.0 copy-start.3
  108.4 0.7 copy-done.3
  109.1 5.5 %aggregate.1 = bf16[32,24,128]{2,1,0:T(8,128)(2,1)} custom-call(s32[48]{0:T(128)S(1)} %multiply_add_fusion.1.pos, s32[16]{0:T(128)S(1)} %copy-done.3, bf16[64,24,256]{2,1,0:T(8,128)(2,1)S(1)} %bitcast.41, bf16[64,24,256]{2,1,0:T(8,128)(2,1)S(1)} %bitcast.42, bf16[48,256,256]{2,1,0:T(8,128)(2,1)} %tiles.1), custom_call_target="tpu_custom_call" | custom-call | flops 150994944 | bytes 7340032 | tf_op jit(solution)/shard_map/aggregate/pallas_call | solution.py:84
  114.6 15.2 %all-to-all-start.3 = ((bf16[32,24,128]{2,1,0:T(8,128)(2,1)}), bf16[32,24,128]{2,1,0:T(8,128)(2,1)S(1)}, u32[]{:S(2)}, u32[]{:S(2)}) async-start(bf16[32,24,128]{2,1,0:T(8,128)(2,1)} %aggregate.1), calls=%async_computation.3 | async-start | bytes 393216 | tf_op jit(solution)/shard_map/all_to_all | solution.py:202
  129.9 0.0 copy-done.4
  129.9 0.3 copy.17
  130.2 16.3 %all-to-all-done.3 = bf16[32,24,128]{2,1,0:T(8,128)(2,1)S(1)} async-done(((bf16[32,24,128]{2,1,0:T(8,128)(2,1)}), bf16[32,24,128]{2,1,0:T(8,128)(2,1)S(1)}, u32[]{:S(2)}, u32[]{:S(2)}) %all-to-all-start.3) | async-done | bytes 196640 | tf_op jit(solution)/shard_map/all_to_all | solution.py:202
  146.4 0.0 copy-done.1
  146.4 0.0 copy-done.2
  146.4 1.2 dense.1
  147.7 17.0 %all_to_all.40.parts = bf16[32,4,24,128]{3,2,1,0:T(8,128)(2,1)S(1)} all-to-all(bf16[32,4,24,128]{3,2,1,0:T(8,128)(2,1)S(1)} %get-tuple-element.17), channel_id=1, replica_groups=mesh['x'=4,'zh'=4,'c'=2,'zl'=8,'y'=4] {'x','c','y'}, dimensions={0} | all-to-all | bytes 1572864 | tf_op jit(solution)/shard_map/all_to_all | solution.py:204
  164.7 0.2 fold.1
  164.9 15.2 %all_to_all.41 = f32[8,16,96]{2,1,0:T(8,128)S(1)} all-to-all(f32[8,16,96]{2,1,0:T(8,128)S(1)} %fold.1), channel_id=1, replica_groups=mesh['x'=4,'zh'=4,'c'=2,'zl'=8,'y'=4] {'zl'}, dimensions={0} | all-to-all | bytes 98304 | tf_op jit(solution)/shard_map/all_to_all | solution.py:205
  180.1 0.1 reshape.130
  180.2 0.1 reshape.140
  180.2 34.9 %all_to_all.42 = f32[4,1,384]{2,1,0:T(1,128)S(1)} all-to-all(f32[4,1,384]{2,1,0:T(1,128)S(1)} %reshape.140), channel_id=1, replica_groups=mesh['x'=4,'zh'=4,'c'=2,'zl'=8,'y'=4] {'zh'}, dimensions={0} | all-to-all | bytes 12288 | tf_op jit(solution)/shard_map/all_to_all | solution.py:208
  215.2 0.5 broadcast.369
  215.7 0.7 reduce.4
  216.4 0.1 reshape.141
  216.5 0.6 broadcast_multiply_fusion
  (5 shorter events, 0.0 us)
Async XLA Ops:
  0.6 34.3 %collective-permute-start = (bf16[24,4096]{1,0:T(8,128)(2,1)}, bf16[24,4096]{1,0:T(8,128)(2,1)S(1)}, u32[]{:S(2)}, u32[]{:S(2)}) collective-permute-start(bf16[24,4096]{1,0:T(8,128)(2,1)} %refs_1_.1), channel_id=1, source_target_pairs={{0,64},{32,224},{64,128},{96,32},{128,192},{160,96},{192,0},{224,1... | collective-permute-start | bytes 589832 | tf_op jit(solution)/shard_map/ppermute | solution.py:162
  34.9 0.9 copy-start
  37.6 92.2 %copy-start.4 = (bf16[768,512]{1,0:T(8,128)(2,1)S(1)}, bf16[768,512]{1,0:T(8,128)(2,1)}, u32[]{:S(2)}) copy-start(bf16[768,512]{1,0:T(8,128)(2,1)} %param.13) | copy-start | bytes 2359300
  37.6 52.5 %all-to-all-start.1 = ((bf16[8,8,24,256]{3,2,1,0:T(8,128)(2,1)}), bf16[8,8,24,256]{3,2,1,0:T(8,128)(2,1)S(1)}, u32[]{:S(2)}, u32[]{:S(2)}) async-start(bf16[8,8,24,256]{3,2,1,0:T(8,128)(2,1)} %pack.2), calls=%async_computation.1 | async-start | bytes 1572864 | tf_op jit(solution)/shard_map/all_to_all | solution.py:185
  48.3 41.8 %collective-permute-start.1 = (bf16[24,4096]{1,0:T(8,128)(2,1)}, bf16[24,4096]{1,0:T(8,128)(2,1)S(1)}, u32[]{:S(2)}, u32[]{:S(2)}) collective-permute-start(bf16[24,4096]{1,0:T(8,128)(2,1)} %refs_1_.1), channel_id=1, source_target_pairs={{0,192},{32,96},{64,0},{96,160},{128,64},{160,224},{192,128},{224,... | collective-permute-start | bytes 589832 | tf_op jit(solution)/shard_map/ppermute | solution.py:162
  62.4 27.7 %collective-permute-start.2 = (bf16[24,4096]{1,0:T(8,128)(2,1)S(1)}, bf16[24,4096]{1,0:T(8,128)(2,1)S(1)}, u32[]{:S(2)}, u32[]{:S(2)}) collective-permute-start(bf16[24,4096]{1,0:T(8,128)(2,1)S(1)} %collective-permute-done.refs_2_), channel_id=1, source_target_pairs={{0,64},{32,224},{64,128},{96,32},{128,192},{160,96},{192,0},{224,1... | collective-permute-start | bytes 589832 | tf_op jit(solution)/shard_map/ppermute | solution.py:162
  90.1 56.3 %copy-start.1 = (bf16[512,128]{1,0:T(8,128)(2,1)S(1)}, bf16[512,128]{1,0:T(8,128)(2,1)}, u32[]{:S(2)}) copy-start(bf16[512,128]{1,0:T(8,128)(2,1)} %self_part.1) | copy-start | bytes 393220
  90.1 56.3 %copy-start.2 = (bf16[512,128]{1,0:T(8,128)(2,1)S(1)}, bf16[512,128]{1,0:T(8,128)(2,1)}, u32[]{:S(2)}) copy-start(bf16[512,128]{1,0:T(8,128)(2,1)} %cotangent.1) | copy-start | bytes 393220
  91.9 16.5 %all-to-all-start.2 = ((bf16[8,8,24,256]{3,2,1,0:T(8,128)(2,1)}), bf16[8,8,24,256]{3,2,1,0:T(8,128)(2,1)S(1)}, u32[]{:S(2)}, u32[]{:S(2)}) async-start(bf16[8,8,24,256]{3,2,1,0:T(8,128)(2,1)} %pack.3), calls=%async_computation.2 | async-start | bytes 1572864 | tf_op jit(solution)/shard_map/all_to_all | solution.py:185
  108.4 0.7 copy-start.3
  114.6 31.8 %all-to-all-start.3 = ((bf16[32,24,128]{2,1,0:T(8,128)(2,1)}), bf16[32,24,128]{2,1,0:T(8,128)(2,1)S(1)}, u32[]{:S(2)}, u32[]{:S(2)}) async-start(bf16[32,24,128]{2,1,0:T(8,128)(2,1)} %aggregate.1), calls=%async_computation.3 | async-start | bytes 393216 | tf_op jit(solution)/shard_map/all_to_all | solution.py:202

commit v4 on v3

--- a/solution.py
+++ b/solution.py
@@ -12,7 +12,7 @@
 CAP = 4
 X, ZH, CORE, ZL, Y = 4, 4, 2, 8, 4
 EACH = 2 * CAP
-VMEM = 48 * 1024 * 1024
+VMEM = 16 * 1024 * 1024
 f32, bf16 = jnp.float32, jnp.bfloat16
 
 
@@ -26,6 +26,7 @@
 
 def pack_kernel(first, width, codes, *refs):
     held, out = refs[:-1], refs[-1]
+    stacked = len(held) == 1
     peers, each = out.shape[0], out.shape[1]
     asked = codes.shape[0] // peers
 
@@ -33,7 +34,10 @@
         for k in range(each):
             code = codes[d * asked + first + k]
             place = pl.ds(pl.multiple_of(code % 16 * width, width), width)
-            out[d, k] = jnp.where(code < 16, held[0][:, place], held[1][:, place])
+            if stacked:
+                out[d, k] = held[0][code // 16, :, place]
+            else:
+                out[d, k] = jnp.where(code < 16, held[0][:, place], held[1][:, place])
         return carry
 
     lax.fori_loop(0, peers, one, 0, unroll=2)
@@ -42,7 +46,7 @@
 def pack(codes, held, first, width):
     return pl.pallas_call(
         lambda *refs: pack_kernel(first, width, *refs),
-        out_shape=jax.ShapeDtypeStruct((X * CORE, EACH, held[0].shape[0], width), held[0].dtype),
+        out_shape=jax.ShapeDtypeStruct((X * CORE, EACH, held[0].shape[-2], width), held[0].dtype),
         in_specs=[smem()] + [vmem()] * len(held),
         out_specs=vmem(),
         compiler_params=pltpu.CompilerParams(vmem_limit_bytes=VMEM),
@@ -51,12 +55,20 @@
     )(codes, *held)
 
 
-def agg_kernel(pos, counts, early, late, tiles, out):
+def agg_kernel(pos, counts, early, late, tiles_in, out, tiles, arrived):
     early_size = early.shape[0]
     half = out.shape[-1]
     per = tiles.shape[1] // half
 
+    def fetch(b):
+        own = pl.ds(b * MAXT, MAXT)
+        return pltpu.make_async_copy(tiles_in.at[own], tiles.at[own], arrived.at[b])
+
+    for b in range(counts.shape[0]):
+        fetch(b).start()
+
     def one(b, carry):
+        fetch(b).wait()
         count = counts[b]
         total = None
         for m in range(MAXT):
@@ -84,9 +96,10 @@
     return pl.pallas_call(
         agg_kernel,
         out_shape=jax.ShapeDtypeStruct((counts.shape[0] * width // node_cols, rows, node_cols), bf16),
-        in_specs=[smem(), smem(), vmem(), vmem(), vmem()],
+        in_specs=[smem(), smem(), vmem(), vmem(), pl.BlockSpec(memory_space=pltpu.HBM)],
         out_specs=vmem(),
-        compiler_params=pltpu.CompilerParams(vmem_limit_bytes=VMEM),
+        scratch_shapes=[pltpu.VMEM(tiles.shape, tiles.dtype), pltpu.SemaphoreType.DMA(counts.shape)],
+        compiler_params=pltpu.CompilerParams(vmem_limit_bytes=50 * 1024 * 1024),
         cost_estimate=pl.CostEstimate(flops=2 * 48 * 24 * 65536, bytes_accessed=7 << 20, transcendentals=0),
         name="aggregate",
     )(pos, counts, early, late, tiles)
@@ -154,11 +167,11 @@
     )(rows, w_t, self_part, cotangent)
 
 
-def onward(value, step):
+def onward(value):
     pairs = []
     for z in range(ZH):
-        pairs.append((z * CORE, (z + step) % ZH * CORE))
-        pairs.append((z * CORE + 1, (z - step) % ZH * CORE + 1))
+        pairs.append((z * CORE, (z + 1) % ZH * CORE))
+        pairs.append((z * CORE + 1, (z - 1) % ZH * CORE + 1))
     return lax.ppermute(value, ("zh", "c"), pairs)
 
 
@@ -166,11 +179,11 @@
     me = lax.axis_index("zh")
     slots = owners.shape[0]
     core = owners % CORE
-    apart = (me + ZH - owners // CORE % ZH) % ZH
-    apart = jnp.where(core == 0, apart, (ZH - apart) % ZH)
-    second = apart > 1
-    held = (apart == 1) | (apart == 2)
-    column = (owners // (ZH * CORE)) * CORE + core
+    apart = (owners // CORE + ZH - me) % ZH
+    server = jnp.where(apart == 3, 0, jnp.where(apart == 1, 1, core))
+    second = (apart == 2) | ((apart % 2 == 1) & (server != core))
+    held = (apart == 2) | ((apart % 2 == 1) & (server == core))
+    column = (owners // (ZH * CORE)) * CORE + server
     group = column + jnp.where(second, X * CORE, 0)
     s = jnp.arange(slots, dtype=jnp.int32)
     earlier = (group[:, None] == group[None, :]) & (s[None, :] < s[:, None])
@@ -189,15 +202,20 @@
     rows, cols = features.shape
     width = tiles.shape[1]
     node_cols = self_part.shape[1]
-    first = onward(features, 1)
+    first = onward(features)
+    other = lax.ppermute(features, "c", [(0, 1), (1, 0)])
     pos, ask = plan(src_owner[:, 0], src_local)
+    ask, other = lax.optimization_barrier((ask, other))
     codes = lax.all_to_all(ask.reshape(X * CORE, -1), ("x", "c"), 0, 0).reshape(-1)
-    codes, first, again = lax.optimization_barrier((codes, first, features))
-    third = onward(first, 1)
-    second = onward(again, -1)
-    early = exchange(pack(codes, (features, first), 0, width))
-    early, second, third = lax.optimization_barrier((early, second, third))
-    late = exchange(pack(codes, (second, third), EACH, width))
+    codes, first, other = lax.optimization_barrier((codes, first, other))
+    late = onward(jnp.concatenate([other[None], first[None]]))
+    early = lax.cond(
+        counts[0] > 0,
+        lambda: exchange(pack(codes, (features, first), 0, width)),
+        lambda: jnp.zeros((X * CORE * EACH, rows, width), bf16),
+    )
+    early, late = lax.optimization_barrier((early, late))
+    late = exchange(pack(codes, (late,), EACH, width))
     aggregated = aggregate(pos, counts, early, late, tiles, node_cols)
     node_rows = lax.all_to_all(aggregated, ("zl", "y"), 0, 0).reshape(-1, node_cols)
     hidden, grad = dense(node_rows, w_neigh.T, self_part, cotangent)

time: 218 us -> 208 us (0.954)
  blocking collectives: 82 us -> 104 us
  starting transfers between devices: 62.5 us -> 46.6 us
  waiting for transfers between devices: 53.8 us -> 37.9 us
    all_to_all x0 -> x1, blocking collectives: none -> 21.2 us  [exchange(): lax.all_to_all(packed, ('x', 'c'), 0, 0).reshape((-1,) + packed.shape[2:])]
    ppermute x3 -> x2, waiting for transfers between devices: 25.8 us -> 9.93 us  [onward(): return lax.ppermute(value, ('zh', 'c'), pairs)]
    all_to_all x2 -> x1, starting transfers between devices: 15.5 us -> 5.8 us  [exchange(): lax.all_to_all(packed, ('x', 'c'), 0, 0).reshape((-1,) + packed.shape[2:])]
    all_to_all x1, starting transfers between devices: 15.2 us -> 9.56 us  [per_device(): lax.all_to_all(aggregated, ('zl', 'y'), 0, 0).reshape(-1, node_cols)]
    ppermute x3 -> x2, starting transfers between devices: 31.7 us -> 29.3 us  [onward(): return lax.ppermute(value, ('zh', 'c'), pairs)]
    all_to_all x2 -> x1, waiting for transfers between devices: 11.7 us -> 11.7 us  [exchange(): lax.all_to_all(packed, ('x', 'c'), 0, 0).reshape((-1,) + packed.shape[2:])]
  transfers between devices with their start and end apart: 6 -> 5, of which waited for: 3 -> 3; matrix products, arithmetic and copies ran while one was open for 2% -> 2% of each run, Pallas kernels for 0% -> 1%
where the time goes in v4:
time: 208 us
  blocking collectives  104 us (50%)
  starting transfers between devices  46.6 us (22%)
  waiting for transfers between devices  37.9 us (18%)
  Pallas kernels  12.2 us (6%)
  other arithmetic  4.35 us (2%)
    all_to_all x1, blocking collectives, per_device(): lax.all_to_all(grad, 'zh', 0, 0)  34.8 us
    ppermute x2, starting transfers between devices, onward(): return lax.ppermute(value, ('zh', 'c'), pairs)  29.3 us
    all_to_all x1, blocking collectives, exchange(): lax.all_to_all(packed, ('x', 'c'), 0, 0).reshape((-1,) + packed.shape[2:])  21.2 us
    all_to_all x1, blocking collectives, per_device(): grad = fold(lax.all_to_all(grad, ('x', 'c', 'y'), 0, 0))  17 us
    all_to_all x1, waiting for transfers between devices, per_device(): lax.all_to_all(aggregated, ('zl', 'y'), 0, 0).reshape(-1, node_cols)  16.3 us
    all_to_all x1, blocking collectives, per_device(): lax.all_to_all(ask.reshape(X * CORE, -1), ('x', 'c'), 0, 0).reshape(-1)  15.5 us
    all_to_all x1, blocking collectives, per_device(): grad = jnp.sum(lax.all_to_all(grad, 'zl', 0, 0), axis=0)  15.2 us
    all_to_all x1, waiting for transfers between devices, exchange(): lax.all_to_all(packed, ('x', 'c'), 0, 0).reshape((-1,) + packed.shape[2:])  11.7 us
  transfers between devices with their start and end apart: 5, of which 3 were waited for; matrix products, arithmetic and copies ran while one was open for 2% of the time, Pallas kernels for 1%

profile of v4, /device:TPU:2, one launch (start us, length us, event | category | flops | bytes accessed | tf_op | source)
XLA Modules:
  0.0 207.9 jit_solution(11379225852998918590)
XLA Ops:
  0.6 0.0 copy-start.2
  0.6 1.9 collective-permute-start
  2.6 15.7 %collective-permute-start.1 = (bf16[24,4096]{1,0:T(8,128)(2,1)}, bf16[24,4096]{1,0:T(8,128)(2,1)S(1)}, u32[]{:S(2)}, u32[]{:S(2)}) collective-permute-start(bf16[24,4096]{1,0:T(8,128)(2,1)} %param.10), channel_id=1, source_target_pairs={{0,64},{32,224},{64,128},{96,32},{128,192},{160,96},{192,0},{224,1... | collective-permute-start | bytes 589832 | tf_op jit(solution)/shard_map/ppermute | solution.py:175
  18.3 0.7 add_bitcast_fusion
  19.0 0.7 fusion.6
  19.7 0.7 add_add_fusion
  20.4 0.2 convert_reduce_fusion
  20.6 0.1 select_reduce_fusion
  20.7 0.0 collective-permute-done
  20.7 0.1 all_to_all.24
  20.8 15.5 %all_to_all.39 = s32[8,1,16]{2,1,0:T(1,128)S(1)} all-to-all(s32[8,1,16]{2,1,0:T(1,128)S(1)} %bitcast.55), channel_id=1, replica_groups=mesh['x'=4,'zh'=4,'c'=2,'zl'=8,'y'=4] {'x','c'}, dimensions={0} | all-to-all | bytes 1024 | tf_op jit(solution)/shard_map/all_to_all | solution.py:209
  36.3 0.5 broadcast.374
  36.8 0.7 reduce.3
  37.5 0.1 reshape.125.refs_0_
  37.5 0.0 collective-permute-done.1
  37.6 13.6 %collective-permute-start.2 = (bf16[2,24,4096]{2,1,0:T(8,128)(2,1)S(1)}, bf16[2,24,4096]{2,1,0:T(8,128)(2,1)S(1)}, u32[]{:S(2)}, u32[]{:S(2)}) collective-permute-start(bf16[2,24,4096]{2,1,0:T(8,128)(2,1)S(1)} %pad_maximum_fusion), channel_id=1, source_target_pairs={{0,64},{32,224},{64,128},{96,32},{128,192},{160,96},{192,0},{224,1... | collective-permute-start | bytes 1179656 | tf_op jit(solution)/shard_map/ppermute | solution.py:175
  51.9 22.5 %conditional.1 = (bf16[64,24,256]{2,1,0:T(8,128)(2,1)S(1)}) conditional(s32[]{:T(128)} %bitcast.3, () %tuple.17, (s32[128]{0:T(128)S(1)}, bf16[24,4096]{1,0:T(8,128)(2,1)}, bf16[24,4096]{1,0:T(8,128)(2,1)S(1)}) %tuple.20), branch_computations={%region_2.3_spmd, %region_3.4_spmd} | conditional | bytes 3670024 | solution.py:212
  51.9 1.3 pack.2
  53.2 21.2 %all_to_all.38 = bf16[8,8,24,256]{3,2,1,0:T(8,128)(2,1)S(1)} all-to-all(bf16[8,8,24,256]{3,2,1,0:T(8,128)(2,1)S(1)} %pack.2), channel_id=1, replica_groups=mesh['x'=4,'zh'=4,'c'=2,'zl'=8,'y'=4] {'x','c'}, dimensions={0} | all-to-all | bytes 1572864 | tf_op jit(solution)/shard_map/cond/branch_1_fun/all_to_all | solution.py:198
  74.4 0.0 copy-start.3
  74.4 0.0 copy-start
  74.4 0.0 copy-start.1
  74.4 9.9 %collective-permute-done.2.refs_1_ = bf16[2,24,4096]{2,1,0:T(8,128)(2,1)S(1)} collective-permute-done((bf16[2,24,4096]{2,1,0:T(8,128)(2,1)S(1)}, bf16[2,24,4096]{2,1,0:T(8,128)(2,1)S(1)}, u32[]{:S(2)}, u32[]{:S(2)}) %collective-permute-start.2) | collective-permute-done | bytes 393248 | tf_op jit(solution)/shard_map/ppermute | solution.py:175
  84.3 1.9 pack.3
  86.2 5.8 %all-to-all-start.2 = ((bf16[8,8,24,256]{3,2,1,0:T(8,128)(2,1)}), bf16[8,8,24,256]{3,2,1,0:T(8,128)(2,1)S(1)}, u32[]{:S(2)}, u32[]{:S(2)}) async-start(bf16[8,8,24,256]{3,2,1,0:T(8,128)(2,1)} %pack.3), calls=%async_computation.2 | async-start | bytes 1572864 | tf_op jit(solution)/shard_map/all_to_all | solution.py:198
  92.0 11.7 %all-to-all-done.2 = bf16[8,8,24,256]{3,2,1,0:T(8,128)(2,1)S(1)} async-done(((bf16[8,8,24,256]{3,2,1,0:T(8,128)(2,1)}), bf16[8,8,24,256]{3,2,1,0:T(8,128)(2,1)S(1)}, u32[]{:S(2)}, u32[]{:S(2)}) %all-to-all-start.2) | async-done | bytes 786464 | tf_op jit(solution)/shard_map/all_to_all | solution.py:198
  103.7 0.0 copy-done.2
  103.7 7.5 %aggregate.1 = bf16[32,24,128]{2,1,0:T(8,128)(2,1)} custom-call(s32[48]{0:T(128)S(1)} %multiply_add_fusion.1.pos, s32[16]{0:T(128)S(1)} %copy-done.2, bf16[64,24,256]{2,1,0:T(8,128)(2,1)S(1)} %get-tuple-element.37.early, bf16[64,24,256]{2,1,0:T(8,128)(2,1)S(1)} %bitcast.47, bf16[48,256,256]{2,1,0:T(8,128)(2,1)} %tiles_in.1), custom_call_target="tpu_custom_call" | custom-call | flops 150994944 | bytes 7340032 | tf_op jit(solution)/shard_map/aggregate/pallas_call | solution.py:96
  111.3 9.6 %all-to-all-start.3 = ((bf16[32,24,128]{2,1,0:T(8,128)(2,1)}), bf16[32,24,128]{2,1,0:T(8,128)(2,1)S(1)}, u32[]{:S(2)}, u32[]{:S(2)}) async-start(bf16[32,24,128]{2,1,0:T(8,128)(2,1)} %aggregate.1), calls=%async_computation.3 | async-start | bytes 393216 | tf_op jit(solution)/shard_map/all_to_all | solution.py:220
  120.8 0.0 copy-done.3
  120.9 0.3 copy.17
  121.1 16.3 %all-to-all-done.3 = bf16[32,24,128]{2,1,0:T(8,128)(2,1)S(1)} async-done(((bf16[32,24,128]{2,1,0:T(8,128)(2,1)}), bf16[32,24,128]{2,1,0:T(8,128)(2,1)S(1)}, u32[]{:S(2)}, u32[]{:S(2)}) %all-to-all-start.3) | async-done | bytes 196640 | tf_op jit(solution)/shard_map/all_to_all | solution.py:220
  137.4 0.0 copy-done
  137.4 0.0 copy-done.1
  137.4 1.2 dense.1
  138.6 17.0 %all_to_all.40.parts = bf16[32,4,24,128]{3,2,1,0:T(8,128)(2,1)S(1)} all-to-all(bf16[32,4,24,128]{3,2,1,0:T(8,128)(2,1)S(1)} %get-tuple-element.31), channel_id=1, replica_groups=mesh['x'=4,'zh'=4,'c'=2,'zl'=8,'y'=4] {'x','c','y'}, dimensions={0} | all-to-all | bytes 1572864 | tf_op jit(solution)/shard_map/all_to_all | solution.py:222
  155.6 0.2 fold.1
  155.8 15.2 %all_to_all.41 = f32[8,16,96]{2,1,0:T(8,128)S(1)} all-to-all(f32[8,16,96]{2,1,0:T(8,128)S(1)} %fold.1), channel_id=1, replica_groups=mesh['x'=4,'zh'=4,'c'=2,'zl'=8,'y'=4] {'zl'}, dimensions={0} | all-to-all | bytes 98304 | tf_op jit(solution)/shard_map/all_to_all | solution.py:223
  171.0 0.1 reshape.128
  171.1 0.1 reshape.139
  171.2 34.8 %all_to_all.42 = f32[4,1,384]{2,1,0:T(1,128)S(1)} all-to-all(f32[4,1,384]{2,1,0:T(1,128)S(1)} %reshape.139), channel_id=1, replica_groups=mesh['x'=4,'zh'=4,'c'=2,'zl'=8,'y'=4] {'zh'}, dimensions={0} | all-to-all | bytes 12288 | tf_op jit(solution)/shard_map/all_to_all | solution.py:226
  206.0 0.5 broadcast.386
  206.5 0.7 reduce.4
  207.2 0.1 reshape.140
  207.3 0.6 broadcast_multiply_fusion
  (6 shorter events, 0.1 us)
Async XLA Ops:
  0.6 103.1 %copy-start.2 = (s32[16]{0:T(128)S(1)}, s32[16]{0:T(128)}, u32[]{:S(2)}) copy-start(s32[16]{0:T(128)} %counts.1) | copy-start | bytes 196
  0.6 20.0 %collective-permute-start = (bf16[24,4096]{1,0:T(8,128)(2,1)}, bf16[24,4096]{1,0:T(8,128)(2,1)S(1)}, u32[]{:S(2)}, u32[]{:S(2)}) collective-permute-start(bf16[24,4096]{1,0:T(8,128)(2,1)} %param.10), channel_id=1, source_target_pairs={{0,32},{32,0},{1,33},{33,1},{2,34},{34,2},{3,35},{35,3},{4,36},{36... | collective-permute-start | bytes 589832 | tf_op jit(solution)/shard_map/ppermute | solution.py:206
  2.6 35.0 %collective-permute-start.1 = (bf16[24,4096]{1,0:T(8,128)(2,1)}, bf16[24,4096]{1,0:T(8,128)(2,1)S(1)}, u32[]{:S(2)}, u32[]{:S(2)}) collective-permute-start(bf16[24,4096]{1,0:T(8,128)(2,1)} %param.10), channel_id=1, source_target_pairs={{0,64},{32,224},{64,128},{96,32},{128,192},{160,96},{192,0},{224,1... | collective-permute-start | bytes 589832 | tf_op jit(solution)/shard_map/ppermute | solution.py:175
  37.6 46.7 %collective-permute-start.2 = (bf16[2,24,4096]{2,1,0:T(8,128)(2,1)S(1)}, bf16[2,24,4096]{2,1,0:T(8,128)(2,1)S(1)}, u32[]{:S(2)}, u32[]{:S(2)}) collective-permute-start(bf16[2,24,4096]{2,1,0:T(8,128)(2,1)S(1)} %pad_maximum_fusion), channel_id=1, source_target_pairs={{0,64},{32,224},{64,128},{96,32},{128,192},{160,96},{192,0},{224,1... | collective-permute-start | bytes 1179656 | tf_op jit(solution)/shard_map/ppermute | solution.py:175
  74.4 46.5 %copy-start.3 = (bf16[768,512]{1,0:T(8,128)(2,1)S(1)}, bf16[768,512]{1,0:T(8,128)(2,1)}, u32[]{:S(2)}) copy-start(bf16[768,512]{1,0:T(8,128)(2,1)} %param.15) | copy-start | bytes 2359300
  74.4 63.0 %copy-start = (bf16[512,128]{1,0:T(8,128)(2,1)S(1)}, bf16[512,128]{1,0:T(8,128)(2,1)}, u32[]{:S(2)}) copy-start(bf16[512,128]{1,0:T(8,128)(2,1)} %self_part.1) | copy-start | bytes 393220
  74.4 63.0 %copy-start.1 = (bf16[512,128]{1,0:T(8,128)(2,1)S(1)}, bf16[512,128]{1,0:T(8,128)(2,1)}, u32[]{:S(2)}) copy-start(bf16[512,128]{1,0:T(8,128)(2,1)} %cotangent.1) | copy-start | bytes 393220
  86.2 17.5 %all-to-all-start.2 = ((bf16[8,8,24,256]{3,2,1,0:T(8,128)(2,1)}), bf16[8,8,24,256]{3,2,1,0:T(8,128)(2,1)S(1)}, u32[]{:S(2)}, u32[]{:S(2)}) async-start(bf16[8,8,24,256]{3,2,1,0:T(8,128)(2,1)} %pack.3), calls=%async_computation.2 | async-start | bytes 1572864 | tf_op jit(solution)/shard_map/all_to_all | solution.py:198
  111.3 26.1 %all-to-all-start.3 = ((bf16[32,24,128]{2,1,0:T(8,128)(2,1)}), bf16[32,24,128]{2,1,0:T(8,128)(2,1)S(1)}, u32[]{:S(2)}, u32[]{:S(2)}) async-start(bf16[32,24,128]{2,1,0:T(8,128)(2,1)} %aggregate.1), calls=%async_computation.3 | async-start | bytes 393216 | tf_op jit(solution)/shard_map/all_to_all | solution.py:220

commit v5 on v4

--- a/solution.py
+++ b/solution.py
@@ -12,6 +12,7 @@
 CAP = 4
 X, ZH, CORE, ZL, Y = 4, 4, 2, 8, 4
 EACH = 2 * CAP
+GROUPS = 4
 VMEM = 16 * 1024 * 1024
 f32, bf16 = jnp.float32, jnp.bfloat16
 
@@ -59,36 +60,39 @@
     early_size = early.shape[0]
     half = out.shape[-1]
     per = tiles.shape[1] // half
-
-    def fetch(b):
-        own = pl.ds(b * MAXT, MAXT)
-        return pltpu.make_async_copy(tiles_in.at[own], tiles.at[own], arrived.at[b])
-
-    for b in range(counts.shape[0]):
-        fetch(b).start()
-
-    def one(b, carry):
-        fetch(b).wait()
-        count = counts[b]
-        total = None
-        for m in range(MAXT):
-            p = pos[b * MAXT + m]
-            block = jnp.where(
-                p < early_size,
-                early[jnp.minimum(p, early_size - 1)],
-                late[jnp.maximum(p - early_size, 0)],
-            )
-            block = jnp.where(m < count, block, jnp.zeros_like(block))
-            part = lax.dot_general(
-                block, tiles[b * MAXT + m], (((1,), (1,)), ((), ())), preferred_element_type=f32
-            )
-            total = part if m == 0 else total + part
-        total = (total / count.astype(f32)).astype(out.dtype)
-        for j in range(per):
-            out[b * per + j] = total[:, j * half : (j + 1) * half]
+    groups = arrived.shape[0]
+    size = counts.shape[0] // groups
+
+    def fetch(g):
+        own = pl.ds(g * size * MAXT, size * MAXT)
+        return pltpu.make_async_copy(tiles_in.at[own], tiles.at[own], arrived.at[g])
+
+    for g in range(groups):
+        fetch(g).start()
+
+    def one(g, carry):
+        fetch(g).wait()
+        for b in [g * size + i for i in range(size)]:
+            count = counts[b]
+            total = None
+            for m in range(MAXT):
+                p = pos[b * MAXT + m]
+                block = jnp.where(
+                    p < early_size,
+                    early[jnp.minimum(p, early_size - 1)],
+                    late[jnp.maximum(p - early_size, 0)],
+                )
+                block = jnp.where(m < count, block, jnp.zeros_like(block))
+                part = lax.dot_general(
+                    block, tiles[b * MAXT + m], (((1,), (1,)), ((), ())), preferred_element_type=f32
+                )
+                total = part if m == 0 else total + part
+            total = (total / count.astype(f32)).astype(out.dtype)
+            for j in range(per):
+                out[b * per + j] = total[:, j * half : (j + 1) * half]
         return carry
 
-    lax.fori_loop(0, counts.shape[0], one, 0, unroll=8)
+    lax.fori_loop(0, groups, one, 0)
 
 
 def aggregate(pos, counts, early, late, tiles, node_cols):
@@ -98,7 +102,7 @@
         out_shape=jax.ShapeDtypeStruct((counts.shape[0] * width // node_cols, rows, node_cols), bf16),
         in_specs=[smem(), smem(), vmem(), vmem(), pl.BlockSpec(memory_space=pltpu.HBM)],
         out_specs=vmem(),
-        scratch_shapes=[pltpu.VMEM(tiles.shape, tiles.dtype), pltpu.SemaphoreType.DMA(counts.shape)],
+        scratch_shapes=[pltpu.VMEM(tiles.shape, tiles.dtype), pltpu.SemaphoreType.DMA((GROUPS,))],
         compiler_params=pltpu.CompilerParams(vmem_limit_bytes=50 * 1024 * 1024),
         cost_estimate=pl.CostEstimate(flops=2 * 48 * 24 * 65536, bytes_accessed=7 << 20, transcendentals=0),
         name="aggregate",
@@ -202,17 +206,27 @@
     rows, cols = features.shape
     width = tiles.shape[1]
     node_cols = self_part.shape[1]
+    peers = X * CORE
+    live = counts[0] > 0
+
+    def asking():
+        pos, ask = plan(src_owner[:, 0], src_local)
+        other = lax.ppermute(features, "c", [(0, 1), (1, 0)])
+        codes = lax.all_to_all(ask.reshape(peers, -1), ("x", "c"), 0, 0)
+        return pos, codes.reshape(-1), other
+
     first = onward(features)
-    other = lax.ppermute(features, "c", [(0, 1), (1, 0)])
-    pos, ask = plan(src_owner[:, 0], src_local)
-    ask, other = lax.optimization_barrier((ask, other))
-    codes = lax.all_to_all(ask.reshape(X * CORE, -1), ("x", "c"), 0, 0).reshape(-1)
+    pos, codes, other = lax.cond(
+        live,
+        asking,
+        lambda: (jnp.zeros_like(src_local), jnp.zeros((2 * peers * EACH,), jnp.int32), jnp.zeros_like(features)),
+    )
     codes, first, other = lax.optimization_barrier((codes, first, other))
     late = onward(jnp.concatenate([other[None], first[None]]))
     early = lax.cond(
-        counts[0] > 0,
+        live,
         lambda: exchange(pack(codes, (features, first), 0, width)),
-        lambda: jnp.zeros((X * CORE * EACH, rows, width), bf16),
+        lambda: jnp.zeros((peers * EACH, rows, width), bf16),
     )
     early, late = lax.optimization_barrier((early, late))
     late = exchange(pack(codes, (late,), EACH, width))

time: 208 us -> 204 us (0.981)
  waiting for transfers between devices: 37.9 us -> 28.1 us
  starting transfers between devices: 46.6 us -> 51.1 us
  Pallas kernels: 12.2 us -> 8.7 us
  blocking collectives: 104 us -> 107 us
    all_to_all x1 -> x2, blocking collectives: 21.2 us -> 39.2 us  [exchange(): lax.all_to_all(packed, ('x', 'c'), 0, 0).reshape((-1,) + packed.shape[2:])]
    all_to_all x1 -> x0, blocking collectives: 15.5 us -> none  [per_device(): lax.all_to_all(ask.reshape(X * CORE, -1), ('x', 'c'), 0, 0).reshape(-1)]
    all_to_all x1, waiting for transfers between devices: 11.7 us -> 1.66 us  [asking(): codes = lax.all_to_all(ask.reshape(peers, -1), ('x', 'c'), 0, 0)]
    all_to_all x1, starting transfers between devices: 5.8 us -> 11.3 us  [asking(): codes = lax.all_to_all(ask.reshape(peers, -1), ('x', 'c'), 0, 0)]
    pallas_call x1, Pallas kernels: 7.55 us -> 4.96 us  [aggregate(): pl.pallas_call(agg_kernel, out_shape=jax.ShapeDtypeStruct((counts.shape[0...]
where the time goes in v5:
time: 204 us
  blocking collectives  107 us (52%)
  starting transfers between devices  51.1 us (25%)
  waiting for transfers between devices  28.1 us (14%)
  Pallas kernels  8.7 us (4%)
  other arithmetic  5.27 us (3%)
  local copies, waits for them, and re-layouts  2.34 us (1%)
    all_to_all x2, blocking collectives, exchange(): lax.all_to_all(packed, ('x', 'c'), 0, 0).reshape((-1,) + packed.shape[2:])  39.2 us
    all_to_all x1, blocking collectives, per_device(): lax.all_to_all(grad, 'zh', 0, 0)  35.5 us
    ppermute x2, starting transfers between devices, onward(): return lax.ppermute(value, ('zh', 'c'), pairs)  28.6 us
    all_to_all x1, blocking collectives, per_device(): grad = fold(lax.all_to_all(grad, ('x', 'c', 'y'), 0, 0))  17 us
    all_to_all x1, waiting for transfers between devices, per_device(): lax.all_to_all(aggregated, ('zl', 'y'), 0, 0).reshape(-1, node_cols)  16.1 us
    all_to_all x1, blocking collectives, per_device(): grad = jnp.sum(lax.all_to_all(grad, 'zl', 0, 0), axis=0)  15.2 us
    all_to_all x1, starting transfers between devices, asking(): codes = lax.all_to_all(ask.reshape(peers, -1), ('x', 'c'), 0, 0)  11.3 us
    ppermute x2, waiting for transfers between devices, onward(): return lax.ppermute(value, ('zh', 'c'), pairs)  10.4 us
  transfers between devices with their start and end apart: 5, of which 3 were waited for; matrix products, arithmetic and copies ran while one was open for 2% of the time, Pallas kernels for 1%

profile of v5, /device:TPU:2, one launch (start us, length us, event | category | flops | bytes accessed | tf_op | source)
XLA Modules:
  0.0 203.8 jit_solution(9125311900660788545)
XLA Ops:
  0.6 0.0 copy-start.2
  0.6 15.7 %collective-permute-start.1 = (bf16[24,4096]{1,0:T(8,128)(2,1)}, bf16[24,4096]{1,0:T(8,128)(2,1)S(1)}, u32[]{:S(2)}, u32[]{:S(2)}) collective-permute-start(bf16[24,4096]{1,0:T(8,128)(2,1)} %param.12), channel_id=1, source_target_pairs={{0,64},{32,224},{64,128},{96,32},{128,192},{160,96},{192,0},{224,1... | collective-permute-start | bytes 589832 | tf_op jit(solution)/shard_map/ppermute | solution.py:179
  17.0 19.3 %conditional.2 = (s32[48]{0:T(128)S(1)}, s32[128]{0:T(128)S(1)}, bf16[24,4096]{1,0:T(8,128)(2,1)}) conditional(s32[]{:T(128)} %bitcast.6, () %tuple.24, (s32[48,1]{0,1:T(1,128)}, s32[48]{0:T(128)}, bf16[24,4096]{1,0:T(8,128)(2,1)}) %tuple.25), branch_computations={%region_0.0_spmd, %region_1.4_spmd} | conditional | flops 38035 | bytes 803284 | solution.py:219
  17.0 0.7 add_bitcast_fusion
  17.7 0.7 fusion.6
  18.4 0.7 add_add_fusion
  19.1 0.2 convert_reduce_fusion
  19.3 0.1 select_reduce_fusion
  19.4 0.7 all_to_all.16
  20.1 11.3 %all-to-all-start.1 = ((s32[8,1,16]{2,1,0:T(1,128)}), s32[8,1,16]{2,1,0:T(1,128)S(1)}, u32[]{:S(2)}, u32[]{:S(2)}) async-start(s32[8,1,16]{2,1,0:T(1,128)} %bitcast.4), calls=%async_computation.1 | async-start | bytes 8192 | tf_op jit(solution)/shard_map/cond/branch_1_fun/all_to_all | solution.py:215
  31.3 2.0 %collective-permute-start = (bf16[24,4096]{1,0:T(8,128)(2,1)}, bf16[24,4096]{1,0:T(8,128)(2,1)}, u32[]{:S(2)}, u32[]{:S(2)}) collective-permute-start(bf16[24,4096]{1,0:T(8,128)(2,1)} %get-tuple-element.17), channel_id=1, source_target_pairs={{0,32},{32,0},{1,33},{33,1},{2,34},{34,2},{3,35},{35,3},{4,36},{36... | collective-permute-start | bytes 589832 | tf_op jit(solution)/shard_map/cond/branch_1_fun/ppermute | solution.py:214
  33.4 1.7 all-to-all-done.1
  35.1 0.5 broadcast.389
  35.6 0.7 reduce.3
  36.3 0.1 reshape.120
  36.3 0.0 collective-permute-done
  36.3 0.0 collective-permute-done.1
  36.4 1.0 pad_maximum_fusion
  37.3 12.9 %collective-permute-start.2 = (bf16[2,24,4096]{2,1,0:T(8,128)(2,1)S(1)}, bf16[2,24,4096]{2,1,0:T(8,128)(2,1)S(1)}, u32[]{:S(2)}, u32[]{:S(2)}) collective-permute-start(bf16[2,24,4096]{2,1,0:T(8,128)(2,1)S(1)} %pad_maximum_fusion), channel_id=1, source_target_pairs={{0,64},{32,224},{64,128},{96,32},{128,192},{160,96},{192,0},{224,1... | collective-permute-start | bytes 1179656 | tf_op jit(solution)/shard_map/ppermute | solution.py:179
  50.2 21.9 %conditional.3 = (bf16[64,24,256]{2,1,0:T(8,128)(2,1)S(1)}) conditional(s32[]{:T(128)} %bitcast.6, () %tuple.26, (s32[128]{0:T(128)S(1)}, bf16[24,4096]{1,0:T(8,128)(2,1)}, bf16[24,4096]{1,0:T(8,128)(2,1)S(1)}) %tuple.28), branch_computations={%region_4.5_spmd, %region_5.6_spmd} | conditional | bytes 3670024 | solution.py:226
  50.2 1.3 pack.2
  51.5 20.5 %all_to_all.36 = bf16[8,8,24,256]{3,2,1,0:T(8,128)(2,1)S(1)} all-to-all(bf16[8,8,24,256]{3,2,1,0:T(8,128)(2,1)S(1)} %pack.2), channel_id=1, replica_groups=mesh['x'=4,'zh'=4,'c'=2,'zl'=8,'y'=4] {'x','c'}, dimensions={0} | all-to-all | bytes 1572864 | tf_op jit(solution)/shard_map/cond/branch_1_fun/all_to_all | solution.py:202
  72.1 0.0 copy-start.3
  72.1 0.0 copy-start
  72.1 0.0 copy-start.1
  72.1 10.4 %collective-permute-done.2.refs_1_ = bf16[2,24,4096]{2,1,0:T(8,128)(2,1)S(1)} collective-permute-done((bf16[2,24,4096]{2,1,0:T(8,128)(2,1)S(1)}, bf16[2,24,4096]{2,1,0:T(8,128)(2,1)S(1)}, u32[]{:S(2)}, u32[]{:S(2)}) %collective-permute-start.2) | collective-permute-done | bytes 393248 | tf_op jit(solution)/shard_map/ppermute | solution.py:179
  82.4 1.0 pack.3
  83.5 18.7 %all_to_all.37 = bf16[8,8,24,256]{3,2,1,0:T(8,128)(2,1)S(1)} all-to-all(bf16[8,8,24,256]{3,2,1,0:T(8,128)(2,1)S(1)} %pack.3), channel_id=1, replica_groups=mesh['x'=4,'zh'=4,'c'=2,'zl'=8,'y'=4] {'x','c'}, dimensions={0} | all-to-all | bytes 1572864 | tf_op jit(solution)/shard_map/all_to_all | solution.py:202
  102.1 0.0 copy-done.2
  102.1 5.0 %aggregate.1 = bf16[32,24,128]{2,1,0:T(8,128)(2,1)} custom-call(s32[48]{0:T(128)S(1)} %get-tuple-element.33.pos, s32[16]{0:T(128)S(1)} %copy-done.2, bf16[64,24,256]{2,1,0:T(8,128)(2,1)S(1)} %get-tuple-element.58.early, bf16[64,24,256]{2,1,0:T(8,128)(2,1)S(1)} %bitcast.47, bf16[48,256,256]{2,1,0:T(8,128)(2,1)} %tiles_in.1), custom_call_target="tpu_custom_call" | custom-call | flops 150994944 | bytes 7340032 | tf_op jit(solution)/shard_map/aggregate/pallas_call | solution.py:100
  107.1 9.1 %all-to-all-start.3 = ((bf16[32,24,128]{2,1,0:T(8,128)(2,1)}), bf16[32,24,128]{2,1,0:T(8,128)(2,1)S(1)}, u32[]{:S(2)}, u32[]{:S(2)}) async-start(bf16[32,24,128]{2,1,0:T(8,128)(2,1)} %aggregate.1), calls=%async_computation.3 | async-start | bytes 393216 | tf_op jit(solution)/shard_map/all_to_all | solution.py:234
  116.3 0.0 copy-done.3
  116.3 0.3 copy.19
  116.6 16.1 %all-to-all-done.3 = bf16[32,24,128]{2,1,0:T(8,128)(2,1)S(1)} async-done(((bf16[32,24,128]{2,1,0:T(8,128)(2,1)}), bf16[32,24,128]{2,1,0:T(8,128)(2,1)S(1)}, u32[]{:S(2)}, u32[]{:S(2)}) %all-to-all-start.3) | async-done | bytes 196640 | tf_op jit(solution)/shard_map/all_to_all | solution.py:234
  132.7 0.0 copy-done
  132.7 0.0 copy-done.1
  132.7 1.2 dense.1
  133.9 17.0 %all_to_all.38.parts = bf16[32,4,24,128]{3,2,1,0:T(8,128)(2,1)S(1)} all-to-all(bf16[32,4,24,128]{3,2,1,0:T(8,128)(2,1)S(1)} %get-tuple-element.42), channel_id=1, replica_groups=mesh['x'=4,'zh'=4,'c'=2,'zl'=8,'y'=4] {'x','c','y'}, dimensions={0} | all-to-all | bytes 1572864 | tf_op jit(solution)/shard_map/all_to_all | solution.py:236
  150.9 0.2 fold.1
  151.1 15.2 %all_to_all.39 = f32[8,16,96]{2,1,0:T(8,128)S(1)} all-to-all(f32[8,16,96]{2,1,0:T(8,128)S(1)} %fold.1), channel_id=1, replica_groups=mesh['x'=4,'zh'=4,'c'=2,'zl'=8,'y'=4] {'zl'}, dimensions={0} | all-to-all | bytes 98304 | tf_op jit(solution)/shard_map/all_to_all | solution.py:237
  166.3 0.1 reshape.127
  166.4 0.1 reshape.138
  166.5 35.5 %all_to_all.40 = f32[4,1,384]{2,1,0:T(1,128)S(1)} all-to-all(f32[4,1,384]{2,1,0:T(1,128)S(1)} %reshape.138), channel_id=1, replica_groups=mesh['x'=4,'zh'=4,'c'=2,'zl'=8,'y'=4] {'zh'}, dimensions={0} | all-to-all | bytes 12288 | tf_op jit(solution)/shard_map/all_to_all | solution.py:240
  202.0 0.5 broadcast.404
  202.5 0.7 reduce.4
  203.1 0.1 reshape.139
  203.2 0.6 broadcast_multiply_fusion
  (5 shorter events, 0.0 us)
Async XLA Ops:
  0.6 101.5 %copy-start.2 = (s32[16]{0:T(128)S(1)}, s32[16]{0:T(128)}, u32[]{:S(2)}) copy-start(s32[16]{0:T(128)} %counts.1) | copy-start | bytes 196
  0.6 35.7 %collective-permute-start.1 = (bf16[24,4096]{1,0:T(8,128)(2,1)}, bf16[24,4096]{1,0:T(8,128)(2,1)S(1)}, u32[]{:S(2)}, u32[]{:S(2)}) collective-permute-start(bf16[24,4096]{1,0:T(8,128)(2,1)} %param.12), channel_id=1, source_target_pairs={{0,64},{32,224},{64,128},{96,32},{128,192},{160,96},{192,0},{224,1... | collective-permute-start | bytes 589832 | tf_op jit(solution)/shard_map/ppermute | solution.py:179
  20.1 15.0 %all-to-all-start.1 = ((s32[8,1,16]{2,1,0:T(1,128)}), s32[8,1,16]{2,1,0:T(1,128)S(1)}, u32[]{:S(2)}, u32[]{:S(2)}) async-start(s32[8,1,16]{2,1,0:T(1,128)} %bitcast.4), calls=%async_computation.1 | async-start | bytes 8192 | tf_op jit(solution)/shard_map/cond/branch_1_fun/all_to_all | solution.py:215
  31.3 5.0 %collective-permute-start = (bf16[24,4096]{1,0:T(8,128)(2,1)}, bf16[24,4096]{1,0:T(8,128)(2,1)}, u32[]{:S(2)}, u32[]{:S(2)}) collective-permute-start(bf16[24,4096]{1,0:T(8,128)(2,1)} %get-tuple-element.17), channel_id=1, source_target_pairs={{0,32},{32,0},{1,33},{33,1},{2,34},{34,2},{3,35},{35,3},{4,36},{36... | collective-permute-start | bytes 589832 | tf_op jit(solution)/shard_map/cond/branch_1_fun/ppermute | solution.py:214
  37.3 45.1 %collective-permute-start.2 = (bf16[2,24,4096]{2,1,0:T(8,128)(2,1)S(1)}, bf16[2,24,4096]{2,1,0:T(8,128)(2,1)S(1)}, u32[]{:S(2)}, u32[]{:S(2)}) collective-permute-start(bf16[2,24,4096]{2,1,0:T(8,128)(2,1)S(1)} %pad_maximum_fusion), channel_id=1, source_target_pairs={{0,64},{32,224},{64,128},{96,32},{128,192},{160,96},{192,0},{224,1... | collective-permute-start | bytes 1179656 | tf_op jit(solution)/shard_map/ppermute | solution.py:179
  72.1 44.2 %copy-start.3 = (bf16[768,512]{1,0:T(8,128)(2,1)S(1)}, bf16[768,512]{1,0:T(8,128)(2,1)}, u32[]{:S(2)}) copy-start(bf16[768,512]{1,0:T(8,128)(2,1)} %param.17) | copy-start | bytes 2359300
  72.1 60.6 %copy-start = (bf16[512,128]{1,0:T(8,128)(2,1)S(1)}, bf16[512,128]{1,0:T(8,128)(2,1)}, u32[]{:S(2)}) copy-start(bf16[512,128]{1,0:T(8,128)(2,1)} %self_part.1) | copy-start | bytes 393220
  72.1 60.6 %copy-start.1 = (bf16[512,128]{1,0:T(8,128)(2,1)S(1)}, bf16[512,128]{1,0:T(8,128)(2,1)}, u32[]{:S(2)}) copy-start(bf16[512,128]{1,0:T(8,128)(2,1)} %cotangent.1) | copy-start | bytes 393220
  107.1 25.5 %all-to-all-start.3 = ((bf16[32,24,128]{2,1,0:T(8,128)(2,1)}), bf16[32,24,128]{2,1,0:T(8,128)(2,1)S(1)}, u32[]{:S(2)}, u32[]{:S(2)}) async-start(bf16[32,24,128]{2,1,0:T(8,128)(2,1)} %aggregate.1), calls=%async_computation.3 | async-start | bytes 393216 | tf_op jit(solution)/shard_map/all_to_all | solution.py:234

commit v6 on v5

--- a/solution.py
+++ b/solution.py
@@ -11,7 +11,8 @@
 MAXT = 3
 CAP = 4
 X, ZH, CORE, ZL, Y = 4, 4, 2, 8, 4
-EACH = 2 * CAP
+OWN, NEAR, FAR = CAP, 2 * CAP, CAP
+PEERS = X * CORE
 GROUPS = 4
 VMEM = 16 * 1024 * 1024
 f32, bf16 = jnp.float32, jnp.bfloat16
@@ -27,7 +28,6 @@
 
 def pack_kernel(first, width, codes, *refs):
     held, out = refs[:-1], refs[-1]
-    stacked = len(held) == 1
     peers, each = out.shape[0], out.shape[1]
     asked = codes.shape[0] // peers
 
@@ -35,19 +35,19 @@
         for k in range(each):
             code = codes[d * asked + first + k]
             place = pl.ds(pl.multiple_of(code % 16 * width, width), width)
-            if stacked:
-                out[d, k] = held[0][code // 16, :, place]
-            else:
-                out[d, k] = jnp.where(code < 16, held[0][:, place], held[1][:, place])
+            block = held[0][:, place]
+            if len(held) > 1:
+                block = jnp.where(code < 16, block, held[1][:, place])
+            out[d, k] = block
         return carry
 
     lax.fori_loop(0, peers, one, 0, unroll=2)
 
 
-def pack(codes, held, first, width):
+def pack(codes, held, first, each, width):
     return pl.pallas_call(
         lambda *refs: pack_kernel(first, width, *refs),
-        out_shape=jax.ShapeDtypeStruct((X * CORE, EACH, held[0].shape[-2], width), held[0].dtype),
+        out_shape=jax.ShapeDtypeStruct((PEERS, each, held[0].shape[0], width), held[0].dtype),
         in_specs=[smem()] + [vmem()] * len(held),
         out_specs=vmem(),
         compiler_params=pltpu.CompilerParams(vmem_limit_bytes=VMEM),
@@ -56,16 +56,16 @@
     )(codes, *held)
 
 
-def agg_kernel(pos, counts, early, late, tiles_in, out, tiles, arrived):
-    early_size = early.shape[0]
+def agg_kernel(pos, counts, own, near, far, tiles_in, out, tiles, arrived):
+    second, third = own.shape[0], own.shape[0] + near.shape[0]
     half = out.shape[-1]
     per = tiles.shape[1] // half
     groups = arrived.shape[0]
     size = counts.shape[0] // groups
 
     def fetch(g):
-        own = pl.ds(g * size * MAXT, size * MAXT)
-        return pltpu.make_async_copy(tiles_in.at[own], tiles.at[own], arrived.at[g])
+        part = pl.ds(g * size * MAXT, size * MAXT)
+        return pltpu.make_async_copy(tiles_in.at[part], tiles.at[part], arrived.at[g])
 
     for g in range(groups):
         fetch(g).start()
@@ -78,9 +78,13 @@
             for m in range(MAXT):
                 p = pos[b * MAXT + m]
                 block = jnp.where(
-                    p < early_size,
-                    early[jnp.minimum(p, early_size - 1)],
-                    late[jnp.maximum(p - early_size, 0)],
+                    p < second,
+                    own[jnp.minimum(p, second - 1)],
+                    jnp.where(
+                        p < third,
+                        near[jnp.clip(p - second, 0, near.shape[0] - 1)],
+                        far[jnp.maximum(p - third, 0)],
+                    ),
                 )
                 block = jnp.where(m < count, block, jnp.zeros_like(block))
                 part = lax.dot_general(
@@ -95,18 +99,18 @@
     lax.fori_loop(0, groups, one, 0)
 
 
-def aggregate(pos, counts, early, late, tiles, node_cols):
-    rows, width = early.shape[1:]
+def aggregate(pos, counts, own, near, far, tiles, node_cols):
+    rows, width = own.shape[1:]
     return pl.pallas_call(
         agg_kernel,
         out_shape=jax.ShapeDtypeStruct((counts.shape[0] * width // node_cols, rows, node_cols), bf16),
-        in_specs=[smem(), smem(), vmem(), vmem(), pl.BlockSpec(memory_space=pltpu.HBM)],
+        in_specs=[smem(), smem(), vmem(), vmem(), vmem(), pl.BlockSpec(memory_space=pltpu.HBM)],
         out_specs=vmem(),
         scratch_shapes=[pltpu.VMEM(tiles.shape, tiles.dtype), pltpu.SemaphoreType.DMA((GROUPS,))],
         compiler_params=pltpu.CompilerParams(vmem_limit_bytes=50 * 1024 * 1024),
         cost_estimate=pl.CostEstimate(flops=2 * 48 * 24 * 65536, bytes_accessed=7 << 20, transcendentals=0),
         name="aggregate",
-    )(pos, counts, early, late, tiles)
+    )(pos, counts, own, near, far, tiles)
 
 
 def dense_kernel(rows, w_t, self_part, cotangent, hidden, grad, gp):
@@ -185,17 +189,21 @@
     core = owners % CORE
     apart = (owners // CORE + ZH - me) % ZH
     server = jnp.where(apart == 3, 0, jnp.where(apart == 1, 1, core))
-    second = (apart == 2) | ((apart % 2 == 1) & (server != core))
-    held = (apart == 2) | ((apart % 2 == 1) & (server == core))
     column = (owners // (ZH * CORE)) * CORE + server
-    group = column + jnp.where(second, X * CORE, 0)
+    near, far = apart % 2 == 1, apart == 2
+    group = column + jnp.where(far, 2 * PEERS, jnp.where(near, PEERS, 0))
     s = jnp.arange(slots, dtype=jnp.int32)
     earlier = (group[:, None] == group[None, :]) & (s[None, :] < s[:, None])
     rank = jnp.sum(earlier.astype(jnp.int32), axis=1)
-    place = column * 2 * EACH + jnp.where(second, EACH, 0) + rank
-    hit = place[:, None] == jnp.arange(X * CORE * 2 * EACH, dtype=jnp.int32)[None, :]
-    ask = jnp.sum(jnp.where(hit, (held.astype(jnp.int32) * 16 + local)[:, None], 0), axis=0)
-    return group * EACH + rank, ask
+    pos = rank + jnp.where(
+        far,
+        PEERS * (OWN + NEAR) + column * FAR,
+        jnp.where(near, PEERS * OWN + column * NEAR, column * OWN),
+    )
+    place = column * (OWN + NEAR + FAR) + rank + jnp.where(far, OWN + NEAR, jnp.where(near, OWN, 0))
+    code = local + jnp.where(near & (server != core), 16, 0)
+    hit = place[:, None] == jnp.arange(PEERS * (OWN + NEAR + FAR), dtype=jnp.int32)[None, :]
+    return pos, jnp.sum(jnp.where(hit, code[:, None], 0), axis=0)
 
 
 def exchange(packed):
@@ -206,31 +214,36 @@
     rows, cols = features.shape
     width = tiles.shape[1]
     node_cols = self_part.shape[1]
-    peers = X * CORE
     live = counts[0] > 0
+
+    def beside(work, *like):
+        return lax.cond(live, work, lambda: tuple(jnp.zeros(shape, kind) for shape, kind in like))
 
     def asking():
         pos, ask = plan(src_owner[:, 0], src_local)
         other = lax.ppermute(features, "c", [(0, 1), (1, 0)])
-        codes = lax.all_to_all(ask.reshape(peers, -1), ("x", "c"), 0, 0)
+        codes = lax.all_to_all(ask.reshape(PEERS, -1), ("x", "c"), 0, 0)
         return pos, codes.reshape(-1), other
 
     first = onward(features)
-    pos, codes, other = lax.cond(
-        live,
+    pos, codes, other = beside(
         asking,
-        lambda: (jnp.zeros_like(src_local), jnp.zeros((2 * peers * EACH,), jnp.int32), jnp.zeros_like(features)),
-    )
-    codes, first, other = lax.optimization_barrier((codes, first, other))
-    late = onward(jnp.concatenate([other[None], first[None]]))
-    early = lax.cond(
-        live,
-        lambda: exchange(pack(codes, (features, first), 0, width)),
-        lambda: jnp.zeros((peers * EACH, rows, width), bf16),
-    )
-    early, late = lax.optimization_barrier((early, late))
-    late = exchange(pack(codes, (late,), EACH, width))
-    aggregated = aggregate(pos, counts, early, late, tiles, node_cols)
+        (src_local.shape, jnp.int32),
+        ((PEERS * (OWN + NEAR + FAR),), jnp.int32),
+        (features.shape, bf16),
+    )
+    second = onward(other)
+    (own,) = beside(
+        lambda: (exchange(pack(codes, (features,), 0, OWN, width)),), ((PEERS * OWN, rows, width), bf16)
+    )
+    own, first = lax.optimization_barrier((own, first))
+    third = onward(first)
+    (near,) = beside(
+        lambda: (exchange(pack(codes, (first, second), OWN, NEAR, width)),), ((PEERS * NEAR, rows, width), bf16)
+    )
+    near, third = lax.optimization_barrier((near, third))
+    far = exchange(pack(codes, (third,), OWN + NEAR, FAR, width))
+    aggregated = aggregate(pos, counts, own, near, far, tiles, node_cols)
     node_rows = lax.all_to_all(aggregated, ("zl", "y"), 0, 0).reshape(-1, node_cols)
     hidden, grad = dense(node_rows, w_neigh.T, self_part, cotangent)
     grad = fold(lax.all_to_all(grad, ("x", "c", "y"), 0, 0))

time: 204 us -> 198 us (0.971)
  waiting for transfers between devices: 28.1 us -> 23.7 us
    ppermute x2 -> x3, waiting for transfers between devices: 10.4 us -> 5.74 us  [onward(): return lax.ppermute(value, ('zh', 'c'), pairs)]
    ppermute x2 -> x3, starting transfers between devices: 28.6 us -> 31.1 us  [onward(): return lax.ppermute(value, ('zh', 'c'), pairs)]
    all_to_all x1, blocking collectives: 35.5 us -> 33.4 us  [per_device(): lax.all_to_all(grad, 'zh', 0, 0)]
    all_to_all x2 -> x3, blocking collectives: 39.2 us -> 39.3 us  [exchange(): lax.all_to_all(packed, ('x', 'c'), 0, 0).reshape((-1,) + packed.shape[2:])]
  transfers between devices with their start and end apart: 5 -> 6, of which waited for: 3 -> 3; matrix products, arithmetic and copies ran while one was open for 2% -> 2% of each run, Pallas kernels for 1% -> 1%
where the time goes in v6:
time: 198 us
  blocking collectives  105 us (53%)
  starting transfers between devices  51.6 us (26%)
  waiting for transfers between devices  23.7 us (12%)
  Pallas kernels  9.52 us (5%)
  other arithmetic  4.32 us (2%)
  local copies, waits for them, and re-layouts  2.34 us (1%)
    all_to_all x3, blocking collectives, exchange(): lax.all_to_all(packed, ('x', 'c'), 0, 0).reshape((-1,) + packed.shape[2:])  39.3 us
    all_to_all x1, blocking collectives, per_device(): lax.all_to_all(grad, 'zh', 0, 0)  33.4 us
    ppermute x3, starting transfers between devices, onward(): return lax.ppermute(value, ('zh', 'c'), pairs)  31.1 us
    all_to_all x1, blocking collectives, per_device(): grad = fold(lax.all_to_all(grad, ('x', 'c', 'y'), 0, 0))  17 us
    all_to_all x1, waiting for transfers between devices, per_device(): lax.all_to_all(aggregated, ('zl', 'y'), 0, 0).reshape(-1, node_cols)  16.3 us
    all_to_all x1, blocking collectives, per_device(): grad = jnp.sum(lax.all_to_all(grad, 'zl', 0, 0), axis=0)  15.2 us
    all_to_all x1, starting transfers between devices, asking(): codes = lax.all_to_all(ask.reshape(PEERS, -1), ('x', 'c'), 0, 0)  11.3 us
    all_to_all x1, starting transfers between devices, per_device(): lax.all_to_all(aggregated, ('zl', 'y'), 0, 0).reshape(-1, node_cols)  7.21 us
  transfers between devices with their start and end apart: 6, of which 3 were waited for; matrix products, arithmetic and copies ran while one was open for 2% of the time, Pallas kernels for 1%

profile of v6, /device:TPU:2, one launch (start us, length us, event | category | flops | bytes accessed | tf_op | source)
XLA Modules:
  0.0 197.8 jit_solution(12698664788047288045)
XLA Ops:
  0.6 0.0 copy-start.2
  0.6 15.7 %collective-permute-start.1 = (bf16[24,4096]{1,0:T(8,128)(2,1)}, bf16[24,4096]{1,0:T(8,128)(2,1)}, u32[]{:S(2)}, u32[]{:S(2)}) collective-permute-start(bf16[24,4096]{1,0:T(8,128)(2,1)} %param.14), channel_id=1, source_target_pairs={{0,64},{32,224},{64,128},{96,32},{128,192},{160,96},{192,0},{224,1... | collective-permute-start | bytes 589832 | tf_op jit(solution)/shard_map/ppermute | solution.py:183
  17.0 19.3 %conditional.3 = (s32[48]{0:T(128)S(1)}, s32[128]{0:T(128)S(1)}, bf16[24,4096]{1,0:T(8,128)(2,1)}) conditional(s32[]{:T(128)} %bitcast.7, () %tuple.30, (s32[48,1]{0,1:T(1,128)}, s32[48]{0:T(128)}, bf16[24,4096]{1,0:T(8,128)(2,1)}) %tuple.31), branch_computations={%region_0.0_spmd, %region_1.4_spmd} | conditional | flops 38179 | bytes 803812 | solution.py:220
  17.0 0.7 fusion.12
  17.7 0.7 fusion.7
  18.4 0.7 fusion.3
  19.1 0.2 convert_reduce_fusion
  19.3 0.1 select_reduce_fusion
  19.4 0.7 all_to_all.18
  20.1 11.3 %all-to-all-start.2 = ((s32[8,1,16]{2,1,0:T(1,128)}), s32[8,1,16]{2,1,0:T(1,128)S(1)}, u32[]{:S(2)}, u32[]{:S(2)}) async-start(s32[8,1,16]{2,1,0:T(1,128)} %bitcast.4), calls=%async_computation.2 | async-start | bytes 8192 | tf_op jit(solution)/shard_map/cond/branch_1_fun/all_to_all | solution.py:225
  31.4 2.0 %collective-permute-start = (bf16[24,4096]{1,0:T(8,128)(2,1)}, bf16[24,4096]{1,0:T(8,128)(2,1)}, u32[]{:S(2)}, u32[]{:S(2)}) collective-permute-start(bf16[24,4096]{1,0:T(8,128)(2,1)} %get-tuple-element.24), channel_id=1, source_target_pairs={{0,32},{32,0},{1,33},{33,1},{2,34},{34,2},{3,35},{35,3},{4,36},{36... | collective-permute-start | bytes 589832 | tf_op jit(solution)/shard_map/cond/branch_1_fun/ppermute | solution.py:224
  33.4 1.7 all-to-all-done.2
  35.1 0.5 broadcast.394
  35.6 0.7 reduce.3
  36.3 0.1 reshape.120
  36.3 0.0 collective-permute-done
  36.3 9.3 %collective-permute-start.2 = (bf16[24,4096]{1,0:T(8,128)(2,1)}, bf16[24,4096]{1,0:T(8,128)(2,1)S(1)}, u32[]{:S(2)}, u32[]{:S(2)}) collective-permute-start(bf16[24,4096]{1,0:T(8,128)(2,1)} %get-tuple-element.45), channel_id=1, source_target_pairs={{0,64},{32,224},{64,128},{96,32},{128,192},{160,96},{192,0},{224,1... | collective-permute-start | bytes 589832 | tf_op jit(solution)/shard_map/ppermute | solution.py:183
  45.6 12.5 %conditional.4 = (bf16[32,24,256]{2,1,0:T(8,128)(2,1)S(1)}) conditional(s32[]{:T(128)} %bitcast.7, () %tuple.32, (s32[128]{0:T(128)S(1)}, bf16[24,4096]{1,0:T(8,128)(2,1)}) %tuple.33), branch_computations={%region_4.5_spmd, %region_5.6_spmd} | conditional | bytes 2883592 | solution.py:220
  45.7 1.1 pack.3
  46.8 11.3 %all_to_all.40 = bf16[8,4,24,256]{3,2,1,0:T(8,128)(2,1)S(1)} all-to-all(bf16[8,4,24,256]{3,2,1,0:T(8,128)(2,1)S(1)} %pack.3), channel_id=1, replica_groups=mesh['x'=4,'zh'=4,'c'=2,'zl'=8,'y'=4] {'x','c'}, dimensions={0} | all-to-all | bytes 786432 | tf_op jit(solution)/shard_map/cond/branch_1_fun/all_to_all | solution.py:210
  58.1 0.0 collective-permute-done.1
  58.1 6.1 %collective-permute-start.3 = (bf16[24,4096]{1,0:T(8,128)(2,1)}, bf16[24,4096]{1,0:T(8,128)(2,1)S(1)}, u32[]{:S(2)}, u32[]{:S(2)}) collective-permute-start(bf16[24,4096]{1,0:T(8,128)(2,1)} %collective-permute-done.1), channel_id=1, source_target_pairs={{0,64},{32,224},{64,128},{96,32},{128,192},{160,96},{192,0},{224,1... | collective-permute-start | bytes 589832 | tf_op jit(solution)/shard_map/ppermute | solution.py:183
  64.2 0.0 collective-permute-done.2
  64.2 0.0 copy-start.3
  64.2 18.3 %conditional.5 = (bf16[64,24,256]{2,1,0:T(8,128)(2,1)S(1)}) conditional(s32[]{:T(128)} %bitcast.7, () %tuple.35, (s32[128]{0:T(128)S(1)}, bf16[24,4096]{1,0:T(8,128)(2,1)}, bf16[24,4096]{1,0:T(8,128)(2,1)S(1)}) %tuple.36), branch_computations={%region_6.7_spmd, %region_7.8_spmd} | conditional | bytes 3670024 | solution.py:220
  64.2 1.4 pack.4
  65.6 16.9 %all_to_all.41 = bf16[8,8,24,256]{3,2,1,0:T(8,128)(2,1)S(1)} all-to-all(bf16[8,8,24,256]{3,2,1,0:T(8,128)(2,1)S(1)} %pack.4), channel_id=1, replica_groups=mesh['x'=4,'zh'=4,'c'=2,'zl'=8,'y'=4] {'x','c'}, dimensions={0} | all-to-all | bytes 1572864 | tf_op jit(solution)/shard_map/cond/branch_1_fun/all_to_all | solution.py:210
  82.5 0.0 copy-start
  82.5 0.0 copy-start.1
  82.5 5.7 %collective-permute-done.3.refs_1_ = bf16[24,4096]{1,0:T(8,128)(2,1)S(1)} collective-permute-done((bf16[24,4096]{1,0:T(8,128)(2,1)}, bf16[24,4096]{1,0:T(8,128)(2,1)S(1)}, u32[]{:S(2)}, u32[]{:S(2)}) %collective-permute-start.3) | collective-permute-done | bytes 196640 | tf_op jit(solution)/shard_map/ppermute | solution.py:183
  88.2 0.7 pack.5
  88.9 11.1 %all_to_all.42 = bf16[8,4,24,256]{3,2,1,0:T(8,128)(2,1)S(1)} all-to-all(bf16[8,4,24,256]{3,2,1,0:T(8,128)(2,1)S(1)} %pack.5), channel_id=1, replica_groups=mesh['x'=4,'zh'=4,'c'=2,'zl'=8,'y'=4] {'x','c'}, dimensions={0} | all-to-all | bytes 786432 | tf_op jit(solution)/shard_map/all_to_all | solution.py:210
  100.0 0.0 copy-done.2
  100.0 5.0 %aggregate.1 = bf16[32,24,128]{2,1,0:T(8,128)(2,1)} custom-call(s32[48]{0:T(128)S(1)} %get-tuple-element.41.pos, s32[16]{0:T(128)S(1)} %copy-done.2, bf16[32,24,256]{2,1,0:T(8,128)(2,1)S(1)} %get-tuple-element.68.own, bf16[64,24,256]{2,1,0:T(8,128)(2,1)S(1)} %get-tuple-element.69.near, bf16[32,24,256]{2,1,0:T(8,128)(2,1)S(1)} %bitcast.50, ...), custom_call_target="tpu_custom_call" | custom-call | flops 150994944 | bytes 7340032 | tf_op jit(solution)/shard_map/aggregate/pallas_call | solution.py:104
  105.0 7.2 %all-to-all-start.4 = ((bf16[32,24,128]{2,1,0:T(8,128)(2,1)}), bf16[32,24,128]{2,1,0:T(8,128)(2,1)S(1)}, u32[]{:S(2)}, u32[]{:S(2)}) async-start(bf16[32,24,128]{2,1,0:T(8,128)(2,1)} %aggregate.1), calls=%async_computation.4 | async-start | bytes 393216 | tf_op jit(solution)/shard_map/all_to_all | solution.py:247
  112.2 0.0 copy-done.3
  112.2 0.3 copy.19
  112.5 16.3 %all-to-all-done.4 = bf16[32,24,128]{2,1,0:T(8,128)(2,1)S(1)} async-done(((bf16[32,24,128]{2,1,0:T(8,128)(2,1)}), bf16[32,24,128]{2,1,0:T(8,128)(2,1)S(1)}, u32[]{:S(2)}, u32[]{:S(2)}) %all-to-all-start.4) | async-done | bytes 196640 | tf_op jit(solution)/shard_map/all_to_all | solution.py:247
  128.7 0.0 copy-done
  128.7 0.0 copy-done.1
  128.7 1.2 dense.1
  130.0 17.0 %all_to_all.43.parts = bf16[32,4,24,128]{3,2,1,0:T(8,128)(2,1)S(1)} all-to-all(bf16[32,4,24,128]{3,2,1,0:T(8,128)(2,1)S(1)} %get-tuple-element.49), channel_id=1, replica_groups=mesh['x'=4,'zh'=4,'c'=2,'zl'=8,'y'=4] {'x','c','y'}, dimensions={0} | all-to-all | bytes 1572864 | tf_op jit(solution)/shard_map/all_to_all | solution.py:249
  147.0 0.2 fold.1
  147.2 15.2 %all_to_all.44 = f32[8,16,96]{2,1,0:T(8,128)S(1)} all-to-all(f32[8,16,96]{2,1,0:T(8,128)S(1)} %fold.1), channel_id=1, replica_groups=mesh['x'=4,'zh'=4,'c'=2,'zl'=8,'y'=4] {'zl'}, dimensions={0} | all-to-all | bytes 98304 | tf_op jit(solution)/shard_map/all_to_all | solution.py:250
  162.4 0.1 reshape.128
  162.5 0.1 reshape.139
  162.6 33.4 %all_to_all.45 = f32[4,1,384]{2,1,0:T(1,128)S(1)} all-to-all(f32[4,1,384]{2,1,0:T(1,128)S(1)} %reshape.139), channel_id=1, replica_groups=mesh['x'=4,'zh'=4,'c'=2,'zl'=8,'y'=4] {'zh'}, dimensions={0} | all-to-all | bytes 12288 | tf_op jit(solution)/shard_map/all_to_all | solution.py:253
  195.9 0.5 broadcast.409
  196.4 0.7 reduce.4
  197.1 0.1 reshape.140
  197.2 0.6 broadcast_multiply_fusion
  (5 shorter events, 0.1 us)
Async XLA Ops:
  0.6 99.4 %copy-start.2 = (s32[16]{0:T(128)S(1)}, s32[16]{0:T(128)}, u32[]{:S(2)}) copy-start(s32[16]{0:T(128)} %counts.1) | copy-start | bytes 196
  0.6 57.5 %collective-permute-start.1 = (bf16[24,4096]{1,0:T(8,128)(2,1)}, bf16[24,4096]{1,0:T(8,128)(2,1)}, u32[]{:S(2)}, u32[]{:S(2)}) collective-permute-start(bf16[24,4096]{1,0:T(8,128)(2,1)} %param.14), channel_id=1, source_target_pairs={{0,64},{32,224},{64,128},{96,32},{128,192},{160,96},{192,0},{224,1... | collective-permute-start | bytes 589832 | tf_op jit(solution)/shard_map/ppermute | solution.py:183
  20.1 15.0 %all-to-all-start.2 = ((s32[8,1,16]{2,1,0:T(1,128)}), s32[8,1,16]{2,1,0:T(1,128)S(1)}, u32[]{:S(2)}, u32[]{:S(2)}) async-start(s32[8,1,16]{2,1,0:T(1,128)} %bitcast.4), calls=%async_computation.2 | async-start | bytes 8192 | tf_op jit(solution)/shard_map/cond/branch_1_fun/all_to_all | solution.py:225
  31.4 5.0 %collective-permute-start = (bf16[24,4096]{1,0:T(8,128)(2,1)}, bf16[24,4096]{1,0:T(8,128)(2,1)}, u32[]{:S(2)}, u32[]{:S(2)}) collective-permute-start(bf16[24,4096]{1,0:T(8,128)(2,1)} %get-tuple-element.24), channel_id=1, source_target_pairs={{0,32},{32,0},{1,33},{33,1},{2,34},{34,2},{3,35},{35,3},{4,36},{36... | collective-permute-start | bytes 589832 | tf_op jit(solution)/shard_map/cond/branch_1_fun/ppermute | solution.py:224
  36.3 27.9 %collective-permute-start.2 = (bf16[24,4096]{1,0:T(8,128)(2,1)}, bf16[24,4096]{1,0:T(8,128)(2,1)S(1)}, u32[]{:S(2)}, u32[]{:S(2)}) collective-permute-start(bf16[24,4096]{1,0:T(8,128)(2,1)} %get-tuple-element.45), channel_id=1, source_target_pairs={{0,64},{32,224},{64,128},{96,32},{128,192},{160,96},{192,0},{224,1... | collective-permute-start | bytes 589832 | tf_op jit(solution)/shard_map/ppermute | solution.py:183
  58.1 30.1 %collective-permute-start.3 = (bf16[24,4096]{1,0:T(8,128)(2,1)}, bf16[24,4096]{1,0:T(8,128)(2,1)S(1)}, u32[]{:S(2)}, u32[]{:S(2)}) collective-permute-start(bf16[24,4096]{1,0:T(8,128)(2,1)} %collective-permute-done.1), channel_id=1, source_target_pairs={{0,64},{32,224},{64,128},{96,32},{128,192},{160,96},{192,0},{224,1... | collective-permute-start | bytes 589832 | tf_op jit(solution)/shard_map/ppermute | solution.py:183
  64.2 48.0 %copy-start.3 = (bf16[768,512]{1,0:T(8,128)(2,1)S(1)}, bf16[768,512]{1,0:T(8,128)(2,1)}, u32[]{:S(2)}) copy-start(bf16[768,512]{1,0:T(8,128)(2,1)} %param.19) | copy-start | bytes 2359300
  82.5 46.3 %copy-start = (bf16[512,128]{1,0:T(8,128)(2,1)S(1)}, bf16[512,128]{1,0:T(8,128)(2,1)}, u32[]{:S(2)}) copy-start(bf16[512,128]{1,0:T(8,128)(2,1)} %self_part.1) | copy-start | bytes 393220
  82.5 46.3 %copy-start.1 = (bf16[512,128]{1,0:T(8,128)(2,1)S(1)}, bf16[512,128]{1,0:T(8,128)(2,1)}, u32[]{:S(2)}) copy-start(bf16[512,128]{1,0:T(8,128)(2,1)} %cotangent.1) | copy-start | bytes 393220
  105.0 23.8 %all-to-all-start.4 = ((bf16[32,24,128]{2,1,0:T(8,128)(2,1)}), bf16[32,24,128]{2,1,0:T(8,128)(2,1)S(1)}, u32[]{:S(2)}, u32[]{:S(2)}) async-start(bf16[32,24,128]{2,1,0:T(8,128)(2,1)} %aggregate.1), calls=%async_computation.4 | async-start | bytes 393216 | tf_op jit(solution)/shard_map/all_to_all | solution.py:247

commit v7 on v6

--- a/solution.py
+++ b/solution.py
@@ -11,7 +11,7 @@
 MAXT = 3
 CAP = 4
 X, ZH, CORE, ZL, Y = 4, 4, 2, 8, 4
-OWN, NEAR, FAR = CAP, 2 * CAP, CAP
+NEAR, FAR = 3 * CAP, CAP
 PEERS = X * CORE
 GROUPS = 4
 VMEM = 16 * 1024 * 1024
@@ -36,8 +36,8 @@
             code = codes[d * asked + first + k]
             place = pl.ds(pl.multiple_of(code % 16 * width, width), width)
             block = held[0][:, place]
-            if len(held) > 1:
-                block = jnp.where(code < 16, block, held[1][:, place])
+            for j in range(1, len(held)):
+                block = jnp.where(code < 16 * j, block, held[j][:, place])
             out[d, k] = block
         return carry
 
@@ -56,8 +56,8 @@
     )(codes, *held)
 
 
-def agg_kernel(pos, counts, own, near, far, tiles_in, out, tiles, arrived):
-    second, third = own.shape[0], own.shape[0] + near.shape[0]
+def agg_kernel(pos, counts, near, far, tiles_in, out, tiles, arrived):
+    size_near = near.shape[0]
     half = out.shape[-1]
     per = tiles.shape[1] // half
     groups = arrived.shape[0]
@@ -78,13 +78,9 @@
             for m in range(MAXT):
                 p = pos[b * MAXT + m]
                 block = jnp.where(
-                    p < second,
-                    own[jnp.minimum(p, second - 1)],
-                    jnp.where(
-                        p < third,
-                        near[jnp.clip(p - second, 0, near.shape[0] - 1)],
-                        far[jnp.maximum(p - third, 0)],
-                    ),
+                    p < size_near,
+                    near[jnp.minimum(p, size_near - 1)],
+                    far[jnp.maximum(p - size_near, 0)],
                 )
                 block = jnp.where(m < count, block, jnp.zeros_like(block))
                 part = lax.dot_general(
@@ -99,18 +95,18 @@
     lax.fori_loop(0, groups, one, 0)
 
 
-def aggregate(pos, counts, own, near, far, tiles, node_cols):
-    rows, width = own.shape[1:]
+def aggregate(pos, counts, near, far, tiles, node_cols):
+    rows, width = near.shape[1:]
     return pl.pallas_call(
         agg_kernel,
         out_shape=jax.ShapeDtypeStruct((counts.shape[0] * width // node_cols, rows, node_cols), bf16),
-        in_specs=[smem(), smem(), vmem(), vmem(), vmem(), pl.BlockSpec(memory_space=pltpu.HBM)],
+        in_specs=[smem(), smem(), vmem(), vmem(), pl.BlockSpec(memory_space=pltpu.HBM)],
         out_specs=vmem(),
         scratch_shapes=[pltpu.VMEM(tiles.shape, tiles.dtype), pltpu.SemaphoreType.DMA((GROUPS,))],
         compiler_params=pltpu.CompilerParams(vmem_limit_bytes=50 * 1024 * 1024),
         cost_estimate=pl.CostEstimate(flops=2 * 48 * 24 * 65536, bytes_accessed=7 << 20, transcendentals=0),
         name="aggregate",
-    )(pos, counts, own, near, far, tiles)
+    )(pos, counts, near, far, tiles)
 
 
 def dense_kernel(rows, w_t, self_part, cotangent, hidden, grad, gp):
@@ -190,19 +186,15 @@
     apart = (owners // CORE + ZH - me) % ZH
     server = jnp.where(apart == 3, 0, jnp.where(apart == 1, 1, core))
     column = (owners // (ZH * CORE)) * CORE + server
-    near, far = apart % 2 == 1, apart == 2
-    group = column + jnp.where(far, 2 * PEERS, jnp.where(near, PEERS, 0))
+    far = apart == 2
+    group = column + jnp.where(far, PEERS, 0)
     s = jnp.arange(slots, dtype=jnp.int32)
     earlier = (group[:, None] == group[None, :]) & (s[None, :] < s[:, None])
     rank = jnp.sum(earlier.astype(jnp.int32), axis=1)
-    pos = rank + jnp.where(
-        far,
-        PEERS * (OWN + NEAR) + column * FAR,
-        jnp.where(near, PEERS * OWN + column * NEAR, column * OWN),
-    )
-    place = column * (OWN + NEAR + FAR) + rank + jnp.where(far, OWN + NEAR, jnp.where(near, OWN, 0))
-    code = local + jnp.where(near & (server != core), 16, 0)
-    hit = place[:, None] == jnp.arange(PEERS * (OWN + NEAR + FAR), dtype=jnp.int32)[None, :]
+    pos = rank + jnp.where(far, PEERS * NEAR + column * FAR, column * NEAR)
+    place = column * (NEAR + FAR) + rank + jnp.where(far, NEAR, 0)
+    code = local + jnp.where(apart % 2 == 1, jnp.where(server == core, 16, 32), 0)
+    hit = place[:, None] == jnp.arange(PEERS * (NEAR + FAR), dtype=jnp.int32)[None, :]
     return pos, jnp.sum(jnp.where(hit, code[:, None], 0), axis=0)
 
 
@@ -229,21 +221,18 @@
     pos, codes, other = beside(
         asking,
         (src_local.shape, jnp.int32),
-        ((PEERS * (OWN + NEAR + FAR),), jnp.int32),
+        ((PEERS * (NEAR + FAR),), jnp.int32),
         (features.shape, bf16),
     )
     second = onward(other)
-    (own,) = beside(
-        lambda: (exchange(pack(codes, (features,), 0, OWN, width)),), ((PEERS * OWN, rows, width), bf16)
-    )
-    own, first = lax.optimization_barrier((own, first))
     third = onward(first)
     (near,) = beside(
-        lambda: (exchange(pack(codes, (first, second), OWN, NEAR, width)),), ((PEERS * NEAR, rows, width), bf16)
+        lambda: (exchange(pack(codes, (features, first, second), 0, NEAR, width)),),
+        ((PEERS * NEAR, rows, width), bf16),
     )
     near, third = lax.optimization_barrier((near, third))
-    far = exchange(pack(codes, (third,), OWN + NEAR, FAR, width))
-    aggregated = aggregate(pos, counts, own, near, far, tiles, node_cols)
+    far = exchange(pack(codes, (third,), NEAR, FAR, width))
+    aggregated = aggregate(pos, counts, near, far, tiles, node_cols)
     node_rows = lax.all_to_all(aggregated, ("zl", "y"), 0, 0).reshape(-1, node_cols)
     hidden, grad = dense(node_rows, w_neigh.T, self_part, cotangent)
     grad = fold(lax.all_to_all(grad, ("x", "c", "y"), 0, 0))

time: 198 us -> 215 us (1.086)
  starting transfers between devices: 51.6 us -> 62.1 us
  blocking collectives: 105 us -> 110 us
    all_to_all x1, starting transfers between devices: 7.21 us -> 17.6 us  [per_device(): lax.all_to_all(aggregated, ('zl', 'y'), 0, 0).reshape(-1, node_cols)]
    all_to_all x3 -> x2, blocking collectives: 39.3 us -> 42.8 us  [exchange(): lax.all_to_all(packed, ('x', 'c'), 0, 0).reshape((-1,) + packed.shape[2:])]
where the time goes in v7:
time: 215 us; the launch traced here: 214 us
  blocking collectives  110 us (51%)
  starting transfers between devices  62.1 us (29%)
  waiting for transfers between devices  24.7 us (11%)
  Pallas kernels  8.72 us (4%)
  other arithmetic  4.3 us (2%)
  local copies, waits for them, and re-layouts  2.34 us (1%)
    all_to_all x2, blocking collectives, exchange(): lax.all_to_all(packed, ('x', 'c'), 0, 0).reshape((-1,) + packed.shape[2:])  42.8 us
    all_to_all x1, blocking collectives, per_device(): lax.all_to_all(grad, 'zh', 0, 0)  35.4 us
    ppermute x3, starting transfers between devices, onward(): return lax.ppermute(value, ('zh', 'c'), pairs)  31.1 us
    all_to_all x1, starting transfers between devices, per_device(): lax.all_to_all(aggregated, ('zl', 'y'), 0, 0).reshape(-1, node_cols)  17.6 us
    all_to_all x1, blocking collectives, per_device(): grad = fold(lax.all_to_all(grad, ('x', 'c', 'y'), 0, 0))  17 us
    all_to_all x1, waiting for transfers between devices, per_device(): lax.all_to_all(aggregated, ('zl', 'y'), 0, 0).reshape(-1, node_cols)  16.3 us
    all_to_all x1, blocking collectives, per_device(): grad = jnp.sum(lax.all_to_all(grad, 'zl', 0, 0), axis=0)  15.2 us
    all_to_all x1, starting transfers between devices, asking(): codes = lax.all_to_all(ask.reshape(PEERS, -1), ('x', 'c'), 0, 0)  11.3 us
  transfers between devices with their start and end apart: 6, of which 3 were waited for; matrix products, arithmetic and copies ran while one was open for 2% of the time, Pallas kernels for 1%

profile of v7, /device:TPU:2, one launch (start us, length us, event | category | flops | bytes accessed | tf_op | source)
XLA Modules:
  0.0 213.9 jit_solution(10599717354783677609)
XLA Ops:
  0.6 15.7 %collective-permute-start.1 = (bf16[24,4096]{1,0:T(8,128)(2,1)}, bf16[24,4096]{1,0:T(8,128)(2,1)}, u32[]{:S(2)}, u32[]{:S(2)}) collective-permute-start(bf16[24,4096]{1,0:T(8,128)(2,1)} %param.12), channel_id=1, source_target_pairs={{0,64},{32,224},{64,128},{96,32},{128,192},{160,96},{192,0},{224,1... | collective-permute-start | bytes 589832 | tf_op jit(solution)/shard_map/ppermute | solution.py:179
  17.0 19.3 %conditional.2 = (s32[48]{0:T(128)S(1)}, s32[128]{0:T(128)S(1)}, bf16[24,4096]{1,0:T(8,128)(2,1)}) conditional(s32[]{:T(128)} %bitcast.6, () %tuple.23, (s32[48,1]{0,1:T(1,128)}, s32[48]{0:T(128)}, bf16[24,4096]{1,0:T(8,128)(2,1)}) %tuple.24), branch_computations={%region_0.0_spmd, %region_1.4_spmd} | conditional | flops 36787 | bytes 803668 | solution.py:212
  17.0 0.7 fusion.10
  17.7 0.7 fusion.6
  18.4 0.7 fusion.3
  19.1 0.2 convert_reduce_fusion
  19.3 0.1 select_reduce_fusion
  19.4 0.7 all_to_all.16
  20.1 11.3 %all-to-all-start.1 = ((s32[8,1,16]{2,1,0:T(1,128)}), s32[8,1,16]{2,1,0:T(1,128)S(1)}, u32[]{:S(2)}, u32[]{:S(2)}) async-start(s32[8,1,16]{2,1,0:T(1,128)} %bitcast.4), calls=%async_computation.1 | async-start | bytes 8192 | tf_op jit(solution)/shard_map/cond/branch_1_fun/all_to_all | solution.py:217
  31.3 2.0 collective-permute-start
  33.4 1.7 all-to-all-done.1
  35.1 0.5 broadcast.344
  35.6 0.7 reduce.3
  36.2 0.1 reshape.105
  36.3 0.0 collective-permute-done
  36.3 9.3 %collective-permute-start.2 = (bf16[24,4096]{1,0:T(8,128)(2,1)}, bf16[24,4096]{1,0:T(8,128)(2,1)S(1)}, u32[]{:S(2)}, u32[]{:S(2)}) collective-permute-start(bf16[24,4096]{1,0:T(8,128)(2,1)} %get-tuple-element.35), channel_id=1, source_target_pairs={{0,64},{32,224},{64,128},{96,32},{128,192},{160,96},{192,0},{224,1... | collective-permute-start | bytes 589832 | tf_op jit(solution)/shard_map/ppermute | solution.py:179
  45.6 0.0 collective-permute-done.1
  45.6 6.1 %collective-permute-start.3 = (bf16[24,4096]{1,0:T(8,128)(2,1)}, bf16[24,4096]{1,0:T(8,128)(2,1)S(1)}, u32[]{:S(2)}, u32[]{:S(2)}) collective-permute-start(bf16[24,4096]{1,0:T(8,128)(2,1)} %collective-permute-done.1), channel_id=1, source_target_pairs={{0,64},{32,224},{64,128},{96,32},{128,192},{160,96},{192,0},{224,1... | collective-permute-start | bytes 589832 | tf_op jit(solution)/shard_map/ppermute | solution.py:179
  51.7 6.7 %collective-permute-done.2 = bf16[24,4096]{1,0:T(8,128)(2,1)S(1)} collective-permute-done((bf16[24,4096]{1,0:T(8,128)(2,1)}, bf16[24,4096]{1,0:T(8,128)(2,1)S(1)}, u32[]{:S(2)}, u32[]{:S(2)}) %collective-permute-start.2) | collective-permute-done | bytes 196640 | tf_op jit(solution)/shard_map/ppermute | solution.py:179
  58.4 33.1 %conditional.3 = (bf16[96,24,256]{2,1,0:T(8,128)(2,1)S(1)}) conditional(s32[]{:T(128)} %bitcast.6, () %tuple.25, (s32[128]{0:T(128)S(1)}, bf16[24,4096]{1,0:T(8,128)(2,1)}, bf16[24,4096]{1,0:T(8,128)(2,1)}, bf16[24,4096]{1,0:T(8,128)(2,1)S(1)}) %tuple.26), branch_computations={%region_4.5_spmd, %region_5.6_spmd} | conditional | bytes 4456456 | solution.py:212
  58.4 1.6 pack.2
  60.1 31.5 %all_to_all.36 = bf16[8,12,24,256]{3,2,1,0:T(8,128)(2,1)S(1)} all-to-all(bf16[8,12,24,256]{3,2,1,0:T(8,128)(2,1)S(1)} %pack.2), channel_id=1, replica_groups=mesh['x'=4,'zh'=4,'c'=2,'zl'=8,'y'=4] {'x','c'}, dimensions={0} | all-to-all | bytes 2359296 | tf_op jit(solution)/shard_map/cond/branch_1_fun/all_to_all | solution.py:202
  91.6 0.0 copy-start.2
  91.6 0.0 collective-permute-done.3.refs_1_
  91.6 0.7 pack.3
  92.3 11.3 %all_to_all.37 = bf16[8,4,24,256]{3,2,1,0:T(8,128)(2,1)S(1)} all-to-all(bf16[8,4,24,256]{3,2,1,0:T(8,128)(2,1)S(1)} %pack.3), channel_id=1, replica_groups=mesh['x'=4,'zh'=4,'c'=2,'zl'=8,'y'=4] {'x','c'}, dimensions={0} | all-to-all | bytes 786432 | tf_op jit(solution)/shard_map/all_to_all | solution.py:202
  103.6 0.0 copy-done.2
  103.6 0.0 copy-start.3
  103.6 5.0 %aggregate.1 = bf16[32,24,128]{2,1,0:T(8,128)(2,1)} custom-call(s32[48]{0:T(128)S(1)} %get-tuple-element.33.pos, s32[16]{0:T(128)S(1)} %copy-done.2, bf16[96,24,256]{2,1,0:T(8,128)(2,1)S(1)} %get-tuple-element.57.near, bf16[32,24,256]{2,1,0:T(8,128)(2,1)S(1)} %bitcast.49, bf16[48,256,256]{2,1,0:T(8,128)(2,1)} %tiles_in.1), custom_call_target="tpu_custom_call" | custom-call | flops 150994944 | bytes 7340032 | tf_op jit(solution)/shard_map/aggregate/pallas_call | solution.py:100
  108.6 0.0 copy-start
  108.6 0.0 copy-start.1
  108.6 17.6 %all-to-all-start.3 = ((bf16[32,24,128]{2,1,0:T(8,128)(2,1)}), bf16[32,24,128]{2,1,0:T(8,128)(2,1)S(1)}, u32[]{:S(2)}, u32[]{:S(2)}) async-start(bf16[32,24,128]{2,1,0:T(8,128)(2,1)} %aggregate.1), calls=%async_computation.3 | async-start | bytes 393216 | tf_op jit(solution)/shard_map/all_to_all | solution.py:236
  126.2 0.0 copy-done.3
  126.2 0.3 copy.19
  126.5 16.3 %all-to-all-done.3 = bf16[32,24,128]{2,1,0:T(8,128)(2,1)S(1)} async-done(((bf16[32,24,128]{2,1,0:T(8,128)(2,1)}), bf16[32,24,128]{2,1,0:T(8,128)(2,1)S(1)}, u32[]{:S(2)}, u32[]{:S(2)}) %all-to-all-start.3) | async-done | bytes 196640 | tf_op jit(solution)/shard_map/all_to_all | solution.py:236
  142.8 0.0 copy-done
  142.8 0.0 copy-done.1
  142.8 1.2 dense.1
  144.0 17.0 %all_to_all.38.parts = bf16[32,4,24,128]{3,2,1,0:T(8,128)(2,1)S(1)} all-to-all(bf16[32,4,24,128]{3,2,1,0:T(8,128)(2,1)S(1)} %get-tuple-element.39), channel_id=1, replica_groups=mesh['x'=4,'zh'=4,'c'=2,'zl'=8,'y'=4] {'x','c','y'}, dimensions={0} | all-to-all | bytes 1572864 | tf_op jit(solution)/shard_map/all_to_all | solution.py:238
  161.0 0.2 fold.1
  161.2 15.2 %all_to_all.39 = f32[8,16,96]{2,1,0:T(8,128)S(1)} all-to-all(f32[8,16,96]{2,1,0:T(8,128)S(1)} %fold.1), channel_id=1, replica_groups=mesh['x'=4,'zh'=4,'c'=2,'zl'=8,'y'=4] {'zl'}, dimensions={0} | all-to-all | bytes 98304 | tf_op jit(solution)/shard_map/all_to_all | solution.py:239
  176.4 0.1 reshape.112
  176.5 0.1 reshape.123
  176.6 35.4 %all_to_all.40 = f32[4,1,384]{2,1,0:T(1,128)S(1)} all-to-all(f32[4,1,384]{2,1,0:T(1,128)S(1)} %reshape.123), channel_id=1, replica_groups=mesh['x'=4,'zh'=4,'c'=2,'zl'=8,'y'=4] {'zh'}, dimensions={0} | all-to-all | bytes 12288 | tf_op jit(solution)/shard_map/all_to_all | solution.py:242
  212.0 0.5 broadcast.357
  212.5 0.7 reduce.4
  213.2 0.1 reshape.124
  213.3 0.6 broadcast_multiply_fusion
  (5 shorter events, 0.0 us)
Async XLA Ops:
  0.6 45.0 %collective-permute-start.1 = (bf16[24,4096]{1,0:T(8,128)(2,1)}, bf16[24,4096]{1,0:T(8,128)(2,1)}, u32[]{:S(2)}, u32[]{:S(2)}) collective-permute-start(bf16[24,4096]{1,0:T(8,128)(2,1)} %param.12), channel_id=1, source_target_pairs={{0,64},{32,224},{64,128},{96,32},{128,192},{160,96},{192,0},{224,1... | collective-permute-start | bytes 589832 | tf_op jit(solution)/shard_map/ppermute | solution.py:179
  20.1 15.0 %all-to-all-start.1 = ((s32[8,1,16]{2,1,0:T(1,128)}), s32[8,1,16]{2,1,0:T(1,128)S(1)}, u32[]{:S(2)}, u32[]{:S(2)}) async-start(s32[8,1,16]{2,1,0:T(1,128)} %bitcast.4), calls=%async_computation.1 | async-start | bytes 8192 | tf_op jit(solution)/shard_map/cond/branch_1_fun/all_to_all | solution.py:217
  31.3 5.0 %collective-permute-start = (bf16[24,4096]{1,0:T(8,128)(2,1)}, bf16[24,4096]{1,0:T(8,128)(2,1)}, u32[]{:S(2)}, u32[]{:S(2)}) collective-permute-start(bf16[24,4096]{1,0:T(8,128)(2,1)} %get-tuple-element.19), channel_id=1, source_target_pairs={{0,32},{32,0},{1,33},{33,1},{2,34},{34,2},{3,35},{35,3},{4,36},{36... | collective-permute-start | bytes 589832 | tf_op jit(solution)/shard_map/cond/branch_1_fun/ppermute | solution.py:216
  36.3 22.1 %collective-permute-start.2 = (bf16[24,4096]{1,0:T(8,128)(2,1)}, bf16[24,4096]{1,0:T(8,128)(2,1)S(1)}, u32[]{:S(2)}, u32[]{:S(2)}) collective-permute-start(bf16[24,4096]{1,0:T(8,128)(2,1)} %get-tuple-element.35), channel_id=1, source_target_pairs={{0,64},{32,224},{64,128},{96,32},{128,192},{160,96},{192,0},{224,1... | collective-permute-start | bytes 589832 | tf_op jit(solution)/shard_map/ppermute | solution.py:179
  45.6 46.0 %collective-permute-start.3 = (bf16[24,4096]{1,0:T(8,128)(2,1)}, bf16[24,4096]{1,0:T(8,128)(2,1)S(1)}, u32[]{:S(2)}, u32[]{:S(2)}) collective-permute-start(bf16[24,4096]{1,0:T(8,128)(2,1)} %collective-permute-done.1), channel_id=1, source_target_pairs={{0,64},{32,224},{64,128},{96,32},{128,192},{160,96},{192,0},{224,1... | collective-permute-start | bytes 589832 | tf_op jit(solution)/shard_map/ppermute | solution.py:179
  91.6 12.0 %copy-start.2 = (s32[16]{0:T(128)S(1)}, s32[16]{0:T(128)}, u32[]{:S(2)}) copy-start(s32[16]{0:T(128)} %counts.1) | copy-start | bytes 196
  103.6 22.6 %copy-start.3 = (bf16[768,512]{1,0:T(8,128)(2,1)S(1)}, bf16[768,512]{1,0:T(8,128)(2,1)}, u32[]{:S(2)}) copy-start(bf16[768,512]{1,0:T(8,128)(2,1)} %param.17) | copy-start | bytes 2359300
  108.6 34.2 %copy-start = (bf16[512,128]{1,0:T(8,128)(2,1)S(1)}, bf16[512,128]{1,0:T(8,128)(2,1)}, u32[]{:S(2)}) copy-start(bf16[512,128]{1,0:T(8,128)(2,1)} %self_part.1) | copy-start | bytes 393220
  108.6 34.2 %copy-start.1 = (bf16[512,128]{1,0:T(8,128)(2,1)S(1)}, bf16[512,128]{1,0:T(8,128)(2,1)}, u32[]{:S(2)}) copy-start(bf16[512,128]{1,0:T(8,128)(2,1)} %cotangent.1) | copy-start | bytes 393220
  108.6 34.2 %all-to-all-start.3 = ((bf16[32,24,128]{2,1,0:T(8,128)(2,1)}), bf16[32,24,128]{2,1,0:T(8,128)(2,1)S(1)}, u32[]{:S(2)}, u32[]{:S(2)}) async-start(bf16[32,24,128]{2,1,0:T(8,128)(2,1)} %aggregate.1), calls=%async_computation.3 | async-start | bytes 393216 | tf_op jit(solution)/shard_map/all_to_all | solution.py:236

commit v8 on v6

--- a/solution.py
+++ b/solution.py
@@ -13,6 +13,7 @@
 X, ZH, CORE, ZL, Y = 4, 4, 2, 8, 4
 OWN, NEAR, FAR = CAP, 2 * CAP, CAP
 PEERS = X * CORE
+LANES = 128
 GROUPS = 4
 VMEM = 16 * 1024 * 1024
 f32, bf16 = jnp.float32, jnp.bfloat16
@@ -175,11 +176,11 @@
     )(rows, w_t, self_part, cotangent)
 
 
-def onward(value):
+def onward(value, step):
     pairs = []
     for z in range(ZH):
-        pairs.append((z * CORE, (z + 1) % ZH * CORE))
-        pairs.append((z * CORE + 1, (z - 1) % ZH * CORE + 1))
+        pairs.append((z * CORE, (z + step) % ZH * CORE))
+        pairs.append((z * CORE + 1, (z - step) % ZH * CORE + 1))
     return lax.ppermute(value, ("zh", "c"), pairs)
 
 
@@ -187,9 +188,9 @@
     me = lax.axis_index("zh")
     slots = owners.shape[0]
     core = owners % CORE
-    apart = (owners // CORE + ZH - me) % ZH
-    server = jnp.where(apart == 3, 0, jnp.where(apart == 1, 1, core))
-    column = (owners // (ZH * CORE)) * CORE + server
+    column = (owners // (ZH * CORE)) * CORE + core
+    apart = (me + ZH - owners // CORE % ZH) % ZH
+    apart = jnp.where(core == 0, apart, (ZH - apart) % ZH)
     near, far = apart % 2 == 1, apart == 2
     group = column + jnp.where(far, 2 * PEERS, jnp.where(near, PEERS, 0))
     s = jnp.arange(slots, dtype=jnp.int32)
@@ -200,9 +201,9 @@
         PEERS * (OWN + NEAR) + column * FAR,
         jnp.where(near, PEERS * OWN + column * NEAR, column * OWN),
     )
-    place = column * (OWN + NEAR + FAR) + rank + jnp.where(far, OWN + NEAR, jnp.where(near, OWN, 0))
-    code = local + jnp.where(near & (server != core), 16, 0)
-    hit = place[:, None] == jnp.arange(PEERS * (OWN + NEAR + FAR), dtype=jnp.int32)[None, :]
+    place = column * LANES + rank + jnp.where(far, OWN + NEAR, jnp.where(near, OWN, 0))
+    code = local + jnp.where(apart == 3, 16, 0)
+    hit = place[:, None] == jnp.arange(PEERS * LANES, dtype=jnp.int32)[None, :]
     return pos, jnp.sum(jnp.where(hit, code[:, None], 0), axis=0)
 
 
@@ -221,23 +222,22 @@
 
     def asking():
         pos, ask = plan(src_owner[:, 0], src_local)
-        other = lax.ppermute(features, "c", [(0, 1), (1, 0)])
-        codes = lax.all_to_all(ask.reshape(PEERS, -1), ("x", "c"), 0, 0)
-        return pos, codes.reshape(-1), other
-
-    first = onward(features)
-    pos, codes, other = beside(
+        codes = lax.all_to_all(ask.reshape(PEERS, 1, LANES), ("x", "c"), 0, 0)
+        return pos, codes.reshape(-1)
+
+    first = onward(features, 1)
+    pos, codes = beside(
         asking,
         (src_local.shape, jnp.int32),
-        ((PEERS * (OWN + NEAR + FAR),), jnp.int32),
-        (features.shape, bf16),
-    )
-    second = onward(other)
+        ((PEERS * LANES,), jnp.int32),
+    )
+    codes, again = lax.optimization_barrier((codes, features))
+    second = onward(again, -1)
     (own,) = beside(
         lambda: (exchange(pack(codes, (features,), 0, OWN, width)),), ((PEERS * OWN, rows, width), bf16)
     )
     own, first = lax.optimization_barrier((own, first))
-    third = onward(first)
+    third = onward(first, 1)
     (near,) = beside(
         lambda: (exchange(pack(codes, (first, second), OWN, NEAR, width)),), ((PEERS * NEAR, rows, width), bf16)
     )
@@ -249,8 +249,9 @@
     grad = fold(lax.all_to_all(grad, ("x", "c", "y"), 0, 0))
     grad = jnp.sum(lax.all_to_all(grad, "zl", 0, 0), axis=0)
     grad = jnp.transpose(grad.reshape(-1, ZH, rows), (1, 0, 2))
+    grad = lax.all_to_all(jnp.pad(grad, ((0, 0), (0, 0), (0, LANES - rows))), "zh", 0, 0)
     grad_scale = 1.0 / math.sqrt(cols * X * ZH * CORE)
-    return hidden, jnp.sum(lax.all_to_all(grad, "zh", 0, 0), axis=0) * grad_scale
+    return hidden, jnp.sum(grad, axis=0)[:, :rows] * grad_scale
 
 
 def solution(mesh):

time: 198 us -> 197 us (level)
  the two profiles are of different devices: /device:TPU:2 before, /device:TPU:32 now
where the time goes in v8:
time: 197 us; the launch traced here: 196 us
  blocking collectives  106 us (54%)
  starting transfers between devices  50.2 us (25%)
  waiting for transfers between devices  25.3 us (13%)
  Pallas kernels  9.74 us (5%)
  other arithmetic  3.6 us (2%)
    all_to_all x3, blocking collectives, exchange(): lax.all_to_all(packed, ('x', 'c'), 0, 0).reshape((-1,) + packed.shape[2:])  39.8 us
    all_to_all x1, blocking collectives, per_device(): lax.all_to_all(jnp.pad(grad, ((0, 0), (0, 0), (0, LANES - rows))), 'zh',...  33.4 us
    ppermute x3, starting transfers between devices, onward(): return lax.ppermute(value, ('zh', 'c'), pairs)  30.5 us
    all_to_all x1, blocking collectives, per_device(): grad = fold(lax.all_to_all(grad, ('x', 'c', 'y'), 0, 0))  17.8 us
    all_to_all x1, waiting for transfers between devices, per_device(): lax.all_to_all(aggregated, ('zl', 'y'), 0, 0).reshape(-1, node_cols)  15 us
    all_to_all x1, blocking collectives, per_device(): grad = jnp.sum(lax.all_to_all(grad, 'zl', 0, 0), axis=0)  14.7 us
    all_to_all x1, starting transfers between devices, asking(): codes = lax.all_to_all(ask.reshape(PEERS, 1, LANES), ('x', 'c'), 0, 0)  9.84 us
    all_to_all x1, starting transfers between devices, per_device(): lax.all_to_all(aggregated, ('zl', 'y'), 0, 0).reshape(-1, node_cols)  9.82 us
  transfers between devices with their start and end apart: 5, of which 4 were waited for; matrix products, arithmetic and copies ran while one was open for 2% of the time, Pallas kernels for 1%

profile of v8, /device:TPU:32, one launch (start us, length us, event | category | flops | bytes accessed | tf_op | source)
XLA Modules:
  0.0 196.3 jit_solution(11204804942718599016)
XLA Ops:
  0.6 0.0 copy-start.2
  0.6 15.7 %collective-permute-start = (bf16[24,4096]{1,0:T(8,128)(2,1)}, bf16[24,4096]{1,0:T(8,128)(2,1)}, u32[]{:S(2)}, u32[]{:S(2)}) collective-permute-start(bf16[24,4096]{1,0:T(8,128)(2,1)} %param.14), channel_id=1, source_target_pairs={{0,64},{32,224},{64,128},{96,32},{128,192},{160,96},{192,0},{224,1... | collective-permute-start | bytes 589832 | tf_op jit(solution)/shard_map/ppermute | solution.py:184
  17.0 18.0 %conditional.3 = (s32[48]{0:T(128)S(1)}, s32[1024]{0:T(1024)}) conditional(s32[]{:T(128)} %bitcast.8, () %tuple.31, (s32[48,1]{0,1:T(1,128)}, s32[48]{0:T(128)}) %tuple.32), branch_computations={%region_0.0_spmd, %region_1.4_spmd} | conditional | flops 168564 | bytes 21284 | solution.py:221
  17.0 0.7 fusion.16
  17.7 0.7 fusion.7
  18.5 0.7 fusion.3
  19.1 0.2 convert_reduce_fusion
  19.3 0.7 select_reduce_fusion
  20.0 9.8 %all-to-all-start.2 = ((s32[8,1,128]{2,1,0:T(1,128)}), s32[8,1,128]{2,1,0:T(1,128)}, u32[]{:S(2)}, u32[]{:S(2)}) async-start(s32[8,1,128]{2,1,0:T(1,128)} %bitcast.4), calls=%async_computation.2 | async-start | bytes 8192 | tf_op jit(solution)/shard_map/cond/branch_1_fun/all_to_all | solution.py:225
  29.9 5.1 %all-to-all-done.2 = s32[8,1,128]{2,1,0:T(1,128)} async-done(((s32[8,1,128]{2,1,0:T(1,128)}), s32[8,1,128]{2,1,0:T(1,128)}, u32[]{:S(2)}, u32[]{:S(2)}) %all-to-all-start.2) | async-done | bytes 4128 | tf_op jit(solution)/shard_map/cond/branch_1_fun/all_to_all | solution.py:225
  35.0 8.4 %collective-permute-start.1 = (bf16[24,4096]{1,0:T(8,128)(2,1)}, bf16[24,4096]{1,0:T(8,128)(2,1)S(1)}, u32[]{:S(2)}, u32[]{:S(2)}) collective-permute-start(bf16[24,4096]{1,0:T(8,128)(2,1)} %param.14), channel_id=1, source_target_pairs={{0,192},{32,96},{64,0},{96,160},{128,64},{160,224},{192,128},{224,... | collective-permute-start | bytes 589832 | tf_op jit(solution)/shard_map/ppermute | solution.py:184
  43.4 12.5 %conditional.4 = (bf16[32,24,256]{2,1,0:T(8,128)(2,1)S(1)}) conditional(s32[]{:T(128)} %bitcast.8, () %tuple.33, (s32[1024]{0:T(1024)}, bf16[24,4096]{1,0:T(8,128)(2,1)}) %tuple.35), branch_computations={%region_4.5_spmd, %region_5.6_spmd} | conditional | bytes 2883592 | solution.py:221
  43.5 1.1 pack.3
  44.6 11.3 %all_to_all.37 = bf16[8,4,24,256]{3,2,1,0:T(8,128)(2,1)S(1)} all-to-all(bf16[8,4,24,256]{3,2,1,0:T(8,128)(2,1)S(1)} %pack.3), channel_id=1, replica_groups=mesh['x'=4,'zh'=4,'c'=2,'zl'=8,'y'=4] {'x','c'}, dimensions={0} | all-to-all | bytes 786432 | tf_op jit(solution)/shard_map/cond/branch_1_fun/all_to_all | solution.py:211
  55.9 0.0 collective-permute-done
  55.9 6.4 %collective-permute-start.2 = (bf16[24,4096]{1,0:T(8,128)(2,1)}, bf16[24,4096]{1,0:T(8,128)(2,1)S(1)}, u32[]{:S(2)}, u32[]{:S(2)}) collective-permute-start(bf16[24,4096]{1,0:T(8,128)(2,1)} %collective-permute-done), channel_id=1, source_target_pairs={{0,64},{32,224},{64,128},{96,32},{128,192},{160,96},{192,0},{224,1... | collective-permute-start | bytes 589832 | tf_op jit(solution)/shard_map/ppermute | solution.py:184
  62.3 3.2 %collective-permute-done.1 = bf16[24,4096]{1,0:T(8,128)(2,1)S(1)} collective-permute-done((bf16[24,4096]{1,0:T(8,128)(2,1)}, bf16[24,4096]{1,0:T(8,128)(2,1)S(1)}, u32[]{:S(2)}, u32[]{:S(2)}) %collective-permute-start.1) | collective-permute-done | bytes 196640 | tf_op jit(solution)/shard_map/ppermute | solution.py:184
  65.5 0.0 copy-start.3
  65.5 17.8 %conditional.5 = (bf16[64,24,256]{2,1,0:T(8,128)(2,1)S(1)}) conditional(s32[]{:T(128)} %bitcast.8, () %tuple.37, (s32[1024]{0:T(1024)}, bf16[24,4096]{1,0:T(8,128)(2,1)}, bf16[24,4096]{1,0:T(8,128)(2,1)S(1)}) %tuple.38), branch_computations={%region_6.7_spmd, %region_7.8_spmd} | conditional | bytes 3670024 | solution.py:221
  65.5 1.4 pack.4
  66.8 16.4 %all_to_all.38 = bf16[8,8,24,256]{3,2,1,0:T(8,128)(2,1)S(1)} all-to-all(bf16[8,8,24,256]{3,2,1,0:T(8,128)(2,1)S(1)} %pack.4), channel_id=1, replica_groups=mesh['x'=4,'zh'=4,'c'=2,'zl'=8,'y'=4] {'x','c'}, dimensions={0} | all-to-all | bytes 1572864 | tf_op jit(solution)/shard_map/cond/branch_1_fun/all_to_all | solution.py:211
  83.2 0.0 copy-start
  83.2 0.0 copy-start.1
  83.2 2.0 %collective-permute-done.2.refs_1_ = bf16[24,4096]{1,0:T(8,128)(2,1)S(1)} collective-permute-done((bf16[24,4096]{1,0:T(8,128)(2,1)}, bf16[24,4096]{1,0:T(8,128)(2,1)S(1)}, u32[]{:S(2)}, u32[]{:S(2)}) %collective-permute-start.2) | collective-permute-done | bytes 196640 | tf_op jit(solution)/shard_map/ppermute | solution.py:184
  85.3 0.9 pack.5
  86.1 12.1 %all_to_all.39 = bf16[8,4,24,256]{3,2,1,0:T(8,128)(2,1)S(1)} all-to-all(bf16[8,4,24,256]{3,2,1,0:T(8,128)(2,1)S(1)} %pack.5), channel_id=1, replica_groups=mesh['x'=4,'zh'=4,'c'=2,'zl'=8,'y'=4] {'x','c'}, dimensions={0} | all-to-all | bytes 786432 | tf_op jit(solution)/shard_map/all_to_all | solution.py:211
  98.2 0.0 copy-done.2
  98.2 5.0 %aggregate.1 = bf16[32,24,128]{2,1,0:T(8,128)(2,1)} custom-call(s32[48]{0:T(128)S(1)} %get-tuple-element.39.pos, s32[16]{0:T(128)S(1)} %copy-done.2, bf16[32,24,256]{2,1,0:T(8,128)(2,1)S(1)} %get-tuple-element.64.own, bf16[64,24,256]{2,1,0:T(8,128)(2,1)S(1)} %get-tuple-element.65.near, bf16[32,24,256]{2,1,0:T(8,128)(2,1)S(1)} %bitcast.49, ...), custom_call_target="tpu_custom_call" | custom-call | flops 150994944 | bytes 7340032 | tf_op jit(solution)/shard_map/aggregate/pallas_call | solution.py:105
  103.2 9.8 %all-to-all-start.4 = ((bf16[32,24,128]{2,1,0:T(8,128)(2,1)}), bf16[32,24,128]{2,1,0:T(8,128)(2,1)S(1)}, u32[]{:S(2)}, u32[]{:S(2)}) async-start(bf16[32,24,128]{2,1,0:T(8,128)(2,1)} %aggregate.1), calls=%async_computation.4 | async-start | bytes 393216 | tf_op jit(solution)/shard_map/all_to_all | solution.py:247
  113.0 0.0 copy-done.3
  113.0 0.3 copy.16
  113.3 15.0 %all-to-all-done.4 = bf16[32,24,128]{2,1,0:T(8,128)(2,1)S(1)} async-done(((bf16[32,24,128]{2,1,0:T(8,128)(2,1)}), bf16[32,24,128]{2,1,0:T(8,128)(2,1)S(1)}, u32[]{:S(2)}, u32[]{:S(2)}) %all-to-all-start.4) | async-done | bytes 196640 | tf_op jit(solution)/shard_map/all_to_all | solution.py:247
  128.2 0.0 copy-done
  128.2 0.0 copy-done.1
  128.2 1.2 dense.1
  129.5 17.8 %all_to_all.40.parts = bf16[32,4,24,128]{3,2,1,0:T(8,128)(2,1)S(1)} all-to-all(bf16[32,4,24,128]{3,2,1,0:T(8,128)(2,1)S(1)} %get-tuple-element.48), channel_id=1, replica_groups=mesh['x'=4,'zh'=4,'c'=2,'zl'=8,'y'=4] {'x','c','y'}, dimensions={0} | all-to-all | bytes 1572864 | tf_op jit(solution)/shard_map/all_to_all | solution.py:249
  147.3 0.2 fold.1
  147.5 14.7 %all_to_all.41 = f32[8,16,96]{2,1,0:T(8,128)S(1)} all-to-all(f32[8,16,96]{2,1,0:T(8,128)S(1)} %fold.1), channel_id=1, replica_groups=mesh['x'=4,'zh'=4,'c'=2,'zl'=8,'y'=4] {'zl'}, dimensions={0} | all-to-all | bytes 98304 | tf_op jit(solution)/shard_map/all_to_all | solution.py:250
  162.2 0.1 reshape.146
  162.3 33.4 %all_to_all.42 = f32[4,16,128]{2,1,0:T(8,128)S(1)} all-to-all(f32[4,16,128]{2,1,0:T(8,128)S(1)} %pad.4.clone), channel_id=1, replica_groups=mesh['x'=4,'zh'=4,'c'=2,'zl'=8,'y'=4] {'zh'}, dimensions={0} | all-to-all | bytes 65536 | tf_op jit(solution)/shard_map/all_to_all | solution.py:252
  195.7 0.6 slice_multiply_fusion
  (6 shorter events, 0.1 us)
Async XLA Ops:
  0.6 97.6 %copy-start.2 = (s32[16]{0:T(128)S(1)}, s32[16]{0:T(128)}, u32[]{:S(2)}) copy-start(s32[16]{0:T(128)} %counts.1) | copy-start | bytes 196
  0.6 55.3 %collective-permute-start = (bf16[24,4096]{1,0:T(8,128)(2,1)}, bf16[24,4096]{1,0:T(8,128)(2,1)}, u32[]{:S(2)}, u32[]{:S(2)}) collective-permute-start(bf16[24,4096]{1,0:T(8,128)(2,1)} %param.14), channel_id=1, source_target_pairs={{0,64},{32,224},{64,128},{96,32},{128,192},{160,96},{192,0},{224,1... | collective-permute-start | bytes 589832 | tf_op jit(solution)/shard_map/ppermute | solution.py:184
  20.0 15.0 %all-to-all-start.2 = ((s32[8,1,128]{2,1,0:T(1,128)}), s32[8,1,128]{2,1,0:T(1,128)}, u32[]{:S(2)}, u32[]{:S(2)}) async-start(s32[8,1,128]{2,1,0:T(1,128)} %bitcast.4), calls=%async_computation.2 | async-start | bytes 8192 | tf_op jit(solution)/shard_map/cond/branch_1_fun/all_to_all | solution.py:225
  35.0 30.5 %collective-permute-start.1 = (bf16[24,4096]{1,0:T(8,128)(2,1)}, bf16[24,4096]{1,0:T(8,128)(2,1)S(1)}, u32[]{:S(2)}, u32[]{:S(2)}) collective-permute-start(bf16[24,4096]{1,0:T(8,128)(2,1)} %param.14), channel_id=1, source_target_pairs={{0,192},{32,96},{64,0},{96,160},{128,64},{160,224},{192,128},{224,... | collective-permute-start | bytes 589832 | tf_op jit(solution)/shard_map/ppermute | solution.py:184
  55.9 29.3 %collective-permute-start.2 = (bf16[24,4096]{1,0:T(8,128)(2,1)}, bf16[24,4096]{1,0:T(8,128)(2,1)S(1)}, u32[]{:S(2)}, u32[]{:S(2)}) collective-permute-start(bf16[24,4096]{1,0:T(8,128)(2,1)} %collective-permute-done), channel_id=1, source_target_pairs={{0,64},{32,224},{64,128},{96,32},{128,192},{160,96},{192,0},{224,1... | collective-permute-start | bytes 589832 | tf_op jit(solution)/shard_map/ppermute | solution.py:184
  65.5 47.5 %copy-start.3 = (bf16[768,512]{1,0:T(8,128)(2,1)S(1)}, bf16[768,512]{1,0:T(8,128)(2,1)}, u32[]{:S(2)}) copy-start(bf16[768,512]{1,0:T(8,128)(2,1)} %param.19) | copy-start | bytes 2359300
  83.2 45.0 %copy-start = (bf16[512,128]{1,0:T(8,128)(2,1)S(1)}, bf16[512,128]{1,0:T(8,128)(2,1)}, u32[]{:S(2)}) copy-start(bf16[512,128]{1,0:T(8,128)(2,1)} %self_part.1) | copy-start | bytes 393220
  83.2 45.0 %copy-start.1 = (bf16[512,128]{1,0:T(8,128)(2,1)S(1)}, bf16[512,128]{1,0:T(8,128)(2,1)}, u32[]{:S(2)}) copy-start(bf16[512,128]{1,0:T(8,128)(2,1)} %cotangent.1) | copy-start | bytes 393220
  103.2 25.1 %all-to-all-start.4 = ((bf16[32,24,128]{2,1,0:T(8,128)(2,1)}), bf16[32,24,128]{2,1,0:T(8,128)(2,1)S(1)}, u32[]{:S(2)}, u32[]{:S(2)}) async-start(bf16[32,24,128]{2,1,0:T(8,128)(2,1)} %aggregate.1), calls=%async_computation.4 | async-start | bytes 393216 | tf_op jit(solution)/shard_map/all_to_all | solution.py:247

commit v9 on v8

--- a/solution.py
+++ b/solution.py
@@ -222,19 +222,16 @@
 
     def asking():
         pos, ask = plan(src_owner[:, 0], src_local)
-        codes = lax.all_to_all(ask.reshape(PEERS, 1, LANES), ("x", "c"), 0, 0)
-        return pos, codes.reshape(-1)
+        codes = lax.all_to_all(ask.reshape(PEERS, 1, LANES), ("x", "c"), 0, 0).reshape(-1)
+        return pos, codes, exchange(pack(codes, (features,), 0, OWN, width))
 
     first = onward(features, 1)
-    pos, codes = beside(
+    second = onward(features, -1)
+    pos, codes, own = beside(
         asking,
         (src_local.shape, jnp.int32),
         ((PEERS * LANES,), jnp.int32),
-    )
-    codes, again = lax.optimization_barrier((codes, features))
-    second = onward(again, -1)
-    (own,) = beside(
-        lambda: (exchange(pack(codes, (features,), 0, OWN, width)),), ((PEERS * OWN, rows, width), bf16)
+        ((PEERS * OWN, rows, width), bf16),
     )
     own, first = lax.optimization_barrier((own, first))
     third = onward(first, 1)

time: 197 us -> 199 us (1.010)
  the two profiles are of different devices: /device:TPU:32 before, /device:TPU:2 now
where the time goes in v9:
time: 199 us; the launch traced here: 198 us
  blocking collectives  107 us (54%)
  starting transfers between devices  51.1 us (26%)
  waiting for transfers between devices  23.9 us (12%)
  Pallas kernels  11.1 us (6%)
  other arithmetic  3 us (2%)
    ppermute x3, starting transfers between devices, onward(): return lax.ppermute(value, ('zh', 'c'), pairs)  38.1 us
    all_to_all x1, blocking collectives, per_device(): lax.all_to_all(jnp.pad(grad, ((0, 0), (0, 0), (0, LANES - rows))), 'zh',...  34.4 us
    all_to_all x2, blocking collectives, exchange(): lax.all_to_all(packed, ('x', 'c'), 0, 0).reshape((-1,) + packed.shape[2:])  31.2 us
    all_to_all x1, blocking collectives, per_device(): grad = fold(lax.all_to_all(grad, ('x', 'c', 'y'), 0, 0))  17 us
    all_to_all x1, waiting for transfers between devices, per_device(): lax.all_to_all(aggregated, ('zl', 'y'), 0, 0).reshape(-1, node_cols)  16.3 us
    all_to_all x1, blocking collectives, per_device(): grad = jnp.sum(lax.all_to_all(grad, 'zl', 0, 0), axis=0)  15.2 us
    all_to_all x1, blocking collectives, asking(): lax.all_to_all(ask.reshape(PEERS, 1, LANES), ('x', 'c'), 0, 0).reshape(-1)  9.57 us
    all_to_all x1, starting transfers between devices, per_device(): lax.all_to_all(aggregated, ('zl', 'y'), 0, 0).reshape(-1, node_cols)  7.73 us
  transfers between devices with their start and end apart: 5, of which 2 were waited for; matrix products, arithmetic and copies ran while one was open for 1% of the time, Pallas kernels for 2%

profile of v9, /device:TPU:2, one launch (start us, length us, event | category | flops | bytes accessed | tf_op | source)
XLA Modules:
  0.0 198.2 jit_solution(8288095608805540819)
XLA Ops:
  0.6 0.0 copy-start.2
  0.6 15.7 %collective-permute-start = (bf16[24,4096]{1,0:T(8,128)(2,1)}, bf16[24,4096]{1,0:T(8,128)(2,1)}, u32[]{:S(2)}, u32[]{:S(2)}) collective-permute-start(bf16[24,4096]{1,0:T(8,128)(2,1)} %param.12), channel_id=1, source_target_pairs={{0,64},{32,224},{64,128},{96,32},{128,192},{160,96},{192,0},{224,1... | collective-permute-start | bytes 589832 | tf_op jit(solution)/shard_map/ppermute | solution.py:184
  16.4 9.2 %collective-permute-start.1 = (bf16[24,4096]{1,0:T(8,128)(2,1)}, bf16[24,4096]{1,0:T(8,128)(2,1)S(1)}, u32[]{:S(2)}, u32[]{:S(2)}) collective-permute-start(bf16[24,4096]{1,0:T(8,128)(2,1)} %param.12), channel_id=1, source_target_pairs={{0,192},{32,96},{64,0},{96,160},{128,64},{160,224},{192,128},{224,... | collective-permute-start | bytes 589832 | tf_op jit(solution)/shard_map/ppermute | solution.py:184
  26.2 26.7 %conditional.2 = (s32[48]{0:T(128)S(1)}, s32[1024]{0:T(1024)}, bf16[32,24,256]{2,1,0:T(8,128)(2,1)}) conditional(s32[]{:T(128)} %bitcast.8, () %tuple.24, (s32[48,1]{0,1:T(1,128)}, s32[48]{0:T(128)}, bf16[24,4096]{1,0:T(8,128)(2,1)}) %tuple.25), branch_computations={%region_0.0_spmd, %region_1.4_spmd} | conditional | flops 168564 | bytes 3293996 | solution.py:221
  26.2 0.7 fusion.16
  27.0 0.7 fusion.7
  27.7 0.7 fusion.3
  28.3 0.2 convert_reduce_fusion
  28.5 0.1 select_reduce_fusion
  28.6 9.6 %all_to_all.37 = s32[8,1,128]{2,1,0:T(1,128)} all-to-all(s32[8,1,128]{2,1,0:T(1,128)S(1)} %bitcast.54), channel_id=1, replica_groups=mesh['x'=4,'zh'=4,'c'=2,'zl'=8,'y'=4] {'x','c'}, dimensions={0} | all-to-all | bytes 8192 | tf_op jit(solution)/shard_map/cond/branch_1_fun/all_to_all | solution.py:225
  38.2 1.8 pack.3
  40.0 5.3 %all-to-all-start.2 = ((bf16[8,4,24,256]{3,2,1,0:T(8,128)(2,1)}), bf16[8,4,24,256]{3,2,1,0:T(8,128)(2,1)}, u32[]{:S(2)}, u32[]{:S(2)}) async-start(bf16[8,4,24,256]{3,2,1,0:T(8,128)(2,1)} %pack.3), calls=%async_computation.2 | async-start | bytes 786432 | tf_op jit(solution)/shard_map/cond/branch_1_fun/all_to_all | solution.py:211
  45.3 7.6 %all-to-all-done.2 = bf16[8,4,24,256]{3,2,1,0:T(8,128)(2,1)} async-done(((bf16[8,4,24,256]{3,2,1,0:T(8,128)(2,1)}), bf16[8,4,24,256]{3,2,1,0:T(8,128)(2,1)}, u32[]{:S(2)}, u32[]{:S(2)}) %all-to-all-start.2) | async-done | bytes 393248 | tf_op jit(solution)/shard_map/cond/branch_1_fun/all_to_all | solution.py:211
  52.9 0.0 collective-permute-done
  52.9 13.1 %collective-permute-start.2 = (bf16[24,4096]{1,0:T(8,128)(2,1)}, bf16[24,4096]{1,0:T(8,128)(2,1)S(1)}, u32[]{:S(2)}, u32[]{:S(2)}) collective-permute-start(bf16[24,4096]{1,0:T(8,128)(2,1)} %collective-permute-done), channel_id=1, source_target_pairs={{0,64},{32,224},{64,128},{96,32},{128,192},{160,96},{192,0},{224,1... | collective-permute-start | bytes 589832 | tf_op jit(solution)/shard_map/ppermute | solution.py:184
  66.1 0.0 collective-permute-done.1
  66.1 0.0 copy-start.3
  66.1 21.3 %conditional.3 = (bf16[64,24,256]{2,1,0:T(8,128)(2,1)S(1)}) conditional(s32[]{:T(128)} %bitcast.8, () %tuple.27, (s32[1024]{0:T(1024)}, bf16[24,4096]{1,0:T(8,128)(2,1)}, bf16[24,4096]{1,0:T(8,128)(2,1)S(1)}) %tuple.28), branch_computations={%region_4.5_spmd, %region_5.6_spmd} | conditional | bytes 3670024 | solution.py:221
  66.1 1.4 pack.4
  67.5 19.9 %all_to_all.38 = bf16[8,8,24,256]{3,2,1,0:T(8,128)(2,1)S(1)} all-to-all(bf16[8,8,24,256]{3,2,1,0:T(8,128)(2,1)S(1)} %pack.4), channel_id=1, replica_groups=mesh['x'=4,'zh'=4,'c'=2,'zl'=8,'y'=4] {'x','c'}, dimensions={0} | all-to-all | bytes 1572864 | tf_op jit(solution)/shard_map/cond/branch_1_fun/all_to_all | solution.py:211
  87.4 0.0 copy-start
  87.4 0.0 copy-start.1
  87.4 0.0 collective-permute-done.2.refs_1_
  87.4 1.0 pack.5
  88.4 11.3 %all_to_all.39 = bf16[8,4,24,256]{3,2,1,0:T(8,128)(2,1)S(1)} all-to-all(bf16[8,4,24,256]{3,2,1,0:T(8,128)(2,1)S(1)} %pack.5), channel_id=1, replica_groups=mesh['x'=4,'zh'=4,'c'=2,'zl'=8,'y'=4] {'x','c'}, dimensions={0} | all-to-all | bytes 786432 | tf_op jit(solution)/shard_map/all_to_all | solution.py:211
  99.8 0.0 copy-done.2
  99.8 5.4 %aggregate.1 = bf16[32,24,128]{2,1,0:T(8,128)(2,1)} custom-call(s32[48]{0:T(128)S(1)} %get-tuple-element.32.pos, s32[16]{0:T(128)S(1)} %copy-done.2, bf16[32,24,256]{2,1,0:T(8,128)(2,1)} %get-tuple-element.34.own, bf16[64,24,256]{2,1,0:T(8,128)(2,1)S(1)} %get-tuple-element.58.near, bf16[32,24,256]{2,1,0:T(8,128)(2,1)S(1)} %bitcast.49, ...), custom_call_target="tpu_custom_call" | custom-call | flops 150994944 | bytes 7340032 | tf_op jit(solution)/shard_map/aggregate/pallas_call | solution.py:105
  105.2 7.7 %all-to-all-start.4 = ((bf16[32,24,128]{2,1,0:T(8,128)(2,1)}), bf16[32,24,128]{2,1,0:T(8,128)(2,1)S(1)}, u32[]{:S(2)}, u32[]{:S(2)}) async-start(bf16[32,24,128]{2,1,0:T(8,128)(2,1)} %aggregate.1), calls=%async_computation.4 | async-start | bytes 393216 | tf_op jit(solution)/shard_map/all_to_all | solution.py:244
  112.9 0.0 copy-done.3
  113.0 0.3 copy.16
  113.2 16.3 %all-to-all-done.4 = bf16[32,24,128]{2,1,0:T(8,128)(2,1)S(1)} async-done(((bf16[32,24,128]{2,1,0:T(8,128)(2,1)}), bf16[32,24,128]{2,1,0:T(8,128)(2,1)S(1)}, u32[]{:S(2)}, u32[]{:S(2)}) %all-to-all-start.4) | async-done | bytes 196640 | tf_op jit(solution)/shard_map/all_to_all | solution.py:244
  129.5 0.0 copy-done
  129.5 0.0 copy-done.1
  129.5 1.2 dense.1
  130.7 17.0 %all_to_all.40.parts = bf16[32,4,24,128]{3,2,1,0:T(8,128)(2,1)S(1)} all-to-all(bf16[32,4,24,128]{3,2,1,0:T(8,128)(2,1)S(1)} %get-tuple-element.40), channel_id=1, replica_groups=mesh['x'=4,'zh'=4,'c'=2,'zl'=8,'y'=4] {'x','c','y'}, dimensions={0} | all-to-all | bytes 1572864 | tf_op jit(solution)/shard_map/all_to_all | solution.py:246
  147.7 0.2 fold.1
  147.9 15.2 %all_to_all.41 = f32[8,16,96]{2,1,0:T(8,128)S(1)} all-to-all(f32[8,16,96]{2,1,0:T(8,128)S(1)} %fold.1), channel_id=1, replica_groups=mesh['x'=4,'zh'=4,'c'=2,'zl'=8,'y'=4] {'zl'}, dimensions={0} | all-to-all | bytes 98304 | tf_op jit(solution)/shard_map/all_to_all | solution.py:247
  163.1 0.1 reshape.146
  163.2 34.4 %all_to_all.42 = f32[4,16,128]{2,1,0:T(8,128)S(1)} all-to-all(f32[4,16,128]{2,1,0:T(8,128)S(1)} %pad.4.clone), channel_id=1, replica_groups=mesh['x'=4,'zh'=4,'c'=2,'zl'=8,'y'=4] {'zh'}, dimensions={0} | all-to-all | bytes 65536 | tf_op jit(solution)/shard_map/all_to_all | solution.py:249
  197.6 0.6 slice_multiply_fusion
  (6 shorter events, 0.1 us)
Async XLA Ops:
  0.6 99.1 %copy-start.2 = (s32[16]{0:T(128)S(1)}, s32[16]{0:T(128)}, u32[]{:S(2)}) copy-start(s32[16]{0:T(128)} %counts.1) | copy-start | bytes 196
  0.6 52.3 %collective-permute-start = (bf16[24,4096]{1,0:T(8,128)(2,1)}, bf16[24,4096]{1,0:T(8,128)(2,1)}, u32[]{:S(2)}, u32[]{:S(2)}) collective-permute-start(bf16[24,4096]{1,0:T(8,128)(2,1)} %param.12), channel_id=1, source_target_pairs={{0,64},{32,224},{64,128},{96,32},{128,192},{160,96},{192,0},{224,1... | collective-permute-start | bytes 589832 | tf_op jit(solution)/shard_map/ppermute | solution.py:184
  16.4 49.7 %collective-permute-start.1 = (bf16[24,4096]{1,0:T(8,128)(2,1)}, bf16[24,4096]{1,0:T(8,128)(2,1)S(1)}, u32[]{:S(2)}, u32[]{:S(2)}) collective-permute-start(bf16[24,4096]{1,0:T(8,128)(2,1)} %param.12), channel_id=1, source_target_pairs={{0,192},{32,96},{64,0},{96,160},{128,64},{160,224},{192,128},{224,... | collective-permute-start | bytes 589832 | tf_op jit(solution)/shard_map/ppermute | solution.py:184
  40.0 12.9 %all-to-all-start.2 = ((bf16[8,4,24,256]{3,2,1,0:T(8,128)(2,1)}), bf16[8,4,24,256]{3,2,1,0:T(8,128)(2,1)}, u32[]{:S(2)}, u32[]{:S(2)}) async-start(bf16[8,4,24,256]{3,2,1,0:T(8,128)(2,1)} %pack.3), calls=%async_computation.2 | async-start | bytes 786432 | tf_op jit(solution)/shard_map/cond/branch_1_fun/all_to_all | solution.py:211
  52.9 34.5 %collective-permute-start.2 = (bf16[24,4096]{1,0:T(8,128)(2,1)}, bf16[24,4096]{1,0:T(8,128)(2,1)S(1)}, u32[]{:S(2)}, u32[]{:S(2)}) collective-permute-start(bf16[24,4096]{1,0:T(8,128)(2,1)} %collective-permute-done), channel_id=1, source_target_pairs={{0,64},{32,224},{64,128},{96,32},{128,192},{160,96},{192,0},{224,1... | collective-permute-start | bytes 589832 | tf_op jit(solution)/shard_map/ppermute | solution.py:184
  66.1 46.8 %copy-start.3 = (bf16[768,512]{1,0:T(8,128)(2,1)S(1)}, bf16[768,512]{1,0:T(8,128)(2,1)}, u32[]{:S(2)}) copy-start(bf16[768,512]{1,0:T(8,128)(2,1)} %param.17) | copy-start | bytes 2359300
  87.4 42.1 %copy-start = (bf16[512,128]{1,0:T(8,128)(2,1)S(1)}, bf16[512,128]{1,0:T(8,128)(2,1)}, u32[]{:S(2)}) copy-start(bf16[512,128]{1,0:T(8,128)(2,1)} %self_part.1) | copy-start | bytes 393220
  87.4 42.1 %copy-start.1 = (bf16[512,128]{1,0:T(8,128)(2,1)S(1)}, bf16[512,128]{1,0:T(8,128)(2,1)}, u32[]{:S(2)}) copy-start(bf16[512,128]{1,0:T(8,128)(2,1)} %cotangent.1) | copy-start | bytes 393220
  105.2 24.3 %all-to-all-start.4 = ((bf16[32,24,128]{2,1,0:T(8,128)(2,1)}), bf16[32,24,128]{2,1,0:T(8,128)(2,1)S(1)}, u32[]{:S(2)}, u32[]{:S(2)}) async-start(bf16[32,24,128]{2,1,0:T(8,128)(2,1)} %aggregate.1), calls=%async_computation.4 | async-start | bytes 393216 | tf_op jit(solution)/shard_map/all_to_all | solution.py:244

commit v10 on v7

--- a/solution.py
+++ b/solution.py
@@ -13,6 +13,7 @@
 X, ZH, CORE, ZL, Y = 4, 4, 2, 8, 4
 NEAR, FAR = 3 * CAP, CAP
 PEERS = X * CORE
+LANES = 128
 GROUPS = 4
 VMEM = 16 * 1024 * 1024
 f32, bf16 = jnp.float32, jnp.bfloat16
@@ -171,11 +172,11 @@
     )(rows, w_t, self_part, cotangent)
 
 
-def onward(value):
+def onward(value, step):
     pairs = []
     for z in range(ZH):
-        pairs.append((z * CORE, (z + 1) % ZH * CORE))
-        pairs.append((z * CORE + 1, (z - 1) % ZH * CORE + 1))
+        pairs.append((z * CORE, (z + step) % ZH * CORE))
+        pairs.append((z * CORE + 1, (z - step) % ZH * CORE + 1))
     return lax.ppermute(value, ("zh", "c"), pairs)
 
 
@@ -183,18 +184,18 @@
     me = lax.axis_index("zh")
     slots = owners.shape[0]
     core = owners % CORE
-    apart = (owners // CORE + ZH - me) % ZH
-    server = jnp.where(apart == 3, 0, jnp.where(apart == 1, 1, core))
-    column = (owners // (ZH * CORE)) * CORE + server
+    column = (owners // (ZH * CORE)) * CORE + core
+    apart = (me + ZH - owners // CORE % ZH) % ZH
+    apart = jnp.where(core == 0, apart, (ZH - apart) % ZH)
     far = apart == 2
     group = column + jnp.where(far, PEERS, 0)
     s = jnp.arange(slots, dtype=jnp.int32)
     earlier = (group[:, None] == group[None, :]) & (s[None, :] < s[:, None])
     rank = jnp.sum(earlier.astype(jnp.int32), axis=1)
     pos = rank + jnp.where(far, PEERS * NEAR + column * FAR, column * NEAR)
-    place = column * (NEAR + FAR) + rank + jnp.where(far, NEAR, 0)
-    code = local + jnp.where(apart % 2 == 1, jnp.where(server == core, 16, 32), 0)
-    hit = place[:, None] == jnp.arange(PEERS * (NEAR + FAR), dtype=jnp.int32)[None, :]
+    place = column * LANES + rank + jnp.where(far, NEAR, 0)
+    code = local + jnp.where(apart == 1, 16, jnp.where(apart == 3, 32, 0))
+    hit = place[:, None] == jnp.arange(PEERS * LANES, dtype=jnp.int32)[None, :]
     return pos, jnp.sum(jnp.where(hit, code[:, None], 0), axis=0)
 
 
@@ -213,19 +214,13 @@
 
     def asking():
         pos, ask = plan(src_owner[:, 0], src_local)
-        other = lax.ppermute(features, "c", [(0, 1), (1, 0)])
-        codes = lax.all_to_all(ask.reshape(PEERS, -1), ("x", "c"), 0, 0)
-        return pos, codes.reshape(-1), other
-
-    first = onward(features)
-    pos, codes, other = beside(
-        asking,
-        (src_local.shape, jnp.int32),
-        ((PEERS * (NEAR + FAR),), jnp.int32),
-        (features.shape, bf16),
-    )
-    second = onward(other)
-    third = onward(first)
+        return pos, lax.all_to_all(ask.reshape(PEERS, 1, LANES), ("x", "c"), 0, 0).reshape(-1)
+
+    first = onward(features, 1)
+    second = onward(features, -1)
+    pos, codes = beside(asking, (src_local.shape, jnp.int32), ((PEERS * LANES,), jnp.int32))
+    codes, first = lax.optimization_barrier((codes, first))
+    third = onward(first, 1)
     (near,) = beside(
         lambda: (exchange(pack(codes, (features, first, second), 0, NEAR, width)),),
         ((PEERS * NEAR, rows, width), bf16),
@@ -238,8 +233,9 @@
     grad = fold(lax.all_to_all(grad, ("x", "c", "y"), 0, 0))
     grad = jnp.sum(lax.all_to_all(grad, "zl", 0, 0), axis=0)
     grad = jnp.transpose(grad.reshape(-1, ZH, rows), (1, 0, 2))
+    grad = lax.all_to_all(jnp.pad(grad, ((0, 0), (0, 0), (0, LANES - rows))), "zh", 0, 0)
     grad_scale = 1.0 / math.sqrt(cols * X * ZH * CORE)
-    return hidden, jnp.sum(lax.all_to_all(grad, "zh", 0, 0), axis=0) * grad_scale
+    return hidden, jnp.sum(grad, axis=0)[:, :rows] * grad_scale
 
 
 def solution(mesh):

time: 215 us -> 202 us (0.940)
  blocking collectives: 110 us -> 103 us
  waiting for transfers between devices: 24.7 us -> 20 us
    ppermute x3, starting transfers between devices: 31.1 us -> 51.5 us  [onward(): return lax.ppermute(value, ('zh', 'c'), pairs)]
    all_to_all x1, starting transfers between devices: 17.6 us -> 5.66 us  [per_device(): lax.all_to_all(aggregated, ('zl', 'y'), 0, 0).reshape(-1, node_cols)]
    ppermute x3, waiting for transfers between devices: 6.71 us -> 0.01 us  [onward(): return lax.ppermute(value, ('zh', 'c'), pairs)]
    all_to_all x2, blocking collectives: 42.8 us -> 37.8 us  [exchange(): lax.all_to_all(packed, ('x', 'c'), 0, 0).reshape((-1,) + packed.shape[2:])]
    all_to_all x1, starting transfers between devices: 11.3 us -> 6.63 us  [asking(): lax.all_to_all(ask.reshape(PEERS, 1, LANES), ('x', 'c'), 0, 0).reshape(-1)]
    all_to_all x1, blocking collectives: 35.4 us -> 33 us  [per_device(): lax.all_to_all(jnp.pad(grad, ((0, 0), (0, 0), (0, LANES - rows))), 'zh',...]
  transfers between devices with their start and end apart: 6 -> 5, of which waited for: 3 -> 2; matrix products, arithmetic and copies ran while one was open for 2% -> 2% of each run, Pallas kernels for 1% -> 1%
where the time goes in v10:
time: 202 us; the launch traced here: 201 us
  blocking collectives  103 us (51%)
  starting transfers between devices  63.8 us (32%)
  waiting for transfers between devices  20 us (10%)
  Pallas kernels  9.04 us (4%)
  other arithmetic  3.58 us (2%)
    ppermute x3, starting transfers between devices, onward(): return lax.ppermute(value, ('zh', 'c'), pairs)  51.5 us
    all_to_all x2, blocking collectives, exchange(): lax.all_to_all(packed, ('x', 'c'), 0, 0).reshape((-1,) + packed.shape[2:])  37.8 us
    all_to_all x1, blocking collectives, per_device(): lax.all_to_all(jnp.pad(grad, ((0, 0), (0, 0), (0, LANES - rows))), 'zh',...  33 us
    all_to_all x1, blocking collectives, per_device(): grad = fold(lax.all_to_all(grad, ('x', 'c', 'y'), 0, 0))  17 us
    all_to_all x1, waiting for transfers between devices, per_device(): lax.all_to_all(aggregated, ('zl', 'y'), 0, 0).reshape(-1, node_cols)  16.3 us
    all_to_all x1, blocking collectives, per_device(): grad = jnp.sum(lax.all_to_all(grad, 'zl', 0, 0), axis=0)  15.2 us
    all_to_all x1, starting transfers between devices, asking(): lax.all_to_all(ask.reshape(PEERS, 1, LANES), ('x', 'c'), 0, 0).reshape(-1)  6.63 us
    all_to_all x1, starting transfers between devices, per_device(): lax.all_to_all(aggregated, ('zl', 'y'), 0, 0).reshape(-1, node_cols)  5.66 us
  transfers between devices with their start and end apart: 5, of which 2 were waited for; matrix products, arithmetic and copies ran while one was open for 2% of the time, Pallas kernels for 1%

profile of v10, /device:TPU:2, one launch (start us, length us, event | category | flops | bytes accessed | tf_op | source)
XLA Modules:
  0.0 201.2 jit_solution(7121613298289840843)
XLA Ops:
  0.6 15.7 %collective-permute-start = (bf16[24,4096]{1,0:T(8,128)(2,1)}, bf16[24,4096]{1,0:T(8,128)(2,1)}, u32[]{:S(2)}, u32[]{:S(2)}) collective-permute-start(bf16[24,4096]{1,0:T(8,128)(2,1)} %param.12), channel_id=1, source_target_pairs={{0,64},{32,224},{64,128},{96,32},{128,192},{160,96},{192,0},{224,1... | collective-permute-start | bytes 589832 | tf_op jit(solution)/shard_map/ppermute | solution.py:180
  16.4 9.2 %collective-permute-start.1 = (bf16[24,4096]{1,0:T(8,128)(2,1)}, bf16[24,4096]{1,0:T(8,128)(2,1)S(1)}, u32[]{:S(2)}, u32[]{:S(2)}) collective-permute-start(bf16[24,4096]{1,0:T(8,128)(2,1)} %param.12), channel_id=1, source_target_pairs={{0,192},{32,96},{64,0},{96,160},{128,64},{160,224},{192,128},{224,... | collective-permute-start | bytes 589832 | tf_op jit(solution)/shard_map/ppermute | solution.py:180
  26.2 13.3 %conditional.2 = (s32[48]{0:T(128)S(1)}, s32[1024]{0:T(1024)}) conditional(s32[]{:T(128)} %bitcast.7, () %tuple.24, (s32[48,1]{0,1:T(1,128)}, s32[48]{0:T(128)}) %tuple.25), branch_computations={%region_0.0_spmd, %region_1.4_spmd} | conditional | flops 166116 | bytes 21284 | solution.py:213
  26.2 0.7 fusion.14
  26.9 0.7 fusion.7
  27.6 0.7 fusion.3
  28.3 0.2 convert_reduce_fusion
  28.5 0.7 select_reduce_fusion
  29.2 6.6 %all-to-all-start.1 = ((s32[8,1,128]{2,1,0:T(1,128)}), s32[8,1,128]{2,1,0:T(1,128)}, u32[]{:S(2)}, u32[]{:S(2)}) async-start(s32[8,1,128]{2,1,0:T(1,128)} %bitcast.4), calls=%async_computation.1 | async-start | bytes 8192 | tf_op jit(solution)/shard_map/cond/branch_1_fun/all_to_all | solution.py:217
  35.8 3.7 %all-to-all-done.1 = s32[8,1,128]{2,1,0:T(1,128)} async-done(((s32[8,1,128]{2,1,0:T(1,128)}), s32[8,1,128]{2,1,0:T(1,128)}, u32[]{:S(2)}, u32[]{:S(2)}) %all-to-all-start.1) | async-done | bytes 4128 | tf_op jit(solution)/shard_map/cond/branch_1_fun/all_to_all | solution.py:217
  39.5 0.0 collective-permute-done
  39.5 26.5 %collective-permute-start.2 = (bf16[24,4096]{1,0:T(8,128)(2,1)}, bf16[24,4096]{1,0:T(8,128)(2,1)S(1)}, u32[]{:S(2)}, u32[]{:S(2)}) collective-permute-start(bf16[24,4096]{1,0:T(8,128)(2,1)} %collective-permute-done), channel_id=1, source_target_pairs={{0,64},{32,224},{64,128},{96,32},{128,192},{160,96},{192,0},{224,1... | collective-permute-start | bytes 589832 | tf_op jit(solution)/shard_map/ppermute | solution.py:180
  66.1 0.0 collective-permute-done.1
  66.1 28.1 %conditional.3 = (bf16[96,24,256]{2,1,0:T(8,128)(2,1)S(1)}) conditional(s32[]{:T(128)} %bitcast.7, () %tuple.26, (s32[1024]{0:T(1024)}, bf16[24,4096]{1,0:T(8,128)(2,1)}, bf16[24,4096]{1,0:T(8,128)(2,1)}, bf16[24,4096]{1,0:T(8,128)(2,1)S(1)}) %tuple.28), branch_computations={%region_4.5_spmd, %region_5.6_spmd} | conditional | bytes 4456456 | solution.py:213
  66.1 1.7 pack.2
  67.8 26.5 %all_to_all.33 = bf16[8,12,24,256]{3,2,1,0:T(8,128)(2,1)S(1)} all-to-all(bf16[8,12,24,256]{3,2,1,0:T(8,128)(2,1)S(1)} %pack.2), channel_id=1, replica_groups=mesh['x'=4,'zh'=4,'c'=2,'zl'=8,'y'=4] {'x','c'}, dimensions={0} | all-to-all | bytes 2359296 | tf_op jit(solution)/shard_map/cond/branch_1_fun/all_to_all | solution.py:203
  94.2 0.0 copy-start.2
  94.2 0.0 collective-permute-done.2.refs_1_
  94.2 1.0 pack.3
  95.3 11.3 %all_to_all.34 = bf16[8,4,24,256]{3,2,1,0:T(8,128)(2,1)S(1)} all-to-all(bf16[8,4,24,256]{3,2,1,0:T(8,128)(2,1)S(1)} %pack.3), channel_id=1, replica_groups=mesh['x'=4,'zh'=4,'c'=2,'zl'=8,'y'=4] {'x','c'}, dimensions={0} | all-to-all | bytes 786432 | tf_op jit(solution)/shard_map/all_to_all | solution.py:203
  106.6 0.0 copy-done.2
  106.6 0.0 copy-start.3
  106.6 5.0 %aggregate.1 = bf16[32,24,128]{2,1,0:T(8,128)(2,1)} custom-call(s32[48]{0:T(128)S(1)} %get-tuple-element.31.pos, s32[16]{0:T(128)S(1)} %copy-done.2, bf16[96,24,256]{2,1,0:T(8,128)(2,1)S(1)} %get-tuple-element.54.near, bf16[32,24,256]{2,1,0:T(8,128)(2,1)S(1)} %bitcast.48, bf16[48,256,256]{2,1,0:T(8,128)(2,1)} %tiles_in.1), custom_call_target="tpu_custom_call" | custom-call | flops 150994944 | bytes 7340032 | tf_op jit(solution)/shard_map/aggregate/pallas_call | solution.py:101
  111.6 0.0 copy-start
  111.6 0.0 copy-start.1
  111.6 5.7 %all-to-all-start.3 = ((bf16[32,24,128]{2,1,0:T(8,128)(2,1)}), bf16[32,24,128]{2,1,0:T(8,128)(2,1)S(1)}, u32[]{:S(2)}, u32[]{:S(2)}) async-start(bf16[32,24,128]{2,1,0:T(8,128)(2,1)} %aggregate.1), calls=%async_computation.3 | async-start | bytes 393216 | tf_op jit(solution)/shard_map/all_to_all | solution.py:231
  117.3 0.0 copy-done.3
  117.3 0.3 copy.16
  117.5 16.3 %all-to-all-done.3 = bf16[32,24,128]{2,1,0:T(8,128)(2,1)S(1)} async-done(((bf16[32,24,128]{2,1,0:T(8,128)(2,1)}), bf16[32,24,128]{2,1,0:T(8,128)(2,1)S(1)}, u32[]{:S(2)}, u32[]{:S(2)}) %all-to-all-start.3) | async-done | bytes 196640 | tf_op jit(solution)/shard_map/all_to_all | solution.py:231
  133.8 0.0 copy-done
  133.8 0.0 copy-done.1
  133.8 1.2 dense.1
  135.1 17.0 %all_to_all.35.parts = bf16[32,4,24,128]{3,2,1,0:T(8,128)(2,1)S(1)} all-to-all(bf16[32,4,24,128]{3,2,1,0:T(8,128)(2,1)S(1)} %get-tuple-element.38), channel_id=1, replica_groups=mesh['x'=4,'zh'=4,'c'=2,'zl'=8,'y'=4] {'x','c','y'}, dimensions={0} | all-to-all | bytes 1572864 | tf_op jit(solution)/shard_map/all_to_all | solution.py:233
  152.0 0.2 fold.1
  152.2 15.2 %all_to_all.36 = f32[8,16,96]{2,1,0:T(8,128)S(1)} all-to-all(f32[8,16,96]{2,1,0:T(8,128)S(1)} %fold.1), channel_id=1, replica_groups=mesh['x'=4,'zh'=4,'c'=2,'zl'=8,'y'=4] {'zl'}, dimensions={0} | all-to-all | bytes 98304 | tf_op jit(solution)/shard_map/all_to_all | solution.py:234
  167.4 0.1 reshape.130
  167.6 33.0 %all_to_all.37 = f32[4,16,128]{2,1,0:T(8,128)S(1)} all-to-all(f32[4,16,128]{2,1,0:T(8,128)S(1)} %pad.4.clone), channel_id=1, replica_groups=mesh['x'=4,'zh'=4,'c'=2,'zl'=8,'y'=4] {'zh'}, dimensions={0} | all-to-all | bytes 65536 | tf_op jit(solution)/shard_map/all_to_all | solution.py:236
  200.6 0.6 slice_multiply_fusion
  (6 shorter events, 0.0 us)
Async XLA Ops:
  0.6 38.9 %collective-permute-start = (bf16[24,4096]{1,0:T(8,128)(2,1)}, bf16[24,4096]{1,0:T(8,128)(2,1)}, u32[]{:S(2)}, u32[]{:S(2)}) collective-permute-start(bf16[24,4096]{1,0:T(8,128)(2,1)} %param.12), channel_id=1, source_target_pairs={{0,64},{32,224},{64,128},{96,32},{128,192},{160,96},{192,0},{224,1... | collective-permute-start | bytes 589832 | tf_op jit(solution)/shard_map/ppermute | solution.py:180
  16.4 49.7 %collective-permute-start.1 = (bf16[24,4096]{1,0:T(8,128)(2,1)}, bf16[24,4096]{1,0:T(8,128)(2,1)S(1)}, u32[]{:S(2)}, u32[]{:S(2)}) collective-permute-start(bf16[24,4096]{1,0:T(8,128)(2,1)} %param.12), channel_id=1, source_target_pairs={{0,192},{32,96},{64,0},{96,160},{128,64},{160,224},{192,128},{224,... | collective-permute-start | bytes 589832 | tf_op jit(solution)/shard_map/ppermute | solution.py:180
  29.2 10.3 %all-to-all-start.1 = ((s32[8,1,128]{2,1,0:T(1,128)}), s32[8,1,128]{2,1,0:T(1,128)}, u32[]{:S(2)}, u32[]{:S(2)}) async-start(s32[8,1,128]{2,1,0:T(1,128)} %bitcast.4), calls=%async_computation.1 | async-start | bytes 8192 | tf_op jit(solution)/shard_map/cond/branch_1_fun/all_to_all | solution.py:217
  39.5 54.7 %collective-permute-start.2 = (bf16[24,4096]{1,0:T(8,128)(2,1)}, bf16[24,4096]{1,0:T(8,128)(2,1)S(1)}, u32[]{:S(2)}, u32[]{:S(2)}) collective-permute-start(bf16[24,4096]{1,0:T(8,128)(2,1)} %collective-permute-done), channel_id=1, source_target_pairs={{0,64},{32,224},{64,128},{96,32},{128,192},{160,96},{192,0},{224,1... | collective-permute-start | bytes 589832 | tf_op jit(solution)/shard_map/ppermute | solution.py:180
  94.2 12.4 %copy-start.2 = (s32[16]{0:T(128)S(1)}, s32[16]{0:T(128)}, u32[]{:S(2)}) copy-start(s32[16]{0:T(128)} %counts.1) | copy-start | bytes 196
  106.6 10.7 %copy-start.3 = (bf16[768,512]{1,0:T(8,128)(2,1)S(1)}, bf16[768,512]{1,0:T(8,128)(2,1)}, u32[]{:S(2)}) copy-start(bf16[768,512]{1,0:T(8,128)(2,1)} %param.17) | copy-start | bytes 2359300
  111.6 22.3 %copy-start = (bf16[512,128]{1,0:T(8,128)(2,1)S(1)}, bf16[512,128]{1,0:T(8,128)(2,1)}, u32[]{:S(2)}) copy-start(bf16[512,128]{1,0:T(8,128)(2,1)} %self_part.1) | copy-start | bytes 393220
  111.6 22.3 %copy-start.1 = (bf16[512,128]{1,0:T(8,128)(2,1)S(1)}, bf16[512,128]{1,0:T(8,128)(2,1)}, u32[]{:S(2)}) copy-start(bf16[512,128]{1,0:T(8,128)(2,1)} %cotangent.1) | copy-start | bytes 393220
  111.6 22.2 %all-to-all-start.3 = ((bf16[32,24,128]{2,1,0:T(8,128)(2,1)}), bf16[32,24,128]{2,1,0:T(8,128)(2,1)S(1)}, u32[]{:S(2)}, u32[]{:S(2)}) async-start(bf16[32,24,128]{2,1,0:T(8,128)(2,1)} %aggregate.1), calls=%async_computation.3 | async-start | bytes 393216 | tf_op jit(solution)/shard_map/all_to_all | solution.py:231

commit v11 on v10

--- a/solution.py
+++ b/solution.py
@@ -11,7 +11,7 @@
 MAXT = 3
 CAP = 4
 X, ZH, CORE, ZL, Y = 4, 4, 2, 8, 4
-NEAR, FAR = 3 * CAP, CAP
+NEAR, FAR = 2 * CAP, 2 * CAP
 PEERS = X * CORE
 LANES = 128
 GROUPS = 4
@@ -187,14 +187,14 @@
     column = (owners // (ZH * CORE)) * CORE + core
     apart = (me + ZH - owners // CORE % ZH) % ZH
     apart = jnp.where(core == 0, apart, (ZH - apart) % ZH)
-    far = apart == 2
+    far = apart > 1
     group = column + jnp.where(far, PEERS, 0)
     s = jnp.arange(slots, dtype=jnp.int32)
     earlier = (group[:, None] == group[None, :]) & (s[None, :] < s[:, None])
     rank = jnp.sum(earlier.astype(jnp.int32), axis=1)
     pos = rank + jnp.where(far, PEERS * NEAR + column * FAR, column * NEAR)
     place = column * LANES + rank + jnp.where(far, NEAR, 0)
-    code = local + jnp.where(apart == 1, 16, jnp.where(apart == 3, 32, 0))
+    code = local + jnp.where((apart == 1) | (apart == 2), 16, 0)
     hit = place[:, None] == jnp.arange(PEERS * LANES, dtype=jnp.int32)[None, :]
     return pos, jnp.sum(jnp.where(hit, code[:, None], 0), axis=0)
 
@@ -217,16 +217,17 @@
         return pos, lax.all_to_all(ask.reshape(PEERS, 1, LANES), ("x", "c"), 0, 0).reshape(-1)
 
     first = onward(features, 1)
-    second = onward(features, -1)
     pos, codes = beside(asking, (src_local.shape, jnp.int32), ((PEERS * LANES,), jnp.int32))
+    codes, again = lax.optimization_barrier((codes, features))
+    second = onward(again, -1)
     codes, first = lax.optimization_barrier((codes, first))
     third = onward(first, 1)
     (near,) = beside(
-        lambda: (exchange(pack(codes, (features, first, second), 0, NEAR, width)),),
+        lambda: (exchange(pack(codes, (features, first), 0, NEAR, width)),),
         ((PEERS * NEAR, rows, width), bf16),
     )
-    near, third = lax.optimization_barrier((near, third))
-    far = exchange(pack(codes, (third,), NEAR, FAR, width))
+    near, second, third = lax.optimization_barrier((near, second, third))
+    far = exchange(pack(codes, (second, third), NEAR, FAR, width))
     aggregated = aggregate(pos, counts, near, far, tiles, node_cols)
     node_rows = lax.all_to_all(aggregated, ("zl", "y"), 0, 0).reshape(-1, node_cols)
     hidden, grad = dense(node_rows, w_neigh.T, self_part, cotangent)

time: 202 us -> 199 us (0.985)
  starting transfers between devices: 63.8 us -> 48.6 us
  waiting for transfers between devices: 20 us -> 29.6 us
  blocking collectives: 103 us -> 106 us
    ppermute x3, starting transfers between devices: 51.5 us -> 30.3 us  [onward(): return lax.ppermute(value, ('zh', 'c'), pairs)]
    ppermute x3, waiting for transfers between devices: 0.01 us -> 9.84 us  [onward(): return lax.ppermute(value, ('zh', 'c'), pairs)]
    all_to_all x1, starting transfers between devices: 6.63 us -> 11.3 us  [asking(): lax.all_to_all(ask.reshape(PEERS, 1, LANES), ('x', 'c'), 0, 0).reshape(-1)]
    all_to_all x1, blocking collectives: 33 us -> 35.2 us  [per_device(): lax.all_to_all(jnp.pad(grad, ((0, 0), (0, 0), (0, LANES - rows))), 'zh',...]
  transfers between devices with their start and end apart: 5 -> 5, of which waited for: 2 -> 3; matrix products, arithmetic and copies ran while one was open for 2% -> 2% of each run, Pallas kernels for 1% -> 1%
where the time goes in v11:
time: 199 us
  blocking collectives  106 us (53%)
  starting transfers between devices  48.6 us (24%)
  waiting for transfers between devices  29.6 us (15%)
  Pallas kernels  8.84 us (4%)
  other arithmetic  3.58 us (2%)
    all_to_all x2, blocking collectives, exchange(): lax.all_to_all(packed, ('x', 'c'), 0, 0).reshape((-1,) + packed.shape[2:])  38.9 us
    all_to_all x1, blocking collectives, per_device(): lax.all_to_all(jnp.pad(grad, ((0, 0), (0, 0), (0, LANES - rows))), 'zh',...  35.2 us
    ppermute x3, starting transfers between devices, onward(): return lax.ppermute(value, ('zh', 'c'), pairs)  30.3 us
    all_to_all x1, blocking collectives, per_device(): grad = fold(lax.all_to_all(grad, ('x', 'c', 'y'), 0, 0))  17 us
    all_to_all x1, waiting for transfers between devices, per_device(): lax.all_to_all(aggregated, ('zl', 'y'), 0, 0).reshape(-1, node_cols)  16.1 us
    all_to_all x1, blocking collectives, per_device(): grad = jnp.sum(lax.all_to_all(grad, 'zl', 0, 0), axis=0)  15.2 us
    all_to_all x1, starting transfers between devices, asking(): lax.all_to_all(ask.reshape(PEERS, 1, LANES), ('x', 'c'), 0, 0).reshape(-1)  11.3 us
    ppermute x3, waiting for transfers between devices, onward(): return lax.ppermute(value, ('zh', 'c'), pairs)  9.84 us
  transfers between devices with their start and end apart: 5, of which 3 were waited for; matrix products, arithmetic and copies ran while one was open for 2% of the time, Pallas kernels for 1%

profile of v11, /device:TPU:2, one launch (start us, length us, event | category | flops | bytes accessed | tf_op | source)
XLA Modules:
  0.0 198.7 jit_solution(7485515061327096222)
XLA Ops:
  0.6 0.0 copy-start.2
  0.6 15.7 %collective-permute-start = (bf16[24,4096]{1,0:T(8,128)(2,1)}, bf16[24,4096]{1,0:T(8,128)(2,1)}, u32[]{:S(2)}, u32[]{:S(2)}) collective-permute-start(bf16[24,4096]{1,0:T(8,128)(2,1)} %param.12), channel_id=1, source_target_pairs={{0,64},{32,224},{64,128},{96,32},{128,192},{160,96},{192,0},{224,1... | collective-permute-start | bytes 589832 | tf_op jit(solution)/shard_map/ppermute | solution.py:180
  17.0 17.9 %conditional.2 = (s32[48]{0:T(128)S(1)}, s32[1024]{0:T(1024)}) conditional(s32[]{:T(128)} %bitcast.7, () %tuple.25, (s32[48,1]{0,1:T(1,128)}, s32[48]{0:T(128)}) %tuple.26), branch_computations={%region_0.0_spmd, %region_1.4_spmd} | conditional | flops 165972 | bytes 21284 | solution.py:213
  17.0 0.7 add_bitcast_fusion
  17.7 0.7 fusion.1
  18.4 0.7 fusion.2
  19.1 0.2 convert_reduce_fusion
  19.3 0.7 select_reduce_fusion
  20.0 11.3 %all-to-all-start.1 = ((s32[8,1,128]{2,1,0:T(1,128)}), s32[8,1,128]{2,1,0:T(1,128)}, u32[]{:S(2)}, u32[]{:S(2)}) async-start(s32[8,1,128]{2,1,0:T(1,128)} %bitcast.4), calls=%async_computation.1 | async-start | bytes 8192 | tf_op jit(solution)/shard_map/cond/branch_1_fun/all_to_all | solution.py:217
  31.3 3.7 %all-to-all-done.1 = s32[8,1,128]{2,1,0:T(1,128)} async-done(((s32[8,1,128]{2,1,0:T(1,128)}), s32[8,1,128]{2,1,0:T(1,128)}, u32[]{:S(2)}, u32[]{:S(2)}) %all-to-all-start.1) | async-done | bytes 4128 | tf_op jit(solution)/shard_map/cond/branch_1_fun/all_to_all | solution.py:217
  35.0 8.4 %collective-permute-start.1 = (bf16[24,4096]{1,0:T(8,128)(2,1)}, bf16[24,4096]{1,0:T(8,128)(2,1)S(1)}, u32[]{:S(2)}, u32[]{:S(2)}) collective-permute-start(bf16[24,4096]{1,0:T(8,128)(2,1)} %param.12), channel_id=1, source_target_pairs={{0,192},{32,96},{64,0},{96,160},{128,64},{160,224},{192,128},{224,... | collective-permute-start | bytes 589832 | tf_op jit(solution)/shard_map/ppermute | solution.py:180
  43.4 0.0 collective-permute-done
  43.4 6.1 %collective-permute-start.2 = (bf16[24,4096]{1,0:T(8,128)(2,1)}, bf16[24,4096]{1,0:T(8,128)(2,1)S(1)}, u32[]{:S(2)}, u32[]{:S(2)}) collective-permute-start(bf16[24,4096]{1,0:T(8,128)(2,1)} %collective-permute-done), channel_id=1, source_target_pairs={{0,64},{32,224},{64,128},{96,32},{128,192},{160,96},{192,0},{224,1... | collective-permute-start | bytes 589832 | tf_op jit(solution)/shard_map/ppermute | solution.py:180
  49.5 21.9 %conditional.3 = (bf16[64,24,256]{2,1,0:T(8,128)(2,1)S(1)}) conditional(s32[]{:T(128)} %bitcast.7, () %tuple.27, (s32[1024]{0:T(1024)}, bf16[24,4096]{1,0:T(8,128)(2,1)}, bf16[24,4096]{1,0:T(8,128)(2,1)}) %tuple.30), branch_computations={%region_4.5_spmd, %region_5.6_spmd} | conditional | bytes 3670024 | solution.py:213
  49.5 1.4 pack.2
  50.9 20.4 %all_to_all.33 = bf16[8,8,24,256]{3,2,1,0:T(8,128)(2,1)S(1)} all-to-all(bf16[8,8,24,256]{3,2,1,0:T(8,128)(2,1)S(1)} %pack.2), channel_id=1, replica_groups=mesh['x'=4,'zh'=4,'c'=2,'zl'=8,'y'=4] {'x','c'}, dimensions={0} | all-to-all | bytes 1572864 | tf_op jit(solution)/shard_map/cond/branch_1_fun/all_to_all | solution.py:203
  71.4 0.0 copy-start.3
  71.4 0.0 copy-start
  71.4 0.0 copy-start.1
  71.4 0.0 collective-permute-done.1.refs_1_
  71.4 9.8 %collective-permute-done.2.refs_2_ = bf16[24,4096]{1,0:T(8,128)(2,1)S(1)} collective-permute-done((bf16[24,4096]{1,0:T(8,128)(2,1)}, bf16[24,4096]{1,0:T(8,128)(2,1)S(1)}, u32[]{:S(2)}, u32[]{:S(2)}) %collective-permute-start.2) | collective-permute-done | bytes 196640 | tf_op jit(solution)/shard_map/ppermute | solution.py:180
  81.2 1.1 pack.3
  82.3 18.5 %all_to_all.34 = bf16[8,8,24,256]{3,2,1,0:T(8,128)(2,1)S(1)} all-to-all(bf16[8,8,24,256]{3,2,1,0:T(8,128)(2,1)S(1)} %pack.3), channel_id=1, replica_groups=mesh['x'=4,'zh'=4,'c'=2,'zl'=8,'y'=4] {'x','c'}, dimensions={0} | all-to-all | bytes 1572864 | tf_op jit(solution)/shard_map/all_to_all | solution.py:203
  100.8 0.0 copy-done.2
  100.8 5.0 %aggregate.1 = bf16[32,24,128]{2,1,0:T(8,128)(2,1)} custom-call(s32[48]{0:T(128)S(1)} %get-tuple-element.31.pos, s32[16]{0:T(128)S(1)} %copy-done.2, bf16[64,24,256]{2,1,0:T(8,128)(2,1)S(1)} %get-tuple-element.57.near, bf16[64,24,256]{2,1,0:T(8,128)(2,1)S(1)} %bitcast.47, bf16[48,256,256]{2,1,0:T(8,128)(2,1)} %tiles_in.1), custom_call_target="tpu_custom_call" | custom-call | flops 150994944 | bytes 7340032 | tf_op jit(solution)/shard_map/aggregate/pallas_call | solution.py:101
  105.7 7.0 %all-to-all-start.3 = ((bf16[32,24,128]{2,1,0:T(8,128)(2,1)}), bf16[32,24,128]{2,1,0:T(8,128)(2,1)S(1)}, u32[]{:S(2)}, u32[]{:S(2)}) async-start(bf16[32,24,128]{2,1,0:T(8,128)(2,1)} %aggregate.1), calls=%async_computation.3 | async-start | bytes 393216 | tf_op jit(solution)/shard_map/all_to_all | solution.py:232
  112.8 0.0 copy-done.3
  112.8 0.3 copy.16
  113.1 16.1 %all-to-all-done.3 = bf16[32,24,128]{2,1,0:T(8,128)(2,1)S(1)} async-done(((bf16[32,24,128]{2,1,0:T(8,128)(2,1)}), bf16[32,24,128]{2,1,0:T(8,128)(2,1)S(1)}, u32[]{:S(2)}, u32[]{:S(2)}) %all-to-all-start.3) | async-done | bytes 196640 | tf_op jit(solution)/shard_map/all_to_all | solution.py:232
  129.2 0.0 copy-done
  129.2 0.0 copy-done.1
  129.2 1.2 dense.1
  130.4 17.0 %all_to_all.35.parts = bf16[32,4,24,128]{3,2,1,0:T(8,128)(2,1)S(1)} all-to-all(bf16[32,4,24,128]{3,2,1,0:T(8,128)(2,1)S(1)} %get-tuple-element.41), channel_id=1, replica_groups=mesh['x'=4,'zh'=4,'c'=2,'zl'=8,'y'=4] {'x','c','y'}, dimensions={0} | all-to-all | bytes 1572864 | tf_op jit(solution)/shard_map/all_to_all | solution.py:234
  147.4 0.2 fold.1
  147.6 15.2 %all_to_all.36 = f32[8,16,96]{2,1,0:T(8,128)S(1)} all-to-all(f32[8,16,96]{2,1,0:T(8,128)S(1)} %fold.1), channel_id=1, replica_groups=mesh['x'=4,'zh'=4,'c'=2,'zl'=8,'y'=4] {'zl'}, dimensions={0} | all-to-all | bytes 98304 | tf_op jit(solution)/shard_map/all_to_all | solution.py:235
  162.8 0.1 reshape.130
  162.9 35.2 %all_to_all.37 = f32[4,16,128]{2,1,0:T(8,128)S(1)} all-to-all(f32[4,16,128]{2,1,0:T(8,128)S(1)} %pad.4.clone), channel_id=1, replica_groups=mesh['x'=4,'zh'=4,'c'=2,'zl'=8,'y'=4] {'zh'}, dimensions={0} | all-to-all | bytes 65536 | tf_op jit(solution)/shard_map/all_to_all | solution.py:237
  198.1 0.6 slice_multiply_fusion
  (6 shorter events, 0.0 us)
Async XLA Ops:
  0.6 100.1 %copy-start.2 = (s32[16]{0:T(128)S(1)}, s32[16]{0:T(128)}, u32[]{:S(2)}) copy-start(s32[16]{0:T(128)} %counts.1) | copy-start | bytes 196
  0.6 42.8 %collective-permute-start = (bf16[24,4096]{1,0:T(8,128)(2,1)}, bf16[24,4096]{1,0:T(8,128)(2,1)}, u32[]{:S(2)}, u32[]{:S(2)}) collective-permute-start(bf16[24,4096]{1,0:T(8,128)(2,1)} %param.12), channel_id=1, source_target_pairs={{0,64},{32,224},{64,128},{96,32},{128,192},{160,96},{192,0},{224,1... | collective-permute-start | bytes 589832 | tf_op jit(solution)/shard_map/ppermute | solution.py:180
  20.0 15.0 %all-to-all-start.1 = ((s32[8,1,128]{2,1,0:T(1,128)}), s32[8,1,128]{2,1,0:T(1,128)}, u32[]{:S(2)}, u32[]{:S(2)}) async-start(s32[8,1,128]{2,1,0:T(1,128)} %bitcast.4), calls=%async_computation.1 | async-start | bytes 8192 | tf_op jit(solution)/shard_map/cond/branch_1_fun/all_to_all | solution.py:217
  35.0 36.4 %collective-permute-start.1 = (bf16[24,4096]{1,0:T(8,128)(2,1)}, bf16[24,4096]{1,0:T(8,128)(2,1)S(1)}, u32[]{:S(2)}, u32[]{:S(2)}) collective-permute-start(bf16[24,4096]{1,0:T(8,128)(2,1)} %param.12), channel_id=1, source_target_pairs={{0,192},{32,96},{64,0},{96,160},{128,64},{160,224},{192,128},{224,... | collective-permute-start | bytes 589832 | tf_op jit(solution)/shard_map/ppermute | solution.py:180
  43.4 37.8 %collective-permute-start.2 = (bf16[24,4096]{1,0:T(8,128)(2,1)}, bf16[24,4096]{1,0:T(8,128)(2,1)S(1)}, u32[]{:S(2)}, u32[]{:S(2)}) collective-permute-start(bf16[24,4096]{1,0:T(8,128)(2,1)} %collective-permute-done), channel_id=1, source_target_pairs={{0,64},{32,224},{64,128},{96,32},{128,192},{160,96},{192,0},{224,1... | collective-permute-start | bytes 589832 | tf_op jit(solution)/shard_map/ppermute | solution.py:180
  71.4 41.4 %copy-start.3 = (bf16[768,512]{1,0:T(8,128)(2,1)S(1)}, bf16[768,512]{1,0:T(8,128)(2,1)}, u32[]{:S(2)}) copy-start(bf16[768,512]{1,0:T(8,128)(2,1)} %param.17) | copy-start | bytes 2359300
  71.4 57.8 %copy-start = (bf16[512,128]{1,0:T(8,128)(2,1)S(1)}, bf16[512,128]{1,0:T(8,128)(2,1)}, u32[]{:S(2)}) copy-start(bf16[512,128]{1,0:T(8,128)(2,1)} %self_part.1) | copy-start | bytes 393220
  71.4 57.8 %copy-start.1 = (bf16[512,128]{1,0:T(8,128)(2,1)S(1)}, bf16[512,128]{1,0:T(8,128)(2,1)}, u32[]{:S(2)}) copy-start(bf16[512,128]{1,0:T(8,128)(2,1)} %cotangent.1) | copy-start | bytes 393220
  105.7 23.4 %all-to-all-start.3 = ((bf16[32,24,128]{2,1,0:T(8,128)(2,1)}), bf16[32,24,128]{2,1,0:T(8,128)(2,1)S(1)}, u32[]{:S(2)}, u32[]{:S(2)}) async-start(bf16[32,24,128]{2,1,0:T(8,128)(2,1)} %aggregate.1), calls=%async_computation.3 | async-start | bytes 393216 | tf_op jit(solution)/shard_map/all_to_all | solution.py:232

commit v12 on v8

--- a/solution.py
+++ b/solution.py
@@ -184,27 +184,52 @@
     return lax.ppermute(value, ("zh", "c"), pairs)
 
 
-def plan(owners, local):
-    me = lax.axis_index("zh")
-    slots = owners.shape[0]
-    core = owners % CORE
-    column = (owners // (ZH * CORE)) * CORE + core
-    apart = (me + ZH - owners // CORE % ZH) % ZH
-    apart = jnp.where(core == 0, apart, (ZH - apart) % ZH)
-    near, far = apart % 2 == 1, apart == 2
+def plan_kernel(here, owner_in, local_in, pos, ask):
+    slots = owner_in.shape[0]
+    s = lax.broadcasted_iota(jnp.int32, (slots, slots), 0)
+    t = lax.broadcasted_iota(jnp.int32, (slots, slots), 1)
+
+    def row(column):
+        return jnp.sum(jnp.where(s == t, column, 0.0), axis=0, keepdims=True)
+
+    owners = owner_in[...]
+    local = jnp.sum(jnp.where(s == t, local_in[...].astype(f32), 0.0), axis=1, keepdims=True).astype(jnp.int32)
+    core = owners & (CORE - 1)
+    column = (owners >> 3) * CORE + core
+    apart = (here[0] + ZH - ((owners >> 1) & (ZH - 1))) & (ZH - 1)
+    apart = jnp.where(core == 0, apart, (ZH - apart) & (ZH - 1))
+    near, far = (apart & 1) == 1, apart == 2
     group = column + jnp.where(far, 2 * PEERS, jnp.where(near, PEERS, 0))
-    s = jnp.arange(slots, dtype=jnp.int32)
-    earlier = (group[:, None] == group[None, :]) & (s[None, :] < s[:, None])
-    rank = jnp.sum(earlier.astype(jnp.int32), axis=1)
-    pos = rank + jnp.where(
+    earlier = (group.astype(f32) == row(group.astype(f32))) & (t < s)
+    rank = jnp.sum(jnp.where(earlier, 1.0, 0.0), axis=1, keepdims=True).astype(jnp.int32)
+    there = rank + jnp.where(
         far,
         PEERS * (OWN + NEAR) + column * FAR,
         jnp.where(near, PEERS * OWN + column * NEAR, column * OWN),
     )
-    place = column * LANES + rank + jnp.where(far, OWN + NEAR, jnp.where(near, OWN, 0))
-    code = local + jnp.where(apart == 3, 16, 0)
-    hit = place[:, None] == jnp.arange(PEERS * LANES, dtype=jnp.int32)[None, :]
-    return pos, jnp.sum(jnp.where(hit, code[:, None], 0), axis=0)
+    pos[...] = row(there.astype(f32)).astype(jnp.int32)
+    place = rank + jnp.where(far, OWN + NEAR, jnp.where(near, OWN, 0))
+    code = (local + jnp.where(apart == 3, 16, 0)).astype(f32)
+    lane = lax.broadcasted_iota(jnp.int32, (slots, LANES), 1)
+    for d in range(PEERS):
+        hit = (lane == place) & (column == d)
+        ask[d] = jnp.sum(jnp.where(hit, code, 0.0), axis=0, keepdims=True).astype(jnp.int32)
+
+
+def plan(owners, local):
+    slots = local.shape[0]
+    pos, ask = pl.pallas_call(
+        plan_kernel,
+        out_shape=(
+            jax.ShapeDtypeStruct((1, slots), jnp.int32),
+            jax.ShapeDtypeStruct((PEERS, 1, LANES), jnp.int32),
+        ),
+        in_specs=[smem(), vmem(), vmem()],
+        out_specs=(vmem(), vmem()),
+        compiler_params=pltpu.CompilerParams(vmem_limit_bytes=VMEM),
+        name="plan",
+    )(lax.axis_index("zh").reshape(1), owners, local.reshape(1, slots))
+    return pos.reshape(slots), ask
 
 
 def exchange(packed):
@@ -221,8 +246,8 @@
         return lax.cond(live, work, lambda: tuple(jnp.zeros(shape, kind) for shape, kind in like))
 
     def asking():
-        pos, ask = plan(src_owner[:, 0], src_local)
-        codes = lax.all_to_all(ask.reshape(PEERS, 1, LANES), ("x", "c"), 0, 0)
+        pos, ask = plan(src_owner, src_local)
+        codes = lax.all_to_all(ask, ("x", "c"), 0, 0)
         return pos, codes.reshape(-1)
 
     first = onward(features, 1)

time: 197 us -> 196 us (level)
  blocking collectives: 106 us -> 121 us
  starting transfers between devices: 50.2 us -> 39.2 us
  waiting for transfers between devices: 25.3 us -> 21.5 us
  other arithmetic: 3.6 us -> 0.62 us
    all_to_all x0 -> x1, blocking collectives: none -> 14.9 us  [asking(): codes = lax.all_to_all(ask, ('x', 'c'), 0, 0)]
    all_to_all x1 -> x0, starting transfers between devices: 9.84 us -> none  [asking(): codes = lax.all_to_all(ask.reshape(PEERS, 1, LANES), ('x', 'c'), 0, 0)]
    all_to_all x1 -> x0, waiting for transfers between devices: 5.13 us -> none  [asking(): codes = lax.all_to_all(ask.reshape(PEERS, 1, LANES), ('x', 'c'), 0, 0)]
  transfers between devices with their start and end apart: 5 -> 4, of which waited for: 4 -> 3; matrix products, arithmetic and copies ran while one was open for 2% -> 1% of each run, Pallas kernels for 1% -> 2%
where the time goes in v12:
time: 196 us; the launch traced here: 195 us
  blocking collectives  121 us (62%)
  starting transfers between devices  39.2 us (20%)
  waiting for transfers between devices  21.5 us (11%)
  Pallas kernels  10.6 us (5%)
    all_to_all x3, blocking collectives, exchange(): lax.all_to_all(packed, ('x', 'c'), 0, 0).reshape((-1,) + packed.shape[2:])  39.7 us
    all_to_all x1, blocking collectives, per_device(): lax.all_to_all(jnp.pad(grad, ((0, 0), (0, 0), (0, LANES - rows))), 'zh',...  33.8 us
    ppermute x3, starting transfers between devices, onward(): return lax.ppermute(value, ('zh', 'c'), pairs)  30.5 us
    all_to_all x1, blocking collectives, per_device(): grad = fold(lax.all_to_all(grad, ('x', 'c', 'y'), 0, 0))  17.8 us
    all_to_all x1, waiting for transfers between devices, per_device(): lax.all_to_all(aggregated, ('zl', 'y'), 0, 0).reshape(-1, node_cols)  15 us
    all_to_all x1, blocking collectives, asking(): codes = lax.all_to_all(ask, ('x', 'c'), 0, 0)  14.9 us
    all_to_all x1, blocking collectives, per_device(): grad = jnp.sum(lax.all_to_all(grad, 'zl', 0, 0), axis=0)  14.7 us
    all_to_all x1, starting transfers between devices, per_device(): lax.all_to_all(aggregated, ('zl', 'y'), 0, 0).reshape(-1, node_cols)  8.75 us
  transfers between devices with their start and end apart: 4, of which 3 were waited for; matrix products, arithmetic and copies ran while one was open for 1% of the time, Pallas kernels for 2%

profile of v12, /device:TPU:32, one launch (start us, length us, event | category | flops | bytes accessed | tf_op | source)
XLA Modules:
  0.0 195.5 jit_solution(9621145100247195709)
XLA Ops:
  0.6 0.0 copy-start.2
  0.6 15.7 %collective-permute-start = (bf16[24,4096]{1,0:T(8,128)(2,1)}, bf16[24,4096]{1,0:T(8,128)(2,1)}, u32[]{:S(2)}, u32[]{:S(2)}) collective-permute-start(bf16[24,4096]{1,0:T(8,128)(2,1)} %param.14), channel_id=1, source_target_pairs={{0,64},{32,224},{64,128},{96,32},{128,192},{160,96},{192,0},{224,1... | collective-permute-start | bytes 589832 | tf_op jit(solution)/shard_map/ppermute | solution.py:184
  17.0 16.6 %conditional.3 = (s32[48]{0:T(128)S(1)}, s32[1024]{0:T(1024)S(1)}) conditional(s32[]{:T(128)} %bitcast.6, () %tuple.31, (s32[48]{0:T(128)}, s32[48,1]{0,1:T(1,128)}) %tuple.32), branch_computations={%region_0.0_spmd, %region_1.0_spmd} | conditional | flops 3 | bytes 8624 | solution.py:246
  17.0 0.7 copy.16.owner_in
  17.8 1.0 plan.1
  18.8 14.9 %all_to_all.37 = s32[8,1,128]{2,1,0:T(1,128)S(1)} all-to-all(s32[8,1,128]{2,1,0:T(1,128)S(1)} %get-tuple-element.23), channel_id=1, replica_groups=mesh['x'=4,'zh'=4,'c'=2,'zl'=8,'y'=4] {'x','c'}, dimensions={0} | all-to-all | bytes 8192 | tf_op jit(solution)/shard_map/cond/branch_1_fun/all_to_all | solution.py:250
  33.7 8.4 %collective-permute-start.1 = (bf16[24,4096]{1,0:T(8,128)(2,1)}, bf16[24,4096]{1,0:T(8,128)(2,1)S(1)}, u32[]{:S(2)}, u32[]{:S(2)}) collective-permute-start(bf16[24,4096]{1,0:T(8,128)(2,1)} %param.14), channel_id=1, source_target_pairs={{0,192},{32,96},{64,0},{96,160},{128,64},{160,224},{192,128},{224,... | collective-permute-start | bytes 589832 | tf_op jit(solution)/shard_map/ppermute | solution.py:184
  42.1 12.5 %conditional.4 = (bf16[32,24,256]{2,1,0:T(8,128)(2,1)S(1)}) conditional(s32[]{:T(128)} %bitcast.6, () %tuple.33, (s32[1024]{0:T(1024)S(1)}, bf16[24,4096]{1,0:T(8,128)(2,1)}) %tuple.35), branch_computations={%region_2.0_spmd, %region_3.0_spmd} | conditional | bytes 2883592 | solution.py:246
  42.1 1.1 pack.3
  43.2 11.3 %all_to_all.38 = bf16[8,4,24,256]{3,2,1,0:T(8,128)(2,1)S(1)} all-to-all(bf16[8,4,24,256]{3,2,1,0:T(8,128)(2,1)S(1)} %pack.3), channel_id=1, replica_groups=mesh['x'=4,'zh'=4,'c'=2,'zl'=8,'y'=4] {'x','c'}, dimensions={0} | all-to-all | bytes 786432 | tf_op jit(solution)/shard_map/cond/branch_1_fun/all_to_all | solution.py:236
  54.6 0.0 collective-permute-done
  54.6 6.3 %collective-permute-start.2 = (bf16[24,4096]{1,0:T(8,128)(2,1)}, bf16[24,4096]{1,0:T(8,128)(2,1)S(1)}, u32[]{:S(2)}, u32[]{:S(2)}) collective-permute-start(bf16[24,4096]{1,0:T(8,128)(2,1)} %collective-permute-done), channel_id=1, source_target_pairs={{0,64},{32,224},{64,128},{96,32},{128,192},{160,96},{192,0},{224,1... | collective-permute-start | bytes 589832 | tf_op jit(solution)/shard_map/ppermute | solution.py:184
  60.9 4.3 %collective-permute-done.1 = bf16[24,4096]{1,0:T(8,128)(2,1)S(1)} collective-permute-done((bf16[24,4096]{1,0:T(8,128)(2,1)}, bf16[24,4096]{1,0:T(8,128)(2,1)S(1)}, u32[]{:S(2)}, u32[]{:S(2)}) %collective-permute-start.1) | collective-permute-done | bytes 196640 | tf_op jit(solution)/shard_map/ppermute | solution.py:184
  65.2 0.0 copy-start.3
  65.2 17.0 %conditional.5 = (bf16[64,24,256]{2,1,0:T(8,128)(2,1)S(1)}) conditional(s32[]{:T(128)} %bitcast.6, () %tuple.37, (s32[1024]{0:T(1024)S(1)}, bf16[24,4096]{1,0:T(8,128)(2,1)}, bf16[24,4096]{1,0:T(8,128)(2,1)S(1)}) %tuple.38), branch_computations={%region_4.0_spmd, %region_5.0_spmd} | conditional | bytes 3670024 | solution.py:246
  65.2 1.4 pack.4
  66.6 15.7 %all_to_all.39 = bf16[8,8,24,256]{3,2,1,0:T(8,128)(2,1)S(1)} all-to-all(bf16[8,8,24,256]{3,2,1,0:T(8,128)(2,1)S(1)} %pack.4), channel_id=1, replica_groups=mesh['x'=4,'zh'=4,'c'=2,'zl'=8,'y'=4] {'x','c'}, dimensions={0} | all-to-all | bytes 1572864 | tf_op jit(solution)/shard_map/cond/branch_1_fun/all_to_all | solution.py:236
  82.3 0.0 copy-start
  82.3 0.0 copy-start.1
  82.3 2.3 %collective-permute-done.2.refs_1_ = bf16[24,4096]{1,0:T(8,128)(2,1)S(1)} collective-permute-done((bf16[24,4096]{1,0:T(8,128)(2,1)}, bf16[24,4096]{1,0:T(8,128)(2,1)S(1)}, u32[]{:S(2)}, u32[]{:S(2)}) %collective-permute-start.2) | collective-permute-done | bytes 196640 | tf_op jit(solution)/shard_map/ppermute | solution.py:184
  84.5 0.7 pack.5
  85.3 12.8 %all_to_all.40 = bf16[8,4,24,256]{3,2,1,0:T(8,128)(2,1)S(1)} all-to-all(bf16[8,4,24,256]{3,2,1,0:T(8,128)(2,1)S(1)} %pack.5), channel_id=1, replica_groups=mesh['x'=4,'zh'=4,'c'=2,'zl'=8,'y'=4] {'x','c'}, dimensions={0} | all-to-all | bytes 786432 | tf_op jit(solution)/shard_map/all_to_all | solution.py:236
  98.0 0.0 copy-done.2
  98.1 5.0 %aggregate.1 = bf16[32,24,128]{2,1,0:T(8,128)(2,1)} custom-call(s32[48]{0:T(128)S(1)} %get-tuple-element.41.pos, s32[16]{0:T(128)S(1)} %copy-done.2, bf16[32,24,256]{2,1,0:T(8,128)(2,1)S(1)} %get-tuple-element.65.own, bf16[64,24,256]{2,1,0:T(8,128)(2,1)S(1)} %get-tuple-element.66.near, bf16[32,24,256]{2,1,0:T(8,128)(2,1)S(1)} %bitcast.13, ...), custom_call_target="tpu_custom_call" | custom-call | flops 150994944 | bytes 7340032 | tf_op jit(solution)/shard_map/aggregate/pallas_call | solution.py:105
  103.0 8.7 %all-to-all-start.4 = ((bf16[32,24,128]{2,1,0:T(8,128)(2,1)}), bf16[32,24,128]{2,1,0:T(8,128)(2,1)S(1)}, u32[]{:S(2)}, u32[]{:S(2)}) async-start(bf16[32,24,128]{2,1,0:T(8,128)(2,1)} %aggregate.1), calls=%async_computation.4 | async-start | bytes 393216 | tf_op jit(solution)/shard_map/all_to_all | solution.py:272
  111.8 0.0 copy-done.3
  111.8 0.3 copy.17
  112.1 15.0 %all-to-all-done.4 = bf16[32,24,128]{2,1,0:T(8,128)(2,1)S(1)} async-done(((bf16[32,24,128]{2,1,0:T(8,128)(2,1)}), bf16[32,24,128]{2,1,0:T(8,128)(2,1)S(1)}, u32[]{:S(2)}, u32[]{:S(2)}) %all-to-all-start.4) | async-done | bytes 196640 | tf_op jit(solution)/shard_map/all_to_all | solution.py:272
  127.0 0.0 copy-done
  127.0 0.0 copy-done.1
  127.0 1.2 dense.1
  128.3 17.8 %all_to_all.41.parts = bf16[32,4,24,128]{3,2,1,0:T(8,128)(2,1)S(1)} all-to-all(bf16[32,4,24,128]{3,2,1,0:T(8,128)(2,1)S(1)} %get-tuple-element.50), channel_id=1, replica_groups=mesh['x'=4,'zh'=4,'c'=2,'zl'=8,'y'=4] {'x','c','y'}, dimensions={0} | all-to-all | bytes 1572864 | tf_op jit(solution)/shard_map/all_to_all | solution.py:274
  146.1 0.2 fold.1
  146.3 14.7 %all_to_all.42 = f32[8,16,96]{2,1,0:T(8,128)S(1)} all-to-all(f32[8,16,96]{2,1,0:T(8,128)S(1)} %fold.1), channel_id=1, replica_groups=mesh['x'=4,'zh'=4,'c'=2,'zl'=8,'y'=4] {'zl'}, dimensions={0} | all-to-all | bytes 98304 | tf_op jit(solution)/shard_map/all_to_all | solution.py:275
  161.0 0.1 reshape.37
  161.1 33.8 %all_to_all.43 = f32[4,16,128]{2,1,0:T(8,128)S(1)} all-to-all(f32[4,16,128]{2,1,0:T(8,128)S(1)} %pad.4.clone), channel_id=1, replica_groups=mesh['x'=4,'zh'=4,'c'=2,'zl'=8,'y'=4] {'zh'}, dimensions={0} | all-to-all | bytes 65536 | tf_op jit(solution)/shard_map/all_to_all | solution.py:277
  194.9 0.6 slice_multiply_fusion
  (4 shorter events, 0.0 us)
Async XLA Ops:
  0.6 97.4 %copy-start.2 = (s32[16]{0:T(128)S(1)}, s32[16]{0:T(128)}, u32[]{:S(2)}) copy-start(s32[16]{0:T(128)} %counts.1) | copy-start | bytes 196
  0.6 53.9 %collective-permute-start = (bf16[24,4096]{1,0:T(8,128)(2,1)}, bf16[24,4096]{1,0:T(8,128)(2,1)}, u32[]{:S(2)}, u32[]{:S(2)}) collective-permute-start(bf16[24,4096]{1,0:T(8,128)(2,1)} %param.14), channel_id=1, source_target_pairs={{0,64},{32,224},{64,128},{96,32},{128,192},{160,96},{192,0},{224,1... | collective-permute-start | bytes 589832 | tf_op jit(solution)/shard_map/ppermute | solution.py:184
  33.7 31.6 %collective-permute-start.1 = (bf16[24,4096]{1,0:T(8,128)(2,1)}, bf16[24,4096]{1,0:T(8,128)(2,1)S(1)}, u32[]{:S(2)}, u32[]{:S(2)}) collective-permute-start(bf16[24,4096]{1,0:T(8,128)(2,1)} %param.14), channel_id=1, source_target_pairs={{0,192},{32,96},{64,0},{96,160},{128,64},{160,224},{192,128},{224,... | collective-permute-start | bytes 589832 | tf_op jit(solution)/shard_map/ppermute | solution.py:184
  54.6 30.0 %collective-permute-start.2 = (bf16[24,4096]{1,0:T(8,128)(2,1)}, bf16[24,4096]{1,0:T(8,128)(2,1)S(1)}, u32[]{:S(2)}, u32[]{:S(2)}) collective-permute-start(bf16[24,4096]{1,0:T(8,128)(2,1)} %collective-permute-done), channel_id=1, source_target_pairs={{0,64},{32,224},{64,128},{96,32},{128,192},{160,96},{192,0},{224,1... | collective-permute-start | bytes 589832 | tf_op jit(solution)/shard_map/ppermute | solution.py:184
  65.2 46.5 %copy-start.3 = (bf16[768,512]{1,0:T(8,128)(2,1)S(1)}, bf16[768,512]{1,0:T(8,128)(2,1)}, u32[]{:S(2)}) copy-start(bf16[768,512]{1,0:T(8,128)(2,1)} %param.19) | copy-start | bytes 2359300
  82.3 44.8 %copy-start = (bf16[512,128]{1,0:T(8,128)(2,1)S(1)}, bf16[512,128]{1,0:T(8,128)(2,1)}, u32[]{:S(2)}) copy-start(bf16[512,128]{1,0:T(8,128)(2,1)} %self_part.1) | copy-start | bytes 393220
  82.3 44.8 %copy-start.1 = (bf16[512,128]{1,0:T(8,128)(2,1)S(1)}, bf16[512,128]{1,0:T(8,128)(2,1)}, u32[]{:S(2)}) copy-start(bf16[512,128]{1,0:T(8,128)(2,1)} %cotangent.1) | copy-start | bytes 393220
  103.0 24.0 %all-to-all-start.4 = ((bf16[32,24,128]{2,1,0:T(8,128)(2,1)}), bf16[32,24,128]{2,1,0:T(8,128)(2,1)S(1)}, u32[]{:S(2)}, u32[]{:S(2)}) async-start(bf16[32,24,128]{2,1,0:T(8,128)(2,1)} %aggregate.1), calls=%async_computation.4 | async-start | bytes 393216 | tf_op jit(solution)/shard_map/all_to_all | solution.py:272
